TPU v7x, 32 devices: a whole 2x2x4 slice. The times are simulated.
32 devices in a mesh: section: 2 (over x), dp: 16 (over z, y, core).
Axes of the slice: x: 2, y: 2, z: 4, core: 2. Of those that a mesh axis runs over, the one named last changes fastest.
Arguments:
- tokens: bfloat16 [2, 4096, 1152], P(None, 'dp'), may hold values from -6 to 6
- kept_index: int32 [2, 2048], P(None, 'dp'), may hold values from 0 to 255, as said below
- big_image: int32 [2, 16], P(None, 'dp'), may hold values from 0 to 1
- timesteps: int32 [2, 64], P(None, 'dp'), may hold values from 0 to 999
- labels: int32 [2, 64], P(None, 'dp'), may hold values from 0 to 999
- cotangent: bfloat16 [2, 4096, 1152], P(None, 'dp'), may hold values from -6 to 6
- mask_token: bfloat16 [1152], replicated, may hold values from -6 to 6
- time_weight: bfloat16 [256, 1152], replicated, may hold values from -0.375 to 0.375
- class_table: bfloat16 [1000, 1152], replicated, may hold values from -6 to 6
- ada_weight: bfloat16 [2, 1152, 6912], P('section', 'dp'), may hold values from -0.1875 to 0.1875
- ada_bias: bfloat16 [2, 6912], P('section', 'dp'), may hold values from -3 to 3
- qkv_weight: bfloat16 [2, 1152, 3456], P('section', 'dp'), may hold values from -0.1875 to 0.1875
- proj_weight: bfloat16 [2, 1152, 1152], P('section', 'dp'), may hold values from -2 to 2
- up_weight: bfloat16 [2, 1152, 4608], P('section', 'dp'), may hold values from -0.1875 to 0.1875
- down_weight: bfloat16 [2, 4608, 1152], P('section', 'dp'), may hold values from -0.09375 to 0.09375
Outputs:
- decoded: bfloat16 [2, 4096, 1152], P(None, 'dp', 'section')
- token_grad: bfloat16 [2, 4096, 1152], P(None, 'dp', 'section')
- mask_grad: float32 [1152], replicated
- time_grad: float32 [256, 1152], replicated
- table_grad: float32 [1000, 1152], replicated
- ada_grad: float32 [2, 1152, 6912], P('section', 'dp')
- ada_bias_grad: float32 [2, 6912], P('section', 'dp')
- qkv_grad: float32 [2, 1152, 3456], P('section', 'dp')
- proj_grad: float32 [2, 1152, 1152], P('section', 'dp')
- up_grad: float32 [2, 1152, 4608], P('section', 'dp')
- down_grad: float32 [2, 4608, 1152], P('section', 'dp')
Inputs may be any that keep to these rules, and one draw needn't show every extreme that they name: `kept_index`: each device's block of 128 entries of a micro-batch lists kept positions among that device's 256 positions, ascending; each of the 4 quarters of 64 positions keeps exactly half of its positions. `big_image`: where it is 1, only the first of the device's 4 image entries is used.
All inputs are finite; a program needn't handle non-finite values.
Results may differ from a plain program's by a relative error of at most 0.035.
The roundings to bfloat16 on the way count: a program that leaves them out, or rounds other values in their place, can miss the bound.
Values may be sent and summed in bfloat16 or wider, within the bound.
A program may use at most 1 GiB of HBM per device.

v0:
```python
from functools import partial
import math

import jax
import jax.numpy as jnp
from jax import lax
from jax.sharding import PartitionSpec as P

HEADS = 16
HD = 72
SMALL_PER = 4


exact_mode = lax.Precision.HIGHEST
norm_eps = 1e-06
masked_score = -1e30
group_heads = 4


def from_partner(x, axis, stride):
    return lax.ppermute(x, axis, [(i, i ^ 1 << stride) for i in range(lax.axis_size(axis))])


def pre_norm(token_row_matrix, shift_rows, scale_rows):
    centred = token_row_matrix - jnp.mean(token_row_matrix, axis=-1, keepdims=True)
    variance = jnp.mean(centred * centred, axis=-1, keepdims=True)
    return centred * lax.rsqrt(variance + norm_eps) * (1.0 + scale_rows) + shift_rows


def gelu_tanh(pre_act):
    return jax.nn.gelu(pre_act, approximate=True)


def split_dot(left_side, right_side, pattern):
    upper_part = left_side.astype(jnp.bfloat16)
    remainder = left_side - upper_part.astype(jnp.float32)
    middle = remainder.astype(jnp.bfloat16)
    lowest = (remainder - middle.astype(jnp.float32)).astype(jnp.bfloat16)
    summed = jnp.einsum(pattern, upper_part, right_side, preferred_element_type=jnp.float32)
    summed = summed + jnp.einsum(pattern, middle, right_side, preferred_element_type=jnp.float32)
    return summed + jnp.einsum(pattern, lowest, right_side, preferred_element_type=jnp.float32)


def to_groups(grouped):
    row_count = grouped.shape[0]
    return jnp.moveaxis(grouped.reshape(row_count, HEADS // group_heads, group_heads, HD), 1, 0)


def merge_groups(grouped):
    return jnp.moveaxis(grouped, 0, 1).reshape(grouped.shape[1], HEADS * HD)


def masked_scores(allowed, query_part, key_part):
    scores = jnp.einsum(
        "qhd,khd->hqk", query_part, key_part, preferred_element_type=jnp.float32
    ) * HD ** (-0.5)
    return jnp.where(allowed[None], scores, masked_score)


def attend_forward(allowed, inputs):
    query_part, key_part, value_part = inputs
    scores = masked_scores(allowed, query_part, key_part)
    highest = jnp.max(scores, axis=-1, keepdims=True)
    exp_scores = jnp.exp(scores - highest)
    totals = jnp.sum(exp_scores, axis=-1, keepdims=True)
    prob_rows = (exp_scores / totals).astype(jnp.bfloat16)
    result = jnp.einsum("hqk,khd->qhd", prob_rows, value_part, preferred_element_type=jnp.float32)
    return (result, highest + jnp.log(totals))


def attend_backward(allowed, inputs):
    query_part, key_part, value_part, log_total, grad_part = inputs
    prob_rows = jnp.exp(masked_scores(allowed, query_part, key_part) - log_total)
    grad_value = jnp.einsum(
        "hqk,qhd->khd",
        prob_rows.astype(jnp.bfloat16),
        grad_part,
        preferred_element_type=jnp.float32,
    )
    grad_prob = jnp.einsum(
        "qhd,khd->hqk", grad_part, value_part, preferred_element_type=jnp.float32
    )
    centre = jnp.sum(prob_rows * grad_prob, axis=-1, keepdims=True)
    grad_scores = (prob_rows * (grad_prob - centre)).astype(jnp.bfloat16)
    grad_query = jnp.einsum(
        "hqk,khd->qhd", grad_scores, key_part, preferred_element_type=jnp.float32
    ) * HD ** (-0.5)
    grad_key = jnp.einsum(
        "hqk,qhd->khd", grad_scores, query_part, preferred_element_type=jnp.float32
    ) * HD ** (-0.5)
    return (grad_query, grad_key, grad_value)


def block_forward(token_row_matrix, segment_index, condition_vector, weights):
    (
        modulation_weight_whole,
        bias_whole,
        query_key_value_whole,
        projection_whole,
        up_weight_whole,
        down_weight_whole,
    ) = weights
    row_count = token_row_matrix.shape[0]
    model_width = token_row_matrix.shape[1]
    member = (segment_index[:, None] == jnp.arange(SMALL_PER)[None, :]).astype(jnp.float32)
    lifted = jax.nn.silu(condition_vector).astype(jnp.bfloat16)
    modulation = jnp.dot(
        lifted, modulation_weight_whole, preferred_element_type=jnp.float32
    ) + bias_whole.astype(jnp.float32)
    pieces = jnp.split(jnp.dot(member, modulation, precision=exact_mode), 6, axis=-1)
    first_in = pre_norm(token_row_matrix, pieces[0], pieces[1]).astype(jnp.bfloat16)
    qkv_rows = jnp.dot(first_in, query_key_value_whole, preferred_element_type=jnp.float32).astype(
        jnp.bfloat16
    )
    query_groups = to_groups(qkv_rows[:, :model_width].reshape(row_count, HEADS, HD))
    key_groups = to_groups(qkv_rows[:, model_width : 2 * model_width].reshape(row_count, HEADS, HD))
    value_groups = to_groups(qkv_rows[:, 2 * model_width :].reshape(row_count, HEADS, HD))
    allowed = segment_index[:, None] == segment_index[None, :]
    attended_groups, logsum_groups = lax.map(
        partial(attend_forward, allowed), (query_groups, key_groups, value_groups)
    )
    attended = merge_groups(attended_groups).astype(jnp.bfloat16)
    branch = jnp.dot(attended, projection_whole, preferred_element_type=jnp.float32)
    middle_rows = token_row_matrix + pieces[2] * branch
    second_in = pre_norm(middle_rows, pieces[3], pieces[4]).astype(jnp.bfloat16)
    hidden = jnp.dot(second_in, up_weight_whole, preferred_element_type=jnp.float32)
    active = gelu_tanh(hidden).astype(jnp.bfloat16)
    mlp_out = jnp.dot(active, down_weight_whole, preferred_element_type=jnp.float32)
    output = middle_rows + pieces[5] * mlp_out
    stored = (
        member,
        lifted,
        pieces,
        first_in,
        (query_groups, key_groups, value_groups),
        logsum_groups,
        attended,
        branch,
        middle_rows,
        second_in,
        hidden,
        active,
        mlp_out,
        allowed,
    )
    return (output, stored)


def block_backward(token_row_matrix, condition_vector, weights, stored, grad_output):
    (
        modulation_weight_whole,
        bias_whole,
        query_key_value_whole,
        projection_whole,
        up_weight_whole,
        down_weight_whole,
    ) = weights
    (
        member,
        lifted,
        pieces,
        first_in,
        qkv_groups,
        logsum_groups,
        attended,
        branch,
        middle_rows,
        second_in,
        hidden,
        active,
        mlp_out,
        allowed,
    ) = stored
    row_count = token_row_matrix.shape[0]
    grad_mlp = (pieces[5] * grad_output).astype(jnp.bfloat16)
    grad_gate_two = grad_output * mlp_out
    down_part = jnp.einsum("ti,to->io", active, grad_mlp, preferred_element_type=jnp.float32)
    grad_active = jnp.einsum(
        "to,io->ti", grad_mlp, down_weight_whole, preferred_element_type=jnp.float32
    )
    unused, gelu_pull = jax.vjp(gelu_tanh, hidden)
    grad_hidden = gelu_pull(grad_active)[0].astype(jnp.bfloat16)
    up_part = jnp.einsum("ti,to->io", second_in, grad_hidden, preferred_element_type=jnp.float32)
    grad_second = jnp.einsum(
        "to,io->ti", grad_hidden, up_weight_whole, preferred_element_type=jnp.float32
    )
    unused, norm_pull = jax.vjp(pre_norm, middle_rows, pieces[3], pieces[4])
    grad_middle, grad_shift_two, grad_scale_two = norm_pull(grad_second)
    grad_middle = grad_middle + grad_output
    grad_gate_one = grad_middle * branch
    grad_branch = (pieces[2] * grad_middle).astype(jnp.bfloat16)
    proj_part = jnp.einsum("ti,to->io", attended, grad_branch, preferred_element_type=jnp.float32)
    grad_attended = jnp.einsum(
        "to,io->ti", grad_branch, projection_whole, preferred_element_type=jnp.float32
    ).astype(jnp.bfloat16)
    grad_groups = to_groups(grad_attended.reshape(row_count, HEADS, HD))
    grad_query, grad_key, grad_value = lax.map(
        partial(attend_backward, allowed),
        (qkv_groups[0], qkv_groups[1], qkv_groups[2], logsum_groups, grad_groups),
    )
    grad_qkv = jnp.concatenate(
        [merge_groups(grad_query), merge_groups(grad_key), merge_groups(grad_value)], axis=-1
    ).astype(jnp.bfloat16)
    qkv_part = jnp.einsum("ti,to->io", first_in, grad_qkv, preferred_element_type=jnp.float32)
    grad_first = jnp.einsum(
        "to,io->ti", grad_qkv, query_key_value_whole, preferred_element_type=jnp.float32
    )
    unused, norm_pull_one = jax.vjp(pre_norm, token_row_matrix, pieces[0], pieces[1])
    grad_rows, grad_shift_one, grad_scale_one = norm_pull_one(grad_first)
    grad_rows = grad_rows + grad_middle
    grad_per_token = jnp.concatenate(
        [
            grad_shift_one,
            grad_scale_one,
            grad_gate_one,
            grad_shift_two,
            grad_scale_two,
            grad_gate_two,
        ],
        axis=-1,
    )
    grad_modulation = jnp.einsum("tg,tm->gm", member, grad_per_token, precision=exact_mode)
    ada_part = jnp.einsum(
        "gi,gm->im", lifted.astype(jnp.float32), grad_modulation, precision=exact_mode
    )
    bias_part = jnp.sum(grad_modulation, axis=0)
    grad_lifted = split_dot(grad_modulation, modulation_weight_whole, "gm,im->gi")
    unused, silu_pull = jax.vjp(jax.nn.silu, condition_vector)
    grad_cond = silu_pull(grad_lifted)[0]
    return (grad_rows, grad_cond, (ada_part, bias_part, qkv_part, proj_part, up_part, down_part))


def conditioning(time_ids, label_ids, time_weight, class_table):
    halfway = time_weight.shape[0] // 2
    frequencies = jnp.exp(-math.log(10000.0) * jnp.arange(halfway, dtype=jnp.float32) / halfway)
    angles = time_ids.astype(jnp.float32)[:, None] * frequencies[None, :]
    embedding = jnp.concatenate([jnp.cos(angles), jnp.sin(angles)], axis=-1).astype(jnp.bfloat16)
    onehot = (label_ids[:, None] == jnp.arange(class_table.shape[0])[None, :]).astype(jnp.bfloat16)
    condition_vector = jnp.dot(embedding, time_weight, preferred_element_type=jnp.float32)
    condition_vector = condition_vector + jnp.dot(
        onehot, class_table, preferred_element_type=jnp.float32
    )
    return (condition_vector, embedding, onehot)


def slot_layout(retained_row, big_flag, slot_len):
    positions = jnp.arange(slot_len, dtype=jnp.int32)
    segment_whole = jnp.where(big_flag > 0, 0, positions // (slot_len // SMALL_PER))
    segment_retained = jnp.take(segment_whole, retained_row, axis=0)
    placement = positions[:, None] == retained_row[None, :]
    return (segment_whole, segment_retained, placement)


def on_device(
    tokens,
    kept_index,
    big_image,
    timesteps,
    labels,
    cotangent,
    mask_token,
    time_weight,
    class_table,
    ada_weight,
    ada_bias,
    qkv_weight,
    proj_weight,
    up_weight,
    down_weight,
):
    section_id = lax.axis_index("section")
    dp_count = lax.axis_size("dp")
    micro_count, slot_len, model_width = tokens.shape
    kept_len = kept_index.shape[1]
    shards = (
        ada_weight[0],
        ada_bias[0],
        qkv_weight[0],
        proj_weight[0],
        up_weight[0],
        down_weight[0],
    )
    grad_zero = tuple(
        (
            jnp.zeros((shard_piece.shape[0] * dp_count,) + shard_piece.shape[1:], jnp.float32)
            for shard_piece in shards
        )
    )

    def slot_info(micro_id):
        segment_whole, segment_retained, placement = slot_layout(
            kept_index[micro_id], big_image[micro_id, 0], slot_len
        )
        condition_vector, embedding, onehot = conditioning(
            timesteps[micro_id], labels[micro_id], time_weight, class_table
        )
        return (segment_whole, segment_retained, placement, condition_vector, embedding, onehot)

    def shared_terms(embedding, onehot, grad_cond):
        time_part = jnp.dot(embedding.astype(jnp.float32).T, grad_cond, precision=exact_mode)
        table_part = jnp.dot(onehot.astype(jnp.float32).T, grad_cond, precision=exact_mode)
        return (time_part, table_part)

    def empty_result():
        return (
            jnp.zeros((kept_len, model_width), jnp.bfloat16),
            grad_zero,
            jnp.zeros(time_weight.shape, jnp.float32),
            jnp.zeros(class_table.shape, jnp.float32),
            jnp.zeros((model_width,), jnp.float32),
            jnp.zeros((slot_len, model_width), jnp.bfloat16),
            jnp.zeros((slot_len, model_width), jnp.float32),
        )

    def encoder_side(tick_num, weights, received):
        outgoing_rows, grad_parts, time_part, table_part, mask_part, decoded, token_part = (
            empty_result()
        )
        if tick_num < micro_count:
            segment_whole, segment_retained, placement, condition_vector, embedding, onehot = (
                slot_info(tick_num)
            )
            enc_in = jnp.einsum(
                "sk,sd->kd",
                placement.astype(jnp.bfloat16),
                tokens[tick_num],
                preferred_element_type=jnp.float32,
            )
            enc_out, unused = block_forward(enc_in, segment_retained, condition_vector, weights)
            outgoing_rows = enc_out.astype(jnp.bfloat16)
        if tick_num >= 2:
            micro_id = tick_num - 2
            segment_whole, segment_retained, placement, condition_vector, embedding, onehot = (
                slot_info(micro_id)
            )
            enc_in = jnp.einsum(
                "sk,sd->kd",
                placement.astype(jnp.bfloat16),
                tokens[micro_id],
                preferred_element_type=jnp.float32,
            )
            enc_out, stored = block_forward(enc_in, segment_retained, condition_vector, weights)
            grad_rows, grad_cond, grad_parts = block_backward(
                enc_in, condition_vector, weights, stored, received.astype(jnp.float32)
            )
            token_part = jnp.einsum(
                "sk,kd->sd", placement.astype(jnp.float32), grad_rows, precision=exact_mode
            )
            time_part, table_part = shared_terms(embedding, onehot, grad_cond)
        return (outgoing_rows, grad_parts, time_part, table_part, mask_part, decoded, token_part)

    def decoder_side(tick_num, weights, received):
        outgoing_rows, grad_parts, time_part, table_part, mask_part, decoded, token_part = (
            empty_result()
        )
        if 1 <= tick_num <= micro_count:
            micro_id = tick_num - 1
            segment_whole, segment_retained, placement, condition_vector, embedding, onehot = (
                slot_info(micro_id)
            )
            kept_flags = jnp.sum(placement.astype(jnp.float32), axis=1)
            decoder_input = jnp.einsum(
                "sk,kd->sd",
                placement.astype(jnp.bfloat16),
                received,
                preferred_element_type=jnp.float32,
            )
            decoder_input = (
                decoder_input
                + (1.0 - kept_flags)[:, None] * mask_token.astype(jnp.float32)[None, :]
            )
            dec_out, stored = block_forward(decoder_input, segment_whole, condition_vector, weights)
            grad_in, grad_cond, grad_parts = block_backward(
                decoder_input,
                condition_vector,
                weights,
                stored,
                cotangent[micro_id].astype(jnp.float32),
            )
            outgoing_rows = jnp.einsum(
                "sk,sd->kd", placement.astype(jnp.float32), grad_in, precision=exact_mode
            ).astype(jnp.bfloat16)
            mask_part = jnp.sum((1.0 - kept_flags)[:, None] * grad_in, axis=0)
            decoded = dec_out.astype(jnp.bfloat16)
            time_part, table_part = shared_terms(embedding, onehot, grad_cond)
        return (outgoing_rows, grad_parts, time_part, table_part, mask_part, decoded, token_part)

    received = jnp.zeros((kept_len, model_width), jnp.bfloat16)
    grad_shards = tuple((jnp.zeros_like(shard_piece, dtype=jnp.float32) for shard_piece in shards))
    time_total = jnp.zeros(time_weight.shape, jnp.float32)
    table_total = jnp.zeros(class_table.shape, jnp.float32)
    mask_total = jnp.zeros((model_width,), jnp.float32)
    decoded_list = []
    token_list = []
    for tick_num in range(micro_count + 2):
        weights = (
            lax.all_gather(ada_weight[0], "dp", axis=0, tiled=True),
            lax.all_gather(ada_bias[0], "dp", axis=0, tiled=True),
            lax.all_gather(qkv_weight[0], "dp", axis=0, tiled=True),
            lax.all_gather(proj_weight[0], "dp", axis=0, tiled=True),
            lax.all_gather(up_weight[0], "dp", axis=0, tiled=True),
            lax.all_gather(down_weight[0], "dp", axis=0, tiled=True),
        )
        result = lax.cond(
            section_id == 0,
            partial(encoder_side, tick_num, weights),
            partial(decoder_side, tick_num, weights),
            received,
        )
        outgoing_rows, grad_parts, time_part, table_part, mask_part, decoded, token_part = result
        if tick_num <= micro_count:
            received = from_partner(outgoing_rows, "section", 0)
        if tick_num >= 1:
            scattered = (
                lax.psum_scatter(grad_parts[0], "dp", scatter_dimension=0, tiled=True),
                lax.psum_scatter(grad_parts[1], "dp", scatter_dimension=0, tiled=True),
                lax.psum_scatter(grad_parts[2], "dp", scatter_dimension=0, tiled=True),
                lax.psum_scatter(grad_parts[3], "dp", scatter_dimension=0, tiled=True),
                lax.psum_scatter(grad_parts[4], "dp", scatter_dimension=0, tiled=True),
                lax.psum_scatter(grad_parts[5], "dp", scatter_dimension=0, tiled=True),
            )
            grad_shards = tuple((before + after for before, after in zip(grad_shards, scattered)))
        time_total = time_total + time_part
        table_total = table_total + table_part
        mask_total = mask_total + mask_part
        if 1 <= tick_num <= micro_count:
            decoded_list.append(decoded)
        if tick_num >= 2:
            token_list.append(token_part)
    shared = lax.psum((time_total, table_total, mask_total), ("section", "dp"))
    decoded_all = jnp.stack(decoded_list)
    token_all = jnp.stack(token_list).astype(jnp.bfloat16)
    half_width = model_width // 2
    outgoing_half = jnp.where(
        section_id == 0, token_all[:, :, half_width:], decoded_all[:, :, :half_width]
    )
    incoming_half = from_partner(outgoing_half, "section", 0)
    decoded_half = jnp.where(section_id == 0, incoming_half, decoded_all[:, :, half_width:])
    token_half = jnp.where(section_id == 0, token_all[:, :, :half_width], incoming_half)
    return (
        decoded_half,
        token_half,
        shared[2],
        shared[0],
        shared[1],
        grad_shards[0][None],
        grad_shards[1][None],
        grad_shards[2][None],
        grad_shards[3][None],
        grad_shards[4][None],
        grad_shards[5][None],
    )


def solution(mesh):
    in_specs = (
        P(None, "dp", None),
        P(None, "dp"),
        P(None, "dp"),
        P(None, "dp"),
        P(None, "dp"),
        P(None, "dp", None),
        P(),
        P(),
        P(),
        P("section", "dp", None),
        P("section", "dp"),
        P("section", "dp", None),
        P("section", "dp", None),
        P("section", "dp", None),
        P("section", "dp", None),
    )
    out_specs = (
        P(None, "dp", "section"),
        P(None, "dp", "section"),
        P(),
        P(),
        P(),
        P("section", "dp", None),
        P("section", "dp"),
        P("section", "dp", None),
        P("section", "dp", None),
        P("section", "dp", None),
        P("section", "dp", None),
    )
    return jax.shard_map(
        on_device, mesh=mesh, in_specs=in_specs, out_specs=out_specs, check_vma=False
    )
```

profile of v0, /device:TPU:0, one launch (start us, length us, event | category | flops | bytes accessed | tf_op | source)
XLA Modules:
  0.0 2359.8 jit_solution(829502744761574944)
XLA Ops:
  12.3 63.8 %all-reduce = bf16[6912]{0:T(1024)(128)(2,1)S(1)} all-reduce(bf16[6912]{0:T(1024)(128)(2,1)S(1)} %dynamic-update-slice), channel_id=3, replica_groups=mesh['section'=2,'dp'=16] {'dp'}, use_global_device_ids=true, to_apply=%add | all-reduce | flops 6912 | bytes 27648 | tf_op jit(solution)/shard_map/all_gather | solution.py:398
  76.2 53.4 %all-gather.14.cloned.1.call-done = bf16[1,1152,3456]{2,1,0:T(8,128)(2,1)} async-done(((bf16[1,72,3456]{2,1,0:T(8,128)(2,1)}), bf16[1,1152,3456]{2,1,0:T(8,128)(2,1)}) %all-gather.14.cloned.1.call-update) | async-done | bytes 7962640 | tf_op jit(solution)/shard_map/all_gather | solution.py:399
  129.5 89.3 %all-gather.18.cloned.1.call-done = bf16[1,1152,4608]{2,1,0:T(8,128)(2,1)} async-done(((bf16[1,72,4608]{2,1,0:T(8,128)(2,1)}), bf16[1,1152,4608]{2,1,0:T(8,128)(2,1)}) %all-gather.18.cloned.1.call-update) | async-done | bytes 10616848 | tf_op jit(solution)/shard_map/all_gather | solution.py:401
  218.9 89.0 %all-gather.20.cloned.1.call-done = bf16[1,4608,1152]{2,1,0:T(8,128)(2,1)} async-done(((bf16[1,288,1152]{2,1,0:T(8,128)(2,1)}), bf16[1,4608,1152]{2,1,0:T(8,128)(2,1)}) %all-gather.20.cloned.1.call-update) | async-done | bytes 10616848 | tf_op jit(solution)/shard_map/all_gather | solution.py:402
  307.9 121.8 %all-gather.12.cloned.1.call-done = bf16[1,1152,6912]{2,1,0:T(8,128)(2,1)} async-done(((bf16[1,72,6912]{2,1,0:T(8,128)(2,1)}), bf16[1,1152,6912]{2,1,0:T(8,128)(2,1)}) %all-gather.12.cloned.1.call-update) | async-done | bytes 15925264 | tf_op jit(solution)/shard_map/all_gather | solution.py:397
  429.7 54.1 %conditional.5 = (bf16[128,1152]{1,0:T(8,128)(2,1)S(1)}, f32[]{:T(128)}) conditional(s32[]{:T(128)} %convert_element_type.544, () %tuple.118, (s32[2,128]{1,0:T(2,128)S(1)}, bf16[2,256,1152]{2,1,0:T(8,128)(2,1)}, s32[2,1]{0,1:T(1,128)S(1)}, s32[2,4]{1,0:T(2,128)S(1)}, bf16[256,1152]{1,0:T(8,128)(2,1)S(1)}, /*index=5*/s32[2,4]{1,0:T(2,128)S(1)}, ...), branch_computations={%region_0.0_spmd, %region_1.11_spmd} | conditional | flops 4308570112 | bytes 103994288 | solution.py:404
  430.0 7.3 convolution_add_fusion.10
  441.0 5.5 convolution_convert_fusion.5
  449.3 19.9 while.162
  472.2 11.5 fusion.339
  483.8 9.2 collective-permute-done
  493.0 107.2 %conditional.6 = (bf16[128,1152]{1,0:T(8,128)(2,1)S(1)}, f32[1152,6912]{1,0:T(8,128)}, f32[6912]{0:T(1024)S(1)}, f32[1152,3456]{1,0:T(8,128)}, f32[1152,1152]{1,...) conditional(s32[]{:T(128)} %convert_element_type.544, ...), branch_computations={%region_10.30_spmd, %region_29.39_spmd} | conditional | flops 26228615168 | bytes 611051584
  502.2 8.9 convolution_add_fusion.12
  524.2 19.9 while.163
  547.2 11.5 fusion.399
  558.7 10.9 broadcast_in_dim.367
  569.6 9.8 broadcast_in_dim.371
  579.4 8.5 broadcast_in_dim.372
  587.9 6.5 broadcast_in_dim.369
  600.3 118.4 %collective-permute-start.1 = (bf16[128,1152]{1,0:T(8,128)(2,1)S(1)}, bf16[128,1152]{1,0:T(8,128)(2,1)S(1)}, u32[]{:S(2)}, u32[]{:S(2)}) collective-permute-start(bf16[128,1152]{1,0:T(8,128)(2,1)S(1)} %get-tuple-element.883), channel_id=1, source_target_pairs={{0,16},{16,0},{1,17},{17,1},{2,18},{18,2},{3,19},{19,3},{4,20},{20... | collective-permute-start | bytes 884744 | tf_op jit(solution)/shard_map/ppermute | solution.py:21
  718.7 6.9 collective-permute-done.1
  725.7 220.0 %conditional.7 = (bf16[128,1152]{1,0:T(8,128)(2,1)S(1)}, f32[1152,6912]{1,0:T(8,128)}, f32[1152,3456]{1,0:T(8,128)}, f32[1152,1152]{1,0:T(8,128)}, f32[1152,4608...) conditional(s32[]{:T(128)} %convert_element_type.544, ...), branch_computations={%region_38.57_spmd, %region_56.73_spmd} | conditional | flops 26228742144 | bytes 612056192 | solution.py:404
  734.6 7.7 convolution_add_fusion.14
  756.7 17.7 while.158
  778.1 7.3 fusion.619
  785.4 9.6 fusion.466
  805.3 36.5 %while.159 = (s32[]{:T(128)}, bf16[4,128,4,72]{1,3,2,0:T(8,128)(2,1)}, bf16[4,128,4,72]{1,3,2,0:T(8,128)(2,1)}, bf16[4,128,4,72]{1,3,2,0:T(8,128)(2,1)}, bf16[4,...) while((s32[]{:T(128)}, ...), condition=%wide.region_69.70_spmd.clone, body=%wide.region_67.69_spmd.clone.sunk | while | flops 47865344 | bytes 2973297 | solution.py:197
  841.9 6.3 multiply_reduce_fusion.18
  851.3 6.0 fusion.458
  858.6 9.8 fusion.481
  868.4 9.8 convolution_add_fusion.16
  878.2 9.7 fusion.491
  898.0 9.2 fusion.477
  907.2 17.1 fusion.506
  924.3 8.8 fusion.621
  933.1 8.9 fusion.507
  948.7 6.2 collective-permute-done.2
  954.9 210.0 %conditional.8 = (f32[1152,6912]{1,0:T(8,128)}, f32[6912]{0:T(1024)}, f32[1152,3456]{1,0:T(8,128)}, f32[1152,1152]{1,0:T(8,128)}, f32[1152,4608]{1,0:T(8,128)}, ...) conditional(s32[]{:T(128)} %convert_element_type.544, ...), branch_computations={%region_72.74_spmd, %region_73.91_spmd} | conditional | flops 13669570560 | bytes 447215040 | solution.py:404
  959.4 7.7 convolution_add_fusion.18
  982.7 12.3 while.160
  998.6 7.5 fusion.622
  1006.1 9.7 fusion.521
  1027.8 31.1 %while.161 = (s32[]{:T(128)}, bf16[4,128,4,72]{1,3,2,0:T(8,128)(2,1)}, bf16[4,128,4,72]{1,3,2,0:T(8,128)(2,1)}, bf16[4,128,4,72]{1,3,2,0:T(8,128)(2,1)}, bf16[4,...) while((s32[]{:T(128)}, ...), condition=%wide.region_86.87_spmd.clone, body=%wide.region_84.86_spmd.clone.sunk | while | flops 47865344 | bytes 2973297 | solution.py:197
  1059.0 6.3 multiply_reduce_fusion.22
  1068.4 6.0 fusion.513
  1076.4 9.8 fusion.536
  1086.1 9.8 convolution_add_fusion.20
  1095.9 9.7 fusion.546
  1116.7 9.0 fusion.532
  1125.8 17.0 fusion.561
  1142.8 8.8 fusion.624
  1151.6 9.9 fusion.562
  1164.9 7.9 add_add_fusion.17
  1175.5 9.5 add_add_fusion.16
  1185.1 22.4 add_add_fusion.15
  1207.5 28.7 %add_add_fusion.13 = f32[4608,1152]{1,0:T(8,128)} fusion(f32[4608,1152]{1,0:T(8,128)} %get-tuple-element.917, f32[4608,1152]{1,0:T(8,128)} %get-tuple-element.915, f32[4608,1152]{1,0:T(8,128)} %get-tuple-element.916), kind=kLoop, calls=%fused_computation.888 | loop fusion | flops 10616832 | bytes 84934656 | tf_op jit(solution)/shard_map/add | solution.py:422
  1236.3 28.6 %add_add_fusion.14 = f32[1152,4608]{1,0:T(8,128)} fusion(f32[1152,4608]{1,0:T(8,128)} %get-tuple-element.914, f32[1152,4608]{1,0:T(8,128)} %get-tuple-element.912, f32[1152,4608]{1,0:T(8,128)} %get-tuple-element.913), kind=kLoop, calls=%fused_computation.889 | loop fusion | flops 10616832 | bytes 84934656 | tf_op jit(solution)/shard_map/add | solution.py:422
  1265.0 42.7 %add_add_fusion.12 = f32[1152,6912]{1,0:T(8,128)} fusion(f32[1152,6912]{1,0:T(8,128)} %get-tuple-element.901, f32[1152,6912]{1,0:T(8,128)} %get-tuple-element.899, f32[1152,6912]{1,0:T(8,128)} %get-tuple-element.900), kind=kLoop, calls=%fused_computation.887 | loop fusion | flops 15925248 | bytes 127401984 | tf_op jit(solution)/shard_map/add | solution.py:422
  1313.7 58.5 %all-reduce.1 = f32[6912]{0:T(1024)S(1)} all-reduce(f32[6912]{0:T(1024)S(1)} %add_add_fusion.19), channel_id=21, replica_groups=mesh['section'=2,'dp'=16] {'dp'}, use_global_device_ids=true, to_apply=%region_96.98.clone | all-reduce | flops 6912 | bytes 55296
  1372.9 37.4 %psum.21 = f32[1152]{0:T(1024)} all-reduce(f32[1152]{0:T(1024)S(1)} %add_add_fusion.20), channel_id=1, replica_groups=mesh['section'=2,'dp'=16] {'section','dp'}, use_global_device_ids=true, to_apply=%region_90.92 | all-reduce | flops 1152 | bytes 9216 | tf_op jit(solution)/shard_map/psum | solution.py:430
  1411.4 175.6 %reduce-scatter.16.cloned.1.call-done = f32[72,3456]{1,0:T(8,128)} async-done(((f32[1152,3456]{1,0:T(8,128)}), f32[72,3456]{1,0:T(8,128)}) %reduce-scatter.16.cloned.1.call-update) | async-done | bytes 995344
  1587.0 217.3 %reduce-scatter.14.cloned.1.call-done = f32[288,1152]{1,0:T(8,128)} async-done(((f32[4608,1152]{1,0:T(8,128)}), f32[288,1152]{1,0:T(8,128)}) %reduce-scatter.14.cloned.1.call-update) | async-done | bytes 1327120 | tf_op jit(solution)/shard_map/reduce_scatter | solution.py:420
  1804.3 216.5 %reduce-scatter.12.cloned.1.call-done = f32[72,4608]{1,0:T(8,128)} async-done(((f32[1152,4608]{1,0:T(8,128)}), f32[72,4608]{1,0:T(8,128)}) %reduce-scatter.12.cloned.1.call-update) | async-done | bytes 1327120 | tf_op jit(solution)/shard_map/reduce_scatter | solution.py:419
  2020.8 325.2 %reduce-scatter.10.cloned.1.call-done = f32[72,6912]{1,0:T(8,128)} async-done(((f32[1152,6912]{1,0:T(8,128)}), f32[72,6912]{1,0:T(8,128)}) %reduce-scatter.10.cloned.1.call-update) | async-done | bytes 1990672 | tf_op jit(solution)/shard_map/reduce_scatter | solution.py:415
  (651 shorter events, 294.3 us)
Async XLA Ops:
  7.2 422.5 %copy-start.202 = (s32[2,128]{1,0:T(2,128)S(1)}, s32[2,128]{1,0:T(2,128)}, u32[]{:S(2)}) copy-start(s32[2,128]{1,0:T(2,128)} %param.46) | copy-start | bytes 3076
  7.2 422.4 %copy-start.208 = (s32[2,1]{0,1:T(1,128)S(1)}, s32[2,1]{0,1:T(1,128)}, u32[]{:S(2)}) copy-start(s32[2,1]{0,1:T(1,128)} %param.47) | copy-start | bytes 28
  7.2 422.4 %copy-start.170 = (s32[2,4]{1,0:T(2,128)S(1)}, s32[2,4]{1,0:T(2,128)}, u32[]{:S(2)}) copy-start(s32[2,4]{1,0:T(2,128)} %param.48) | copy-start | bytes 100
  7.2 422.4 %copy-start.171 = (s32[2,4]{1,0:T(2,128)S(1)}, s32[2,4]{1,0:T(2,128)}, u32[]{:S(2)}) copy-start(s32[2,4]{1,0:T(2,128)} %param.49) | copy-start | bytes 100
  7.2 422.4 %copy-start.31 = (bf16[256,1152]{1,0:T(8,128)(2,1)S(1)}, bf16[256,1152]{1,0:T(8,128)(2,1)}, u32[]{:S(2)}) copy-start(bf16[256,1152]{1,0:T(8,128)(2,1)} %param.52) | copy-start | bytes 1769476
  7.3 422.4 %copy-start.6 = (bf16[1000,1152]{1,0:T(8,128)(2,1)S(1)}, bf16[1000,1152]{1,0:T(8,128)(2,1)}, u32[]{:S(2)}) copy-start(bf16[1000,1152]{1,0:T(8,128)(2,1)} %param.53) | copy-start | bytes 6912004
  7.3 68.9 %all-gather.16.cloned.1.call-start = ((), (), s32[]{:S(2)}) async-start(), calls=%async_computation.7 | async-start | bytes 2820096 | tf_op jit(solution)/shard_map/all_gather | solution.py:400
  8.0 121.5 %all-gather.14.cloned.1.call-start = ((), (), s32[]{:S(2)}) async-start(), calls=%async_computation.6 | async-start | bytes 8460288 | tf_op jit(solution)/shard_map/all_gather | solution.py:399
  8.8 210.1 %all-gather.18.cloned.1.call-start = ((), (), s32[]{:S(2)}) async-start(), calls=%async_computation.8 | async-start | bytes 11280384 | tf_op jit(solution)/shard_map/all_gather | solution.py:401
  9.5 298.4 %all-gather.20.cloned.1.call-start = ((), (), s32[]{:S(2)}) async-start(), calls=%async_computation.9 | async-start | bytes 11280384 | tf_op jit(solution)/shard_map/all_gather | solution.py:402
  10.1 419.6 %all-gather.12.cloned.1.call-start = ((), (), s32[]{:S(2)}) async-start(), calls=%async_computation.5 | async-start | bytes 16920576 | tf_op jit(solution)/shard_map/all_gather | solution.py:397
  10.7 1400.8 %all-reduce.7.cloned.1.call-start = ((), (), s32[]{:S(2)}) async-start(), calls=%async_computation.15 | async-start | bytes 11575296 | tf_op jit(solution)/shard_map/psum | solution.py:430
  448.4 20.8 copy-start
  483.8 9.2 collective-permute-start
  523.4 20.8 copy-start.2
  600.3 125.4 %copy-start.150 = (f32[6912]{0:T(1024)}, f32[6912]{0:T(1024)S(1)}, u32[]{:S(2)}) copy-start(f32[6912]{0:T(1024)S(1)} %get-tuple-element.902) | copy-start | bytes 82948
  600.3 125.4 %copy-start.154 = (f32[1152]{0:T(1024)}, f32[1152]{0:T(1024)S(1)}, u32[]{:S(2)}) copy-start(f32[1152]{0:T(1024)S(1)} %get-tuple-element.890) | copy-start | bytes 13828
  600.3 125.4 %copy-start.82 = (f32[256,1152]{1,0:T(8,128)}, f32[256,1152]{1,0:T(8,128)S(1)}, u32[]{:S(2)}) copy-start(f32[256,1152]{1,0:T(8,128)S(1)} %get-tuple-element.893) | copy-start | bytes 3538948
  600.3 125.4 %copy-start.138 = (bf16[1,256,1152]{1,2,0:T(8,128)(2,1)}, bf16[1,256,1152]{1,2,0:T(8,128)(2,1)S(1)}, u32[]{:S(2)}) copy-start(bf16[1,256,1152]{1,2,0:T(8,128)(2,1)S(1)} %get-tuple-element.1110) | copy-start | bytes 1769476
  600.3 125.4 %collective-permute-start.1 = (bf16[128,1152]{1,0:T(8,128)(2,1)S(1)}, bf16[128,1152]{1,0:T(8,128)(2,1)S(1)}, u32[]{:S(2)}, u32[]{:S(2)}) collective-permute-start(bf16[128,1152]{1,0:T(8,128)(2,1)S(1)} %get-tuple-element.883), channel_id=1, source_target_pairs={{0,16},{16,0},{1,17},{17,1},{2,18},{18,2},{3,19},{19,3},{4,20},{20... | collective-permute-start | bytes 884744 | tf_op jit(solution)/shard_map/ppermute | solution.py:21
  731.3 11.0 copy-start.71
  732.1 10.2 copy-start.178
  732.2 10.1 copy-start.166
  732.2 10.1 copy-start.168
  745.7 28.8 %copy-start.27 = (f32[128,1152]{1,0:T(8,128)}, f32[128,1152]{1,0:T(8,128)S(1)}, u32[]{:S(2)}) copy-start(f32[128,1152]{1,0:T(8,128)S(1)} %get-tuple-element.1385) | copy-start | bytes 1769476 | tf_op jit(solution)/shard_map/cond
  754.0 20.5 copy-start.4
  777.3 22.6 copy-start.160
  777.5 22.4 copy-start.180
  778.1 17.0 slice-start.10
  778.1 17.0 slice-start.11
  785.4 9.7 slice-start.12
  785.4 9.7 copy-start.33
  803.8 38.0 %copy-start.26 = (f32[128,6912]{1,0:T(8,128)S(1)}, f32[128,6912]{1,0:T(8,128)}, u32[]{:S(2)}) copy-start(f32[128,6912]{1,0:T(8,128)} %copy-done.24) | copy-start | bytes 10616836 | tf_op jit(solution)/shard_map/cond
  858.6 19.5 copy-start.52
  868.4 9.8 copy-start.146
  878.1 9.8 copy-start.179
  907.2 17.1 copy-start.80
  907.2 17.1 copy-start.99
  945.7 9.2 copy-start.140
  945.7 9.2 collective-permute-start.2
  955.8 11.3 copy-start.176
  971.7 23.4 copy-start.29
  980.0 15.1 copy-start.5
  998.1 22.6 copy-start.182
  998.6 17.2 slice-start.13
  998.6 17.2 slice-start.14
  1006.1 9.7 slice-start.15
  1006.1 9.7 copy-start.36
  1026.3 32.6 %copy-start.23 = (f32[128,6912]{1,0:T(8,128)S(1)}, f32[128,6912]{1,0:T(8,128)}, u32[]{:S(2)}) copy-start(f32[128,6912]{1,0:T(8,128)} %copy-done.21) | copy-start | bytes 10616836 | tf_op jit(solution)/shard_map/cond
  1076.4 19.5 copy-start.100
  1086.1 9.8 copy-start.143
  1095.9 9.8 copy-start.177
  1125.7 17.1 copy-start.79
  1125.7 17.1 copy-start.97
  1151.6 9.9 copy-start.95
  1151.6 9.9 copy-start.103
  1175.4 236.0 %reduce-scatter.18.cloned.1.call-start = ((), (), s32[]{:S(2)}) async-start(), calls=%async_computation.14 | async-start | bytes 5640192
  1185.0 402.0 %reduce-scatter.16.cloned.1.call-start = ((), (), s32[]{:S(2)}) async-start(), calls=%async_computation.13 | async-start | bytes 16920576
  1207.5 596.8 %reduce-scatter.14.cloned.1.call-start = ((), (), s32[]{:S(2)}) async-start(), calls=%async_computation.12 | async-start | bytes 22560768 | tf_op jit(solution)/shard_map/reduce_scatter | solution.py:420
  1236.3 784.6 %reduce-scatter.12.cloned.1.call-start = ((), (), s32[]{:S(2)}) async-start(), calls=%async_computation.11 | async-start | bytes 22560768 | tf_op jit(solution)/shard_map/reduce_scatter | solution.py:419
  1264.9 1081.1 %reduce-scatter.10.cloned.1.call-start = ((), (), s32[]{:S(2)}) async-start(), calls=%async_computation.10 | async-start | bytes 33841152 | tf_op jit(solution)/shard_map/reduce_scatter | solution.py:415
  1309.0 63.9 %copy-start.155 = (f32[1152]{0:T(1024)S(1)}, f32[1152]{0:T(1024)}, u32[]{:S(2)}) copy-start(f32[1152]{0:T(1024)} %copy-done.154) | copy-start | bytes 13828
  1309.0 63.9 %copy-start.157 = (f32[1152]{0:T(1024)S(1)}, f32[1152]{0:T(1024)}, u32[]{:S(2)}) copy-start(f32[1152]{0:T(1024)} %copy-done.156) | copy-start | bytes 13828
  1312.2 98.1 %collective-permute-start.3 = (bf16[2,256,576]{1,2,0:T(8,128)(2,1)}, bf16[2,256,576]{1,2,0:T(8,128)(2,1)S(1)}, u32[]{:S(2)}, u32[]{:S(2)}) collective-permute-start(bf16[2,256,576]{1,2,0:T(8,128)(2,1)} %slice_select_fusion.2), channel_id=1, source_target_pairs={{0,16},{16,0},{1,17},{17,1},{2,18},{18,2},{3,19},{19,3},{4,20},{20... | collective-permute-start | bytes 1769480 | tf_op jit(solution)/shard_map/ppermute | solution.py:21
  (102 other events, 453.7 us)
Sparse Core Ops, SparseCore 0:
  10.3 46.2 all-gather.15
  58.7 70.7 all-gather.13
  131.8 87.0 all-gather.17
  221.0 86.8 all-gather.19
  309.9 119.6 all-gather.11
  1175.5 150.0 all-reduce.6
  1330.7 80.0 reduce-scatter.17
  1416.1 170.8 reduce-scatter.15
  1592.2 211.9 reduce-scatter.13
  1808.8 211.9 reduce-scatter.11
  2026.2 319.6 reduce-scatter.9
where the time goes:
time: 2370 us; the launch traced here: 2360 us
  waiting for transfers between devices  1310 us (55%)
  matrix products  459 us (19%)
  other arithmetic  173 us (7%)
  blocking collectives  160 us (7%)
  starting transfers between devices  122 us (5%)
  local copies, waits for them, and re-layouts  98 us (4%)
    reduce_scatter x1, waiting for transfers between devices, on_device(): lax.psum_scatter(grad_parts[0], 'dp', scatter_dimension=0, tiled=True)  325 us
    reduce_scatter x1, waiting for transfers between devices, on_device(): lax.psum_scatter(grad_parts[5], 'dp', scatter_dimension=0, tiled=True)  217 us
    reduce_scatter x1, waiting for transfers between devices, on_device(): lax.psum_scatter(grad_parts[4], 'dp', scatter_dimension=0, tiled=True)  217 us
    unnamed x13, waiting for transfers between devices  179 us
    add x6, other arithmetic, on_device(): before + after  133 us
    all_gather x1, waiting for transfers between devices, on_device(): lax.all_gather(ada_weight[0], 'dp', axis=0, tiled=True)  122 us
    ppermute x4, starting transfers between devices, from_partner(): lax.ppermute(x, axis, [(i, i ^ 1 << stride) for i in range(lax.axis_size(...  122 us
    all_gather x1, waiting for transfers between devices, on_device(): lax.all_gather(up_weight[0], 'dp', axis=0, tiled=True)  89.3 us
  transfers between devices with their start and end apart: 15, of which 11 were waited for; matrix products, arithmetic and copies ran while one was open for 6% of the time, Pallas kernels for 0%

commit v1 on v0

v1 whole, which is shorter than its diff:
```python
import functools
import math

import jax
import jax.numpy as jnp
from jax import lax
from jax.experimental import pallas as pl
from jax.experimental.pallas import tpu as pltpu
from jax.sharding import PartitionSpec as P

HEADS = 16
HD = 72
SMALL_PER = 4
ATT_ROWS = 256
EPS = 1e-6
MASKED = -1e30
MESH = pl.DeviceIdType.MESH
F32 = jnp.float32
BF16 = jnp.bfloat16


def remote(src, dst, send_sem, recv_sem, target):
    return pltpu.make_async_remote_copy(
        src_ref=src,
        dst_ref=dst,
        send_sem=send_sem,
        recv_sem=recv_sem,
        device_id=target,
        device_id_type=MESH,
    )


def when(condition, run):
    pl.when(condition)(run)


def position():
    me = lax.axis_index("dp")
    return me // 4, (me // 2) % 2, me % 2


def at(line, pair, core):
    return {"dp": (line * 2 + pair) * 2 + core}


def greet(length, a, b, c):
    has_up, has_down = a < length - 1, a > 0
    barrier = pltpu.get_barrier_semaphore()

    def tell(target):
        pl.semaphore_signal(barrier, inc=1, device_id=target, device_id_type=MESH)

    tell(at(a, 1 - b, c))
    tell(at(a, b, 1 - c))
    when(has_up, lambda: tell(at(a + 1, b, c)))
    when(has_down, lambda: tell(at(a - 1, b, c)))
    pl.semaphore_wait(barrier, 2 + has_up.astype(jnp.int32) + has_down.astype(jnp.int32))
    return has_up, has_down


def piece(ref, lead, plan_entry):
    _, low, size, _ = plan_entry
    if size == 0:
        return ref.at[lead + (low,)]
    return ref.at[lead + (slice(None), pl.ds(low, size))]


def gather_kernel(length, plan, count, *refs):
    sources = refs[:count]
    outs = refs[count : 2 * count]
    up_s, up_r, down_s, down_r, pair_s, pair_r, core_s, core_r, own_sem = refs[2 * count :]
    a, b, c = position()
    has_up, has_down = greet(length, a, b, c)
    chunks = range(len(plan))
    line_first = [plan[i][3] == "line" for i in chunks]

    def slot(i, aa, bb, cc):
        return piece(outs[plan[i][0]], (aa, bb, cc), plan[i])

    def own(i):
        return piece(sources[plan[i][0]], (), plan[i])

    def rows_of(i):
        return (b,) if line_first[i] else (b, 1 - b)

    def up(i, k, bb, src=None):
        s = slot(i, a - k, bb, c)
        return remote(s if src is None else src, s, up_s.at[i, k, bb], up_r.at[i, k, bb], at(a + 1, b, c))

    def up_arrival(i, k, bb):
        s = slot(i, a - 1 - k, bb, c)
        return remote(s, s, up_s.at[i, k, bb], up_r.at[i, k, bb], at(a + 1, b, c))

    def down(i, k, bb, src=None):
        s = slot(i, a + k, bb, c)
        return remote(s if src is None else src, s, down_s.at[i, k, bb], down_r.at[i, k, bb], at(a - 1, b, c))

    def down_arrival(i, k, bb):
        s = slot(i, a + 1 + k, bb, c)
        return remote(s, s, down_s.at[i, k, bb], down_r.at[i, k, bb], at(a - 1, b, c))

    def across(i, aa, src=None):
        s = slot(i, aa, b, c)
        return remote(s if src is None else src, s, pair_s.at[i, aa], pair_r.at[i, aa], at(a, 1 - b, c))

    def across_arrival(i, aa):
        s = slot(i, aa, 1 - b, c)
        return remote(s, s, pair_s.at[i, aa], pair_r.at[i, aa], at(a, 1 - b, c))

    def to_core(i, aa, bb, src=None):
        s = slot(i, aa, bb, c)
        return remote(s if src is None else src, s, core_s.at[i, aa, bb], core_r.at[i, aa, bb], at(a, b, 1 - c))

    def core_arrival(i, aa, bb):
        s = slot(i, aa, bb, 1 - c)
        return remote(s, s, core_s.at[i, aa, bb], core_r.at[i, aa, bb], at(a, b, 1 - c))

    def after_across(i, aa):
        across_arrival(i, aa).wait_recv()
        to_core(i, aa, 1 - b).start()

    for i in chunks:
        src = own(i)
        pltpu.make_async_copy(src, slot(i, a, b, c), own_sem.at[i]).start()
        across(i, a, src).start()
        when(has_up, lambda: up(i, 0, b, src).start())
        when(has_down, lambda: down(i, 0, b, src).start())
        to_core(i, a, b, src).start()
    for i in chunks:
        if not line_first[i]:
            across_arrival(i, a).wait_recv()
            when(has_up, lambda: up(i, 0, 1 - b).start())
            when(has_down, lambda: down(i, 0, 1 - b).start())
            to_core(i, a, 1 - b).start()
    for k in range(1, length):
        for i in chunks:
            for bb in rows_of(i):

                def from_below():
                    up_arrival(i, k - 1, bb).wait_recv()
                    when(has_up, lambda: up(i, k, bb).start())
                    if line_first[i]:
                        across(i, a - k).start()
                    to_core(i, a - k, bb).start()

                def from_above():
                    down_arrival(i, k - 1, bb).wait_recv()
                    when(has_down, lambda: down(i, k, bb).start())
                    if line_first[i]:
                        across(i, a + k).start()
                    to_core(i, a + k, bb).start()

                when(a - k >= 0, from_below)
                when(a + k <= length - 1, from_above)
            if line_first[i]:
                if k == 1:
                    after_across(i, a)
                else:
                    when(a - k + 1 >= 0, lambda: after_across(i, a - k + 1))
                    when(a + k - 1 <= length - 1, lambda: after_across(i, a + k - 1))
    for i in chunks:
        if line_first[i]:
            k = length - 1
            when(a - k >= 0, lambda: after_across(i, a - k))
            when(a + k <= length - 1, lambda: after_across(i, a + k))
    for i in chunks:
        pltpu.make_async_copy(own(i), slot(i, a, b, c), own_sem.at[i]).wait()
        for aa in range(length):
            for bb in range(2):
                core_arrival(i, aa, bb).wait_recv()
                to_core(i, aa, bb).wait_send()
            if line_first[i]:
                across(i, aa).wait_send()
        if not line_first[i]:
            across(i, a).wait_send()
        for k in range(length - 1):
            for bb in rows_of(i):
                when(jnp.logical_and(has_up, a - k >= 0), lambda: up(i, k, bb).wait_send())
                when(
                    jnp.logical_and(has_down, a + k <= length - 1),
                    lambda: down(i, k, bb).wait_send(),
                )


def gather_all(shards, plan, length):
    count, n = len(shards), len(plan)
    dma = pltpu.SemaphoreType.DMA
    anywhere = [pl.BlockSpec(memory_space=pl.ANY)] * count
    return pl.pallas_call(
        functools.partial(gather_kernel, length, plan, count),
        out_shape=tuple(jax.ShapeDtypeStruct((length, 2, 2) + s.shape, s.dtype) for s in shards),
        in_specs=anywhere,
        out_specs=anywhere,
        scratch_shapes=[dma((n, length, 2))] * 4
        + [dma((n, length))] * 2
        + [dma((n, length, 2))] * 2
        + [dma((n,))],
        compiler_params=pltpu.CompilerParams(collective_id=0, has_side_effects=True),
        name="gather_weights",
    )(*shards)


def scatter_kernel(length, plan, count, slots, *refs):
    grads = refs[:count]
    outs = refs[count : 2 * count]
    (held, core_in, pair_in, up_in, down_in) = refs[2 * count : 2 * count + 5]
    (
        core_s, core_r, load_sem, pair_s, pair_r, up_s, up_r, down_s, down_r, out_sem, credit,
    ) = refs[2 * count + 5 :]
    a, b, c = position()
    greet(length, a, b, c)
    n = len(plan)
    pair_first = [plan[i][3] == "pair" for i in range(n)]
    base, total = [], 0
    for i in range(n):
        base.append(total)
        total += (length - 1) * (1 if pair_first[i] else 2)

    def chunk_of(i, cc):
        w, low, size, _ = plan[i]
        if size == 0:
            return grads[w].at[:, :, cc, low]
        return grads[w].at[:, :, cc, :, pl.ds(low, size)]

    def to_core(i):
        return remote(chunk_of(i, 1 - c), core_in.at[i % slots], core_s.at[i], core_r.at[i], at(a, b, 1 - c))

    def load(i):
        return pltpu.make_async_copy(chunk_of(i, c), held.at[i], load_sem.at[i])

    def across(i):
        if pair_first[i]:
            return remote(held.at[i, :, 1 - b], pair_in.at[i], pair_s.at[i], pair_r.at[i], at(a, 1 - b, c))
        return remote(
            held.at[i, a, 1 - b], pair_in.at[i, 0], pair_s.at[i], pair_r.at[i], at(a, 1 - b, c)
        )

    def rows_of(i):
        return (b,) if pair_first[i] else (b, 1 - b)

    def flow_index(i, dest, bb):
        if pair_first[i]:
            return base[i] + dest
        return base[i] + dest * 2 + bb

    def up(i, line, dest, bb):
        x = flow_index(i, dest - 1, bb)
        return remote(held.at[i, dest, bb], up_in.at[x], up_s.at[x], up_r.at[x], at(line + 1, b, c))

    def down(i, line, dest, bb):
        x = flow_index(i, dest, bb)
        return remote(held.at[i, dest, bb], down_in.at[x], down_s.at[x], down_r.at[x], at(line - 1, b, c))

    def add(dst, src):
        dst[...] = dst[...] + src[...]

    def first_add(i):
        to_core(i).wait_recv()
        load(i).wait()

        def body(s, carry):
            add(held.at[i, s // 2, s % 2], core_in.at[i % slots, s // 2, s % 2])
            return carry

        lax.fori_loop(0, 2 * length, body, 0)
        if i + slots < n:
            pl.semaphore_signal(credit, inc=1, device_id=at(a, b, 1 - c), device_id_type=MESH)
        if pair_first[i]:
            across(i).start()

    def second_add(i):
        if not pair_first[i]:
            return
        across(i).wait_recv()

        def body(s, carry):
            add(held.at[i, s, b], pair_in.at[i, s])
            return carry

        lax.fori_loop(0, length, body, 0)

    def line_step(i, j):
        def going_up():
            for dest in range(length - 1, j - 1, -1):
                for bb in rows_of(i):
                    if j > 0:
                        up(i, j - 1, dest, bb).wait_recv()
                        add(held.at[i, dest, bb], up_in.at[flow_index(i, dest - 1, bb)])
                    if dest > j:
                        up(i, j, dest, bb).start()

        def going_down():
            here = length - 1 - j
            for dest in range(0, here + 1):
                for bb in rows_of(i):
                    if j > 0:
                        down(i, here + 1, dest, bb).wait_recv()
                        add(held.at[i, dest, bb], down_in.at[flow_index(i, dest, bb)])
                    if dest < here:
                        down(i, here, dest, bb).start()

        when(a == j, going_up)
        when(a == length - 1 - j, going_down)

    def result(i):
        w, low, size, _ = plan[i]
        dst = outs[w].at[low] if size == 0 else outs[w].at[:, pl.ds(low, size)]
        return pltpu.make_async_copy(held.at[i, a, b], dst, out_sem.at[i])

    def finish(i):
        if pair_first[i]:
            result(i).start()
        else:
            across(i).start()

    def finish_late(i):
        if not pair_first[i]:
            across(i).wait_recv()
            add(held.at[i, a, b], pair_in.at[i, 0])
            result(i).start()

    for i in range(n):
        load(i).start()
        if i < slots:
            to_core(i).start()
    for t in range(n + length + 3):
        if t < n:
            first_add(t)
            if t + slots < n:
                pl.semaphore_wait(credit, 1)
                to_core(t + slots).start()
        if 0 <= t - 1 < n:
            second_add(t - 1)
        for j in range(length):
            if 0 <= t - 2 - j < n:
                line_step(t - 2 - j, j)
        if 0 <= t - 1 - length < n:
            finish(t - 1 - length)
        if 0 <= t - 2 - length < n:
            finish_late(t - 2 - length)
    for i in range(n):
        to_core(i).wait_send()
        across(i).wait_send()
        result(i).wait()
        for bb in rows_of(i):
            for here in range(length):

                def sent():
                    for dest in range(here + 1, length):
                        up(i, here, dest, bb).wait_send()
                    for dest in range(0, here):
                        down(i, here, dest, bb).wait_send()

                when(a == here, sent)


def scatter_all(grads, plan, length):
    count, n = len(grads), len(plan)
    slots = 3
    rows = grads[0].shape[3]
    width = plan[0][2]
    dtype = grads[0].dtype
    flows = sum((length - 1) * (1 if p[3] == "pair" else 2) for p in plan)
    dma = pltpu.SemaphoreType.DMA
    anywhere = [pl.BlockSpec(memory_space=pl.ANY)] * count
    slab = (rows, width)
    return pl.pallas_call(
        functools.partial(scatter_kernel, length, plan, count, slots),
        out_shape=tuple(jax.ShapeDtypeStruct(g.shape[3:], dtype) for g in grads),
        in_specs=anywhere,
        out_specs=anywhere,
        scratch_shapes=[
            pltpu.VMEM((n, length, 2) + slab, dtype),
            pltpu.VMEM((slots, length, 2) + slab, dtype),
            pltpu.VMEM((n, length) + slab, dtype),
            pltpu.VMEM((flows,) + slab, dtype),
            pltpu.VMEM((flows,) + slab, dtype),
            dma((n,)), dma((n,)), dma((n,)), dma((n,)), dma((n,)),
            dma((flows,)), dma((flows,)), dma((flows,)), dma((flows,)), dma((n,)),
            pltpu.SemaphoreType.REGULAR,
        ],
        compiler_params=pltpu.CompilerParams(
            collective_id=1, has_side_effects=True, vmem_limit_bytes=60 * 1024 * 1024
        ),
        name="scatter_grads",
    )(*grads)


def head_window(h):
    low, high = h * HD, h * HD + HD
    start = low // 128 * 128
    return low, high, start, -(-high // 128) * 128


def contract(x, y, dims):
    return lax.dot_general(x, y, ((dims[0], dims[1]), ((), ())), preferred_element_type=F32)


def head_operands(qkv_ref, h):
    width = qkv_ref.shape[1] // 3
    low, high, start, stop = head_window(h)
    lane = lax.broadcasted_iota(jnp.int32, (1, stop - start), 1) + start
    inside = jnp.logical_and(lane >= low, lane < high)
    parts = [qkv_ref[:, j * width + start : j * width + stop] for j in range(3)]
    return inside, slice(start, stop), parts


def only(inside, x):
    return jnp.where(inside, x, jnp.zeros_like(x))


def softmax_of(query, key, allowed):
    scores = jnp.where(allowed, contract(query, key, ((1,), (1,))) * HD**-0.5, MASKED)
    weights = jnp.exp(scores - jnp.max(scores, axis=-1, keepdims=True))
    return weights * (1.0 / jnp.sum(weights, axis=-1, keepdims=True))


def attend_kernel(qkv_ref, row_ref, column_ref, out_ref, total):
    allowed = row_ref[...] == column_ref[0]
    total[...] = jnp.zeros_like(total)
    for h in range(HEADS):
        inside, window, (query, key, value) = head_operands(qkv_ref, h)
        probs = softmax_of(only(inside, query), key, allowed).astype(BF16)
        mixed = contract(probs, value, ((1,), (0,)))
        total[:, window] += only(inside, mixed)
    out_ref[...] = total[...].astype(BF16)


def attend_back_kernel(qkv_ref, grad_ref, row_ref, column_ref, out_ref, total):
    allowed = row_ref[...] == column_ref[0]
    width = grad_ref.shape[1]
    total[...] = jnp.zeros_like(total)
    for h in range(HEADS):
        inside, window, (query, key, value) = head_operands(qkv_ref, h)
        query, key = only(inside, query), only(inside, key)
        grad = only(inside, grad_ref[:, window])
        probs = softmax_of(query, key, allowed)
        grad_probs = contract(grad, value, ((1,), (1,)))
        centre = jnp.sum(probs * grad_probs, axis=-1, keepdims=True)
        grad_scores = (probs * (grad_probs - centre)).astype(BF16)
        start, stop = window.start, window.stop
        total[:, start:stop] += contract(grad_scores, key, ((1,), (0,))) * HD**-0.5
        total[:, width + start : width + stop] += contract(grad_scores, query, ((0,), (0,))) * HD**-0.5
        total[:, 2 * width + start : 2 * width + stop] += contract(probs.astype(BF16), grad, ((0,), (0,)))
    out_ref[...] = total[...].astype(BF16)


def attention_call(kernel, operands, segments, out_width, matmuls):
    rows = operands[0].shape[0]
    blocks = rows // ATT_ROWS
    row_ids = segments.reshape(rows, 1)
    column_ids = segments.reshape(blocks, 1, ATT_ROWS)
    wide = lambda n: pl.BlockSpec((ATT_ROWS, n), lambda i: (i, 0))
    return pl.pallas_call(
        kernel,
        grid=(blocks,),
        out_shape=jax.ShapeDtypeStruct((rows, out_width), BF16),
        in_specs=[wide(x.shape[1]) for x in operands]
        + [wide(1), pl.BlockSpec((1, 1, ATT_ROWS), lambda i: (i, 0, 0))],
        out_specs=wide(out_width),
        scratch_shapes=[pltpu.VMEM((ATT_ROWS, out_width), F32)],
        compiler_params=pltpu.CompilerParams(vmem_limit_bytes=32 * 1024 * 1024),
        cost_estimate=pl.CostEstimate(
            flops=matmuls * blocks * HEADS * 2 * ATT_ROWS**3,
            bytes_accessed=2 * rows * (out_width + sum(x.shape[1] for x in operands)),
            transcendentals=blocks * HEADS * ATT_ROWS**2,
        ),
    )(*operands, row_ids, column_ids)


def dot(x, y):
    return jnp.dot(x, y, preferred_element_type=F32)


def dot_back(x, y):
    return lax.dot_general(x, y, (((1,), (1,)), ((), ())), preferred_element_type=F32)


def dot_rows(x, y):
    return lax.dot_general(x, y, (((0,), (0,)), ((), ())), preferred_element_type=F32)


def flat(x):
    return x.reshape(-1, x.shape[-1])


def normal(x):
    centred = x - jnp.mean(x, axis=-1, keepdims=True)
    scale = lax.rsqrt(jnp.mean(centred * centred, axis=-1, keepdims=True) + EPS)
    return centred * scale, scale


def pieces_of(modulation):
    return [p[:, None, :] for p in jnp.split(modulation, 6, axis=-1)]


def block_forward(x, segments, modulation, weights):
    qkv_weight, proj_weight, up_weight, down_weight = weights
    shape, width = x.shape, x.shape[-1]
    shift1, scale1, gate1, shift2, scale2, gate2 = pieces_of(modulation)
    first_in = flat((normal(x)[0] * (1.0 + scale1) + shift1).astype(BF16))
    qkv = dot(first_in, qkv_weight).astype(BF16)
    attended = attention_call(attend_kernel, (qkv,), segments, width, 2)
    branch = dot(attended, proj_weight).reshape(shape)
    middle = x + gate1 * branch
    second_in = flat((normal(middle)[0] * (1.0 + scale2) + shift2).astype(BF16))
    hidden = dot(second_in, up_weight)
    active = jax.nn.gelu(hidden, approximate=True).astype(BF16)
    mlp = dot(active, down_weight).reshape(shape)
    output = middle + gate2 * mlp
    return output, (first_in, qkv, attended, branch, middle, second_in, hidden, active, mlp)


def norm_back(grad, x, scale):
    hat, inverse = normal(x)
    inner = grad * (1.0 + scale)
    along = jnp.mean(inner * hat, axis=-1, keepdims=True)
    grad_x = inverse * (inner - jnp.mean(inner, axis=-1, keepdims=True) - hat * along)
    return grad_x, jnp.sum(grad, axis=1), jnp.sum(grad * hat, axis=1)


def block_backward(x, segments, modulation, weights, kept, grad_out):
    qkv_weight, proj_weight, up_weight, down_weight = weights
    first_in, qkv, attended, branch, middle, second_in, hidden, active, mlp = kept
    shape, width = x.shape, x.shape[-1]
    shift1, scale1, gate1, shift2, scale2, gate2 = pieces_of(modulation)
    grad_mlp = flat((gate2 * grad_out).astype(BF16))
    grad_gate2 = jnp.sum(grad_out * mlp, axis=1)
    _, pull = jax.vjp(lambda h: jax.nn.gelu(h, approximate=True), hidden)
    grad_hidden = pull(dot_back(grad_mlp, down_weight))[0].astype(BF16)
    down_grad = dot_rows(active, grad_mlp).astype(BF16)
    grad_second = dot_back(grad_hidden, up_weight).reshape(shape)
    up_grad = dot_rows(second_in, grad_hidden).astype(BF16)
    grad_middle, grad_shift2, grad_scale2 = norm_back(grad_second, middle, scale2)
    grad_middle = grad_middle + grad_out
    grad_gate1 = jnp.sum(grad_middle * branch, axis=1)
    grad_branch = flat((gate1 * grad_middle).astype(BF16))
    grad_attended = dot_back(grad_branch, proj_weight).astype(BF16)
    proj_grad = dot_rows(attended, grad_branch).astype(BF16)
    grad_qkv = attention_call(attend_back_kernel, (qkv, grad_attended), segments, 3 * width, 5)
    grad_first = dot_back(grad_qkv, qkv_weight).reshape(shape)
    qkv_grad = dot_rows(first_in, grad_qkv).astype(BF16)
    grad_x, grad_shift1, grad_scale1 = norm_back(grad_first, x, scale1)
    grad_modulation = jnp.concatenate(
        [grad_shift1, grad_scale1, grad_gate1, grad_shift2, grad_scale2, grad_gate2], axis=-1
    )
    return grad_x + grad_middle, grad_modulation, (qkv_grad, proj_grad, up_grad, down_grad)


def plan_of(widths, lead, unit, other, last, names):
    plan = []
    for w, width in enumerate(widths):
        for low in range(0, width, unit):
            plan.append([w, low, unit, names[0]])
    for j in range(lead):
        plan.append([len(widths), j, 0, names[0]])
    chosen = range(len(plan) - other, len(plan)) if last else range(other)
    for j in chosen:
        plan[j][3] = names[1]
    return tuple(tuple(p) for p in plan)


def swap_sections(x):
    return lax.ppermute(x, "section", [(0, 1), (1, 0)])


def on_device(
    tokens, kept_index, big_image, timesteps, labels, cotangent, mask_token, time_weight, class_table,
    ada_weight, ada_bias, qkv_weight, proj_weight, up_weight, down_weight,
):
    section = lax.axis_index("section")
    me = lax.axis_index("dp")
    devices = lax.axis_size("dp")
    micro, slot, width = tokens.shape
    kept_count = kept_index.shape[1]
    own_width = ada_weight.shape[1]
    images = micro * SMALL_PER
    quarters = micro * SMALL_PER
    ada = ada_weight[0]

    ids = jnp.stack([timesteps, labels])
    ids = lax.all_gather(ids, "dp", axis=0)
    times = ids[:, 0].reshape(devices * images)
    classes = ids[:, 1].reshape(devices * images)
    half = time_weight.shape[0] // 2
    frequencies = jnp.exp(-math.log(10000.0) * jnp.arange(half, dtype=F32) / half)
    angles = times.astype(F32)[:, None] * frequencies[None, :]
    embedding = jnp.concatenate([jnp.cos(angles), jnp.sin(angles)], axis=-1).astype(BF16)
    onehot = (classes[:, None] == jnp.arange(class_table.shape[0])[None, :]).astype(BF16)
    cond = dot(embedding, time_weight) + dot(onehot, class_table)
    cond = lax.dynamic_slice_in_dim(cond, me * own_width, own_width, axis=1)
    lifted = jax.nn.silu(cond).astype(BF16)
    bias_width = ada_bias.shape[1]
    bias = lax.dynamic_update_slice_in_dim(
        jnp.zeros((1, 6 * width), F32), ada_bias.astype(F32), me * bias_width, axis=1
    )
    partial = (dot(lifted, ada) + bias).astype(BF16).reshape(devices, images, 6 * width)
    modulation = lax.psum_scatter(partial, "dp", scatter_dimension=0, tiled=False).astype(F32)

    shards = (qkv_weight[0], proj_weight[0], up_weight[0])
    lead = down_weight.shape[1] // qkv_weight.shape[1]
    down_shard = down_weight[0].reshape(lead, own_width, width)
    length = devices // 4
    widths = [s.shape[1] for s in shards]
    if length == 4:
        plan = plan_of(widths, lead, width, 2, True, ("line", "pair"))
        whole = gather_all(shards + (down_shard,), plan, length)
    else:
        whole = tuple(lax.all_gather(s, "dp", axis=0) for s in shards + (down_shard,))
    weights = tuple(w.reshape(-1, w.shape[-1]) for w in whole)

    big = big_image[:, :1] > 0
    modulation = modulation.reshape(micro, SMALL_PER, 6 * width)
    modulation = jnp.where(big[:, :, None], modulation[:, :1], modulation).reshape(quarters, 6 * width)
    quarter_ids = jnp.arange(quarters, dtype=jnp.int32).reshape(micro, SMALL_PER)
    segment_of = jnp.where(big, quarter_ids[:, :1], quarter_ids).reshape(quarters)
    positions = jnp.arange(slot, dtype=jnp.int32)
    placement = (positions[None, :, None] == kept_index[:, None, :]).astype(BF16)
    enc_segments = jnp.repeat(segment_of, kept_count // SMALL_PER)
    dec_segments = jnp.repeat(segment_of, slot // SMALL_PER)

    def to_kept(rows):
        return jnp.einsum("msk,msd->mkd", placement, rows, preferred_element_type=F32)

    def to_slots(rows):
        return jnp.einsum("msk,mkd->msd", placement, rows, preferred_element_type=F32)

    enc_rows = (quarters, kept_count // SMALL_PER, width)
    dec_rows = (quarters, slot // SMALL_PER, width)

    def encode():
        x = to_kept(tokens).reshape(enc_rows)
        out, kept = block_forward(x, enc_segments, modulation, weights)
        return out.astype(BF16), (x, kept)

    idle = lambda f: jax.tree.map(lambda s: jnp.zeros(s.shape, s.dtype), jax.eval_shape(f))
    encoded, enc_kept = lax.cond(section == 0, encode, lambda: idle(encode))
    received = swap_sections(encoded).reshape(micro, kept_count, width)

    def decode():
        flags = jnp.sum(placement.astype(F32), axis=2)[:, :, None]
        x = to_slots(received) + (1.0 - flags) * mask_token.astype(F32)[None, None, :]
        x = x.reshape(dec_rows)
        out, kept = block_forward(x, dec_segments, modulation, weights)
        grad = cotangent.astype(F32).reshape(dec_rows)
        grad_x, grad_mod, grads = block_backward(x, dec_segments, modulation, weights, kept, grad)
        grad_x = grad_x.reshape(micro, slot, width)
        mask_part = jnp.sum((1.0 - flags) * grad_x, axis=(0, 1))
        back = to_kept(grad_x.astype(BF16)).astype(BF16)
        return out.astype(BF16).reshape(micro, slot, width), mask_part, back, grad_mod, grads

    decoded, mask_part, back, grad_mod, grads = lax.cond(section == 1, decode, lambda: idle(decode))
    received = swap_sections(back)

    def encode_back():
        x, kept = enc_kept
        grad = received.astype(F32).reshape(enc_rows)
        grad_x, grad_mod, grads = block_backward(x, enc_segments, modulation, weights, kept, grad)
        grad_x = grad_x.astype(BF16).reshape(micro, kept_count, width)
        return to_slots(grad_x).astype(BF16), grad_mod, grads

    token_grad, grad_mod, grads = lax.cond(
        section == 0, encode_back, lambda: (jnp.zeros_like(decoded), grad_mod, grads)
    )

    half_width = width // 2
    outgoing = jnp.where(section == 0, token_grad[:, :, half_width:], decoded[:, :, :half_width])
    incoming = swap_sections(outgoing)
    decoded_half = jnp.where(section == 0, incoming, decoded[:, :, half_width:])
    token_half = jnp.where(section == 0, token_grad[:, :, :half_width], incoming)

    grad_mod = grad_mod.reshape(micro, SMALL_PER, 6 * width)
    first_only = (jnp.arange(SMALL_PER) == 0)[None, :, None]
    grad_mod = jnp.where(
        big[:, :, None], jnp.where(first_only, jnp.sum(grad_mod, axis=1, keepdims=True), 0.0), grad_mod
    )
    grad_mod = grad_mod.reshape(images, 6 * width).astype(BF16)
    every_mod = lax.all_gather(grad_mod, "dp", axis=0, tiled=True)
    ada_grad = dot_rows(lifted, every_mod)
    bias_grad = jnp.sum(
        lax.dynamic_slice_in_dim(every_mod, me * bias_width, bias_width, axis=1).astype(F32), axis=0
    )
    grad_lifted = dot_back(every_mod, ada)
    _, pull = jax.vjp(jax.nn.silu, cond)
    grad_cond = pull(grad_lifted)[0].astype(BF16)
    every_cond = lax.all_gather(grad_cond.T, ("section", "dp"), axis=0)
    every_cond = every_cond.reshape(2, width, devices * images)
    inputs = jnp.concatenate([embedding, onehot], axis=1)
    shared = lax.dot_general(
        jnp.concatenate([inputs, inputs], axis=0),
        jnp.concatenate([every_cond[0], every_cond[1]], axis=1),
        (((0,), (1,)), ((), ())),
        preferred_element_type=F32,
    )
    time_grad, table_grad = shared[: time_weight.shape[0]], shared[time_weight.shape[0] :]
    mask_grad = lax.psum(mask_part, ("section", "dp"))

    split = tuple(g.reshape((devices,) + s.shape) for g, s in zip(grads, shards + (down_shard,)))
    if length == 4:
        plan = plan_of(widths, lead, width, 2, False, ("pair", "line"))
        split = tuple(g.reshape((length, 2, 2) + g.shape[1:]) for g in split)
        mine = scatter_all(split, plan, length)
    else:
        mine = tuple(lax.psum_scatter(g, "dp", scatter_dimension=0) for g in split)
    qkv_grad, proj_grad, up_grad, down_grad = (g.astype(F32) for g in mine)
    return (
        decoded_half,
        token_half,
        mask_grad,
        time_grad,
        table_grad,
        ada_grad[None],
        bias_grad[None],
        qkv_grad[None],
        proj_grad[None],
        up_grad[None],
        down_grad.reshape(down_weight.shape),
    )


def solution(mesh):
    rows = P(None, "dp", None)
    ids = P(None, "dp")
    weight = P("section", "dp", None)
    halves = P(None, "dp", "section")
    in_specs = (rows, ids, ids, ids, ids, rows, P(), P(), P(), weight, P("section", "dp")) + (weight,) * 4
    out_specs = (halves, halves, P(), P(), P(), weight, P("section", "dp")) + (weight,) * 4
    return jax.shard_map(
        on_device, mesh=mesh, in_specs=in_specs, out_specs=out_specs, check_vma=False
    )
```

time: 2370 us -> 922 us (0.39)
  waiting for transfers between devices: 1310 us -> 16 us
  Pallas kernels: 0 us -> 390 us
  matrix products: 459 us -> 86.9 us
  other arithmetic: 173 us -> 46.9 us
  blocking collectives: 160 us -> 108 us
  starting transfers between devices: 122 us -> 164 us
    reduce_scatter x3 -> x1, waiting for transfers between devices: 759 us -> 0.02 us  [on_device(): lax.psum_scatter(partial, 'dp', scatter_dimension=0, tiled=False)]
    pallas_call x0 -> x4, Pallas kernels: none -> 390 us  [the longest x1 201 us: scatter_all(): pl.pallas_call(functools.partial(scatter_kernel, length, plan, count, slo...]
    dot_general x136 -> x20, matrix products: 449 us -> 86.9 us  [the longest x7 32.3 us: dot(): return jnp.dot(x, y, preferred_element_type=F32)]
    all_gather x5 -> x1, waiting for transfers between devices: 353 us -> 0.02 us  [on_device(): every_mod = lax.all_gather(grad_mod, 'dp', axis=0, tiled=True)]
    unnamed x13 -> x2, waiting for transfers between devices: 179 us -> 0.03 us
    add x9 -> x2, other arithmetic: 143 us -> 2.31 us  [the longest x1 1.63 us: norm_back(): inner = grad * (1.0 + scale)]
    unnamed x1 -> x0, blocking collectives: 58.5 us -> none
    ppermute x4 -> x3, starting transfers between devices: 122 us -> 164 us  [swap_sections(): return lax.ppermute(x, 'section', [(0, 1), (1, 0)])]
  transfers between devices with their start and end apart: 15 -> 5, of which waited for: 11 -> 1; matrix products, arithmetic and copies ran while one was open for 6% -> 1% of each run, Pallas kernels for 0% -> 41%
where the time goes in v1:
time: 922 us; the launch traced here: 912 us
  Pallas kernels  390 us (42%)
  starting transfers between devices  164 us (18%)
  blocking collectives  108 us (12%)
  matrix products  86.9 us (9%)
  local copies, waits for them, and re-layouts  81.5 us (9%)
  other arithmetic  46.9 us (5%)
  waiting for transfers between devices  16 us (2%)
  between operations  14.7 us (2%)
    pallas_call x1, Pallas kernels, scatter_all(): pl.pallas_call(functools.partial(scatter_kernel, length, plan, count, slo...  201 us
    pallas_call x1, Pallas kernels, gather_all(): pl.pallas_call(functools.partial(gather_kernel, length, plan, count), out...  173 us
    ppermute x3, starting transfers between devices, swap_sections(): return lax.ppermute(x, 'section', [(0, 1), (1, 0)])  164 us
    cond x4, local copies, waits for them, and re-layouts, on_device(): lax.cond(section == 0, encode_back, lambda: (jnp.zeros_like(decoded), gra...  45.4 us
    psum x1, blocking collectives, on_device(): mask_grad = lax.psum(mask_part, ('section', 'dp'))  43.8 us
    all_gather x1, blocking collectives, on_device(): every_cond = lax.all_gather(grad_cond.T, ('section', 'dp'), axis=0)  40.7 us
    dot_general x7, matrix products, dot(): return jnp.dot(x, y, preferred_element_type=F32)  32.3 us
    dot_general x5, matrix products, dot_rows(): lax.dot_general(x, y, (((0,), (0,)), ((), ())), preferred_element_type=F32)  28.1 us
  transfers between devices with their start and end apart: 5, of which 1 were waited for; matrix products, arithmetic and copies ran while one was open for 1% of the time, Pallas kernels for 41%

profile of v1, /device:TPU:0, one launch (start us, length us, event | category | flops | bytes accessed | tf_op | source)
XLA Modules:
  0.0 912.5 jit_solution(5368542201988180120)
XLA Ops:
  8.1 23.3 %all-gather = s32[32,2,4]{2,1,0:T(2,128)S(1)} all-gather(s32[2,2,4]{2,1,0:T(2,128)S(1)} %pad_add_fusion), channel_id=2, replica_groups=mesh['section'=2,'dp'=16] {'dp'}, dimensions={0}, use_global_device_ids=true | all-gather | bytes 1088 | tf_op jit(solution)/shard_map/all_gather | solution.py:582
  32.7 1.9 fusion.96
  34.6 1.4 fusion.101
  37.9 1.9 fusion.76
  40.5 173.2 %gather_weights.1 = (bf16[4,2,2,72,3456]{4,3,2,1,0:T(8,128)(2,1)}, bf16[4,2,2,72,1152]{4,3,2,1,0:T(8,128)(2,1)}, bf16[4,2,2,72,4608]{4,3,2,1,0:T(8,128)(2,1)}, bf16[4,2,2,4,72,1152]{5,4,3,2,1,0:T(8,128)(2,1)}) custom-call(bf16[72,3456]{1,0:T(8,128)(2,1)} %bitcast.389, bf16[72,1152]{1,0:T(8,128)(2,1)} %bitcast.391, bf16[72,4608]{1,0:T(8,128)(2,1)} %bitcast.386, ...), custom_call_target="tpu_custom_call" | custom-call | tf_op jit(solution)/shard_map/gather_weights/pallas_call | solution.py:189
  216.6 49.8 %conditional.3 = (bf16[8,32,1152]{2,1,0:T(8,128)(2,1)}, f32[8,32,1152]{2,1,0:T(8,128)}, bf16[256,1152]{1,0:T(8,128)(2,1)}, bf16[256,3456]{1,0:T(8,128)(2,1)}, bf...) conditional(s32[]{:T(128)} %convert_element_type.209, () %tuple.47, ...), branch_computations={%region_1.2_spmd, %region_2.7_spmd} | conditional | flops 9398536192 | bytes 114729152 | solution.py:637
  216.9 2.7 fusion.121
  219.6 1.5 multiply_reduce_fusion.1
  221.2 2.4 fusion.13
  223.5 7.2 convolution_convert_fusion.qkv_ref
  230.9 5.0 branch_1_fun.7
  236.0 3.1 fusion.127
  239.1 1.9 fusion.15
  241.0 2.0 multiply_reduce_fusion
  243.0 3.0 fusion.8
  246.0 10.8 %fusion.7 = (bf16[256,4608]{1,0:T(8,128)(2,1)}, f32[256,4608]{1,0:T(8,128)}) fusion(bf16[256,1152]{1,0:T(8,128)(2,1)} %fusion.8, bf16[1152,4608]{1,0:T(8,128)(2,1)} %get-tuple-element.158), kind=kOutput, calls=%fused_computation.9 | convolution fusion | flops 2728525824 | bytes 18284544 | tf_op jit(solution)/shard_map/cond/branch_1_fun/dot_general | solution.py:472
  256.9 6.0 fusion.128
  262.8 3.1 add_convert_fusion
  266.5 15.9 %collective-permute-done = bf16[8,32,1152]{2,1,0:T(8,128)(2,1)} collective-permute-done((bf16[8,32,1152]{2,1,0:T(8,128)(2,1)}, bf16[8,32,1152]{2,1,0:T(8,128)(2,1)}, u32[]{:S(2)}, u32[]{:S(2)}) %collective-permute-start) | collective-permute-done | bytes 589856 | tf_op jit(solution)/shard_map/ppermute | solution.py:564
  282.4 21.9 %conditional.4 = (f32[1152]{0:T(1024)}, bf16[2,128,1152]{1,2,0:T(8,128)(2,1)}, f32[8,6912]{1,0:T(8,128)}, bf16[1152,3456]{1,0:T(8,128)(2,1)}, bf16[1152,1152]{1,...) conditional(s32[]{:T(128)} %convert_element_type.210, () %tuple.46, ...), branch_computations={%region_7.8_spmd, %region_8.25_spmd} | conditional | flops 56903139328 | bytes 550815488 | solution.py:652
  282.4 4.7 broadcast.497
  287.1 4.7 broadcast.498
  291.8 3.7 broadcast.495
  295.5 1.7 broadcast.496
  304.4 1.4 copy.74
  305.7 164.0 %collective-permute-start.1 = (bf16[2,128,1152]{2,1,0:T(8,128)(2,1)S(1)}, bf16[2,128,1152]{2,1,0:T(8,128)(2,1)S(1)}, u32[]{:S(2)}, u32[]{:S(2)}) collective-permute-start(bf16[2,128,1152]{2,1,0:T(8,128)(2,1)S(1)} %copy.74), channel_id=1, source_target_pairs={{0,16},{16,0},{1,17},{17,1},{2,18},{18,2},{3,19},{19,3},{4,20},{20... | collective-permute-start | bytes 1769480 | tf_op jit(solution)/shard_map/ppermute | solution.py:564
  470.4 1.5 fusion.95
  471.9 43.8 %psum.7 = f32[1152]{0:T(1024)} all-reduce(f32[1152]{0:T(1024)} %get-tuple-element.264), channel_id=1, replica_groups=mesh['section'=2,'dp'=16] {'section','dp'}, use_global_device_ids=true, to_apply=%region_41.42 | all-reduce | flops 1152 | bytes 9216 | tf_op jit(solution)/shard_map/psum | solution.py:696
  515.6 125.2 %conditional.5 = (f32[8,6912]{1,0:T(8,128)}, bf16[2,256,576]{1,2,0:T(8,128)(2,1)}, bf16[2,256,576]{1,2,0:T(8,128)(2,1)}, bf16[1152,3456]{1,0:T(8,128)(2,1)}, bf1...) conditional(s32[]{:T(128)} %convert_element_type.209, ...), branch_computations={%region_25.26_spmd, %region_26.41_spmd} | conditional | flops 19199389696 | bytes 276077280 | solution.py:662
  515.7 1.6 slice_add_fusion.4
  517.5 8.8 fusion.67
  526.3 3.3 fusion.71
  530.1 2.8 fusion.73
  534.8 2.6 multiply_reduce_fusion.11
  537.6 1.0 convolution_convert_fusion.13.grad_ref
  538.9 10.6 %branch_1_fun.10 = bf16[256,3456]{1,0:T(8,128)(2,1)S(1)} custom-call(bf16[256,3456]{1,0:T(8,128)(2,1)} %get-tuple-element.175.qkv_ref, bf16[256,1152]{1,0:T(8,128)(2,1)S(1)} %convolution_convert_fusion.13.grad_ref, s32[256,1]{1,0:T(8,128)S(1)} %reshape_reshape.35.row_ref, s32[1,1,256]{2,1,0:T(1,128)S(1)} %reshape_reshape.25.column_ref), custom_call_target="tpu_custom_call" | custom-call | flops 2684354560 | bytes 4128768 | tf_op jit(solution)/shard_map/cond/branch_1_fun/pallas_call | solution.py:454
  549.5 6.7 fusion.59
  556.3 11.6 %copy.93 = bf16[1152,3456]{1,0:T(8,128)(2,1)} copy(bf16[1152,3456]{0,1:T(8,128)(2,1)} %fusion.59) | data formatting | bytes 15925248 | tf_op jit(solution)/shard_map/cond | solution.py:662
  567.9 6.8 bitcast_multiply_fusion.18
  574.9 1.5 reduce_sum.349
  576.5 1.6 multiply_reduce_fusion.12
  578.1 1.8 multiply_reduce_fusion.9
  580.0 1.8 add_convert_fusion.1
  582.3 1.1 fusion.125
  587.1 2.1 fusion.60
  589.2 3.3 copy.95
  592.5 9.0 fusion.57
  601.5 15.3 %copy.97 = bf16[1152,4608]{1,0:T(8,128)(2,1)} copy(bf16[1152,4608]{0,1:T(8,128)(2,1)} %fusion.57) | data formatting | bytes 21233664 | tf_op jit(solution)/shard_map/cond | solution.py:662
  616.8 8.6 fusion.58
  625.4 15.3 %copy.99 = bf16[4608,1152]{1,0:T(8,128)(2,1)} copy(bf16[4608,1152]{0,1:T(8,128)(2,1)} %fusion.58) | data formatting | bytes 21233664 | tf_op jit(solution)/shard_map/cond | solution.py:662
  640.9 1.0 reshape.623
  642.1 1.7 select_convert_fusion
  643.8 1.1 broadcast_select_fusion.2
  645.0 201.0 %scatter_grads.1 = (bf16[72,3456]{1,0:T(8,128)(2,1)}, bf16[72,1152]{1,0:T(8,128)(2,1)}, bf16[72,4608]{1,0:T(8,128)(2,1)}, bf16[4,72,1152]{2,1,0:T(8,128)(2,1)}) custom-call(bf16[4,2,2,72,3456]{4,3,2,1,0:T(8,128)(2,1)} %bitcast.72.refs_0_, bf16[4,2,2,72,1152]{4,3,2,1,0:T(8,128)(2,1)} %bitcast.73.refs_1_, bf16[4,2,2,72,4608]{4,3,2,1,0:T(8,128)(2,1)} %bitcast.74.refs_2_, ...), custom_call_target="tpu_custom_call" | custom-call | tf_op jit(solution)/shard_map/scatter_grads/pallas_call | solution.py:367
  846.0 2.1 bitcast_convert_fusion.2
  848.1 2.3 bitcast_convert_fusion.1
  851.1 1.1 bitcast_convert_fusion
  852.3 2.2 broadcast_select_fusion
  854.5 2.3 fusion.110
  856.8 40.7 %all-gather.1 = bf16[2304,128]{1,0:T(8,128)(2,1)S(1)} all-gather(bf16[72,128]{1,0:T(8,128)(2,1)S(1)} %fusion.110), channel_id=3, replica_groups=mesh['section'=2,'dp'=16] {'section','dp'}, dimensions={0}, use_global_device_ids=true | all-gather | bytes 608256 | tf_op jit(solution)/shard_map/all_gather | solution.py:686
  897.6 1.1 fusion.80
  898.6 2.5 slice.79
  901.1 1.1 slice.78
  903.0 1.7 convolution_bitcast_fusion
  (188 shorter events, 22.5 us)
Async XLA Ops:
  7.2 25.5 %copy-start = (bf16[1000,1152]{1,0:T(8,128)(2,1)S(1)}, bf16[1000,1152]{1,0:T(8,128)(2,1)}, u32[]{:S(2)}) copy-start(bf16[1000,1152]{1,0:T(8,128)(2,1)} %param.29) | copy-start | bytes 6912004
  7.2 30.8 %copy-start.32 = (bf16[1,72,6912]{2,1,0:T(8,128)(2,1)S(1)}, bf16[1,72,6912]{2,1,0:T(8,128)(2,1)}, u32[]{:S(2)}) copy-start(bf16[1,72,6912]{2,1,0:T(8,128)(2,1)} %param.30) | copy-start | bytes 2985988
  7.2 206.6 %reduce-scatter.2.cloned.1.call-start = ((), (), s32[]{:S(2)}) async-start(), calls=%async_computation.1 | async-start | bytes 1880064 | tf_op jit(solution)/shard_map/reduce_scatter | solution.py:598
  31.7 8.2 copy-start.94
  32.7 7.2 copy-start.57
  32.7 7.1 copy-start.59
  36.0 0.8 copy-start.48
  36.8 3.1 copy-start.101
  37.6 176.1 %copy-start.61 = (bf16[128,72]{0,1:T(8,128)(2,1)}, bf16[128,72]{0,1:T(8,128)(2,1)S(1)}, u32[]{:S(2)}) copy-start(bf16[128,72]{0,1:T(8,128)(2,1)S(1)} %multiply_convert_fusion.4) | copy-start | bytes 55300
  39.8 173.9 %copy-start.96 = (s32[2,128]{1,0:T(2,128)S(1)}, s32[2,128]{1,0:T(2,128)}, u32[]{:S(2)}) copy-start(s32[2,128]{1,0:T(2,128)} %param.22) | copy-start | bytes 3076
  39.9 814.6 %all-gather.4.cloned.1.call-start = ((), (), s32[]{:S(2)}) async-start(), calls=%async_computation.2 | async-start | bytes 1880064 | tf_op jit(solution)/shard_map/all_gather | solution.py:678
  40.1 175.9 %copy-start.93 = (pred[8]{0:T(512)(128)(4,1)}, pred[8]{0:T(512)(128)(4,1)S(1)}, u32[]{:S(2)}) copy-start(pred[8]{0:T(512)(128)(4,1)S(1)} %broadcast_in_dim.175) | copy-start | bytes 28
  213.8 68.6 %copy-start.27 = (bf16[2,256,128]{2,1,0:T(8,128)(2,1)}, bf16[2,256,128]{2,1,0:T(8,128)(2,1)S(1)}, u32[]{:S(2)}) copy-start(bf16[2,256,128]{2,1,0:T(8,128)(2,1)S(1)} %fusion.98) | copy-start | bytes 393220
  215.9 66.4 %copy-start.34 = (f32[8,6912]{1,0:T(8,128)}, f32[8,6912]{1,0:T(8,128)S(1)}, u32[]{:S(2)}) copy-start(f32[8,6912]{1,0:T(8,128)S(1)} %convert_select_fusion) | copy-start | bytes 663556
  216.0 0.6 copy-start.69
  216.0 66.4 %copy-start.20 = (bf16[2,256,1152]{2,1,0:T(8,128)(2,1)S(1)}, bf16[2,256,1152]{2,1,0:T(8,128)(2,1)}, u32[]{:S(2)}) copy-start(bf16[2,256,1152]{2,1,0:T(8,128)(2,1)} %param.26) | copy-start | bytes 3538948
  216.0 66.4 %copy-start.95 = (bf16[1152]{0:T(1024)(128)(2,1)S(1)}, bf16[1152]{0:T(1024)(128)(2,1)}, u32[]{:S(2)}) copy-start(bf16[1152]{0:T(1024)(128)(2,1)} %param.27) | copy-start | bytes 6916
  230.9 5.0 copy-start.97
  243.0 13.8 %slice-start.2 = ((s8[10616832]{0:T(1024)(128)(4,1)}), s8[4194304]{0:T(1024)(128)(4,1)S(1)}, s32[]{:S(2)}) async-start(s8[10616832]{0:T(1024)(128)(4,1)} %bitcast.369), calls=%async_computation.5 | async-start | bytes 8388608 | tf_op jit(solution)/shard_map/cond
  246.0 10.9 %slice-start.3 = ((s8[10616832]{0:T(1024)(128)(4,1)}), s8[4194304]{0:T(1024)(128)(4,1)S(1)}, s32[]{:S(2)}) async-start(s8[10616832]{0:T(1024)(128)(4,1)} %bitcast.369), calls=%async_computation.6 | async-start | bytes 8388608 | tf_op jit(solution)/shard_map/cond
  246.0 10.9 %slice-start.4 = ((s8[10616832]{0:T(1024)(128)(4,1)}), s8[2228224]{0:T(1024)(128)(4,1)S(1)}, s32[]{:S(2)}) async-start(s8[10616832]{0:T(1024)(128)(4,1)} %bitcast.369), calls=%async_computation.7 | async-start | bytes 4456448 | tf_op jit(solution)/shard_map/cond
  266.4 16.0 %copy-start.13 = (f32[8,32,1152]{2,1,0:T(8,128)}, f32[8,32,1152]{2,1,0:T(8,128)S(1)}, u32[]{:S(2)}) copy-start(f32[8,32,1152]{2,1,0:T(8,128)S(1)} %get-tuple-element.249) | copy-start | bytes 3538948
  266.4 16.0 %collective-permute-start = (bf16[8,32,1152]{2,1,0:T(8,128)(2,1)}, bf16[8,32,1152]{2,1,0:T(8,128)(2,1)}, u32[]{:S(2)}, u32[]{:S(2)}) collective-permute-start(bf16[8,32,1152]{2,1,0:T(8,128)(2,1)} %get-tuple-element.243), channel_id=1, source_target_pairs={{0,16},{16,0},{1,17},{17,1},{2,18},{18,2},{3,19},{19,3},{4,20},{20... | collective-permute-start | bytes 1769480 | tf_op jit(solution)/shard_map/ppermute | solution.py:564
  282.4 233.3 %copy-start.70 = (s32[8,32]{1,0:T(8,128)S(1)}, s32[8,32]{1,0:T(8,128)}, u32[]{:S(2)}) copy-start(s32[8,32]{1,0:T(8,128)} %copy-done.69) | copy-start | bytes 3076
  305.7 209.9 %collective-permute-start.1 = (bf16[2,128,1152]{2,1,0:T(8,128)(2,1)S(1)}, bf16[2,128,1152]{2,1,0:T(8,128)(2,1)S(1)}, u32[]{:S(2)}, u32[]{:S(2)}) collective-permute-start(bf16[2,128,1152]{2,1,0:T(8,128)(2,1)S(1)} %copy.74), channel_id=1, source_target_pairs={{0,16},{16,0},{1,17},{17,1},{2,18},{18,2},{3,19},{19,3},{4,20},{20... | collective-permute-start | bytes 1769480 | tf_op jit(solution)/shard_map/ppermute | solution.py:564
  515.7 10.6 %copy-start.37 = (bf16[2,128,1152]{2,1,0:T(8,128)(2,1)}, bf16[2,128,1152]{2,1,0:T(8,128)(2,1)S(1)}, u32[]{:S(2)}) copy-start(bf16[2,128,1152]{2,1,0:T(8,128)(2,1)S(1)} %get-tuple-element.178) | copy-start | bytes 1769476 | tf_op jit(solution)/shard_map/cond
  517.3 9.0 copy-start.54
  517.4 8.8 copy-start.35
  517.4 8.9 slice-start.5
  517.4 8.9 slice-start.6
  517.4 8.9 slice-start.7
  526.3 3.4 copy-start.22
  526.3 3.3 copy-start.14
  534.8 2.7 copy-start.64
  534.8 2.8 copy-start.100
  537.5 1.2 copy-start.23
  537.6 1.1 copy-start.30
  556.3 11.6 %copy-start.50 = (f32[8,1152]{1,0:T(8,128)S(1)}, f32[8,1152]{1,0:T(8,128)}, u32[]{:S(2)}) copy-start(f32[8,1152]{1,0:T(8,128)} %get-tuple-element.395) | copy-start | bytes 110596 | tf_op jit(solution)/shard_map/cond
  574.7 3.4 copy-start.26
  576.5 3.5 copy-start.24
  579.9 1.8 copy-start.29
  581.7 2.9 copy-start.68
  581.7 3.5 copy-start.67
  581.8 4.1 copy-start.66
  581.8 4.8 copy-start.65
  581.8 5.4 copy-start.31
  601.5 15.3 %copy-start.36 = (bf16[256,1152]{1,0:T(8,128)(2,1)S(1)}, bf16[256,1152]{1,0:T(8,128)(2,1)}, u32[]{:S(2)}) copy-start(bf16[256,1152]{1,0:T(8,128)(2,1)} %copy-done.35) | copy-start | bytes 1769476 | tf_op jit(solution)/shard_map/cond
  644.9 207.4 %collective-permute-start.2 = (bf16[2,256,576]{1,2,0:T(8,128)(2,1)S(1)}, bf16[2,256,576]{1,2,0:T(8,128)(2,1)S(1)}, u32[]{:S(2)}, u32[]{:S(2)}) collective-permute-start(bf16[2,256,576]{1,2,0:T(8,128)(2,1)S(1)} %broadcast_select_fusion.2), channel_id=1, source_target_pairs={{0,16},{16,0},{1,17},{17,1},{2,18},{18,2},{3,19},{19,3},{4,20},{20... | collective-permute-start | bytes 1769480 | tf_op jit(solution)/shard_map/ppermute | solution.py:564
  846.0 4.4 copy-start.63
  846.0 5.1 copy-start.49
  851.1 3.4 copy-start.33
  854.5 43.1 %copy-start.43 = (bf16[128,1000]{1,0:T(8,128)(2,1)S(1)}, bf16[128,1000]{1,0:T(8,128)(2,1)}, u32[]{:S(2)}) copy-start(bf16[128,1000]{1,0:T(8,128)(2,1)} %fusion.95) | copy-start | bytes 768004
  854.5 43.1 %copy-start.58 = (bf16[128,128]{1,0:T(8,128)(2,1)S(1)}, bf16[128,128]{1,0:T(8,128)(2,1)}, u32[]{:S(2)}) copy-start(bf16[128,128]{1,0:T(8,128)(2,1)} %copy-done.57) | copy-start | bytes 98308
  854.5 43.1 %copy-start.60 = (bf16[128,128]{1,0:T(8,128)(2,1)S(1)}, bf16[128,128]{1,0:T(8,128)(2,1)}, u32[]{:S(2)}) copy-start(bf16[128,128]{1,0:T(8,128)(2,1)} %copy-done.59) | copy-start | bytes 98308
  901.1 1.9 copy-start.25
  901.1 1.9 copy-start.62
  901.1 4.3 copy-start.1
Sparse Core Ops, SparseCore 0:
  40.0 64.7 reduce-scatter.1
  643.9 46.0 all-gather.3

commit v2 on v1

--- a/solution.py
+++ b/solution.py
@@ -200,40 +200,109 @@
     )(*shards)
 
 
-def scatter_kernel(length, plan, count, slots, *refs):
-    grads = refs[:count]
-    outs = refs[count : 2 * count]
-    (held, core_in, pair_in, up_in, down_in) = refs[2 * count : 2 * count + 5]
+def scatter_kernel(length, plan, slots, pair_slots, *refs):
+    lefts, rights = refs[:4], refs[4:8]
+    outs = refs[8:12]
     (
-        core_s, core_r, load_sem, pair_s, pair_r, up_s, up_r, down_s, down_r, out_sem, credit,
-    ) = refs[2 * count + 5 :]
+        raw, right, left_t, held, sent, core_in, pair_in, pair_late, up_in, down_in,
+    ) = refs[12:22]
+    (
+        raw_sem, right_sem, core_s, core_r, pair_s, pair_r, up_s, up_r, down_s, down_r, out_sem,
+        core_credit, pair_credit,
+    ) = refs[22:]
     a, b, c = position()
     greet(length, a, b, c)
     n = len(plan)
-    pair_first = [plan[i][3] == "pair" for i in range(n)]
+    rows, width = held.shape[3:]
+    total_rows = raw.shape[1]
+    pair_first = [p[3] == "pair" for p in plan]
+    order = [sum(pair_first[:i]) if pair_first[i] else i - sum(pair_first[:i]) for i in range(n)]
     base, total = [], 0
     for i in range(n):
         base.append(total)
         total += (length - 1) * (1 if pair_first[i] else 2)
-
-    def chunk_of(i, cc):
+    groups = 2 * length
+
+    def blocks_of(w):
+        return lefts[w].shape[1] // width
+
+    raw_jobs = []
+    right_jobs = []
+    for i, (w, low, size, _) in enumerate(plan):
+        if i == 0 or plan[i - 1][0] != w:
+            raw_jobs += [(w, k) for k in range(blocks_of(w))]
+        if size != 0 or plan[i - 1][0] != w:
+            right_jobs.append(i)
+
+    def raw_load(x):
+        w, k = raw_jobs[x]
+        src = lefts[w].at[:, pl.ds(k * width, width)]
+        return pltpu.make_async_copy(src, raw.at[x % 2], raw_sem.at[x])
+
+    def right_load(x):
+        w, low, size, _ = plan[right_jobs[x]]
+        src = rights[w].at[:, pl.ds(low if size else 0, width)]
+        return pltpu.make_async_copy(src, right.at[x % 2], right_sem.at[x])
+
+    progress = {"raw": 0, "right": -1}
+
+    def turn(w):
+        count = blocks_of(w)
+        for k in range(count):
+            x = progress["raw"]
+            progress["raw"] += 1
+            raw_load(x).wait()
+            slot = x % 2
+
+            def body(r, carry):
+                start = pl.multiple_of(r * 128, 128)
+                block = raw[slot, pl.ds(start, 128), :].astype(F32).T
+                if count == 1:
+                    split = block.reshape(groups, 2, rows, 128)
+                    for q in range(2):
+                        part = split[:, q].reshape(groups * rows, 128)
+                        left_t[q, :, pl.ds(start, 128)] = part.astype(BF16)
+                else:
+                    near = groups // count
+                    split = block.reshape(near, 2, count, rows, 128)
+                    for q in range(2):
+                        for j in range(count):
+                            part = split[:, q, j].reshape(near * rows, 128)
+                            left_t[
+                                q * count + j, pl.ds(k * near * rows, near * rows), pl.ds(start, 128)
+                            ] = part.astype(BF16)
+                return carry
+
+            lax.fori_loop(0, total_rows // 128, body, 0)
+            if x + 2 < len(raw_jobs):
+                raw_load(x + 2).start()
+
+    def product(i, q, put):
         w, low, size, _ = plan[i]
-        if size == 0:
-            return grads[w].at[:, :, cc, low]
-        return grads[w].at[:, :, cc, :, pl.ds(low, size)]
+        count = blocks_of(w)
+        row_set = q if count == 1 else q * count + low
+        slot = progress["right"] % 2
+        tile = width // 3
+
+        def body(k, carry):
+            columns = pl.ds(pl.multiple_of(k * tile, 128), tile)
+            result = jnp.dot(left_t[row_set], right[slot, :, columns], preferred_element_type=F32)
+            for s in range(groups):
+                put(s, columns, result[s * rows : (s + 1) * rows].astype(BF16))
+            return carry
+
+        lax.fori_loop(0, 3, body, 0)
 
     def to_core(i):
-        return remote(chunk_of(i, 1 - c), core_in.at[i % slots], core_s.at[i], core_r.at[i], at(a, b, 1 - c))
-
-    def load(i):
-        return pltpu.make_async_copy(chunk_of(i, c), held.at[i], load_sem.at[i])
+        return remote(sent.at[i % slots], core_in.at[i % slots], core_s.at[i], core_r.at[i], at(a, b, 1 - c))
 
     def across(i):
+        target = at(a, 1 - b, c)
         if pair_first[i]:
-            return remote(held.at[i, :, 1 - b], pair_in.at[i], pair_s.at[i], pair_r.at[i], at(a, 1 - b, c))
-        return remote(
-            held.at[i, a, 1 - b], pair_in.at[i, 0], pair_s.at[i], pair_r.at[i], at(a, 1 - b, c)
-        )
+            return remote(
+                held.at[i, :, 1 - b], pair_in.at[order[i] % pair_slots], pair_s.at[i], pair_r.at[i], target
+            )
+        return remote(held.at[i, a, 1 - b], pair_late.at[order[i]], pair_s.at[i], pair_r.at[i], target)
 
     def rows_of(i):
         return (b,) if pair_first[i] else (b, 1 - b)
@@ -254,18 +323,46 @@
     def add(dst, src):
         dst[...] = dst[...] + src[...]
 
+    def credit(sem, target):
+        pl.semaphore_signal(sem, inc=1, device_id=target, device_id_type=MESH)
+
+    def produce(i):
+        w = plan[i][0]
+        if i == 0 or plan[i - 1][0] != w:
+            turn(w)
+        if progress["right"] + 1 < len(right_jobs) and right_jobs[progress["right"] + 1] == i:
+            progress["right"] += 1
+            right_load(progress["right"]).wait()
+            if progress["right"] + 1 < len(right_jobs):
+                right_load(progress["right"] + 1).start()
+        if i >= slots:
+            to_core(i - slots).wait_send()
+
+        def put_sent(s, columns, value):
+            sent[i % slots, s // 2, s % 2, :, columns] = value
+
+        def put_held(s, columns, value):
+            held[i, s // 2, s % 2, :, columns] = value
+
+        product(i, 1 - c, put_sent)
+        if i >= slots:
+            pl.semaphore_wait(core_credit, 1)
+        to_core(i).start()
+        product(i, c, put_held)
+
     def first_add(i):
         to_core(i).wait_recv()
-        load(i).wait()
 
         def body(s, carry):
             add(held.at[i, s // 2, s % 2], core_in.at[i % slots, s // 2, s % 2])
             return carry
 
-        lax.fori_loop(0, 2 * length, body, 0)
+        lax.fori_loop(0, groups, body, 0)
         if i + slots < n:
-            pl.semaphore_signal(credit, inc=1, device_id=at(a, b, 1 - c), device_id_type=MESH)
+            credit(core_credit, at(a, b, 1 - c))
         if pair_first[i]:
+            if order[i] >= pair_slots:
+                pl.semaphore_wait(pair_credit, 1)
             across(i).start()
 
     def second_add(i):
@@ -274,10 +371,12 @@
         across(i).wait_recv()
 
         def body(s, carry):
-            add(held.at[i, s, b], pair_in.at[i, s])
+            add(held.at[i, s, b], pair_in.at[order[i] % pair_slots, s])
             return carry
 
         lax.fori_loop(0, length, body, 0)
+        if order[i] + pair_slots < sum(pair_first):
+            credit(pair_credit, at(a, 1 - b, c))
 
     def line_step(i, j):
         def going_up():
@@ -316,19 +415,18 @@
     def finish_late(i):
         if not pair_first[i]:
             across(i).wait_recv()
-            add(held.at[i, a, b], pair_in.at[i, 0])
+            add(held.at[i, a, b], pair_late.at[order[i]])
             result(i).start()
 
-    for i in range(n):
-        load(i).start()
-        if i < slots:
-            to_core(i).start()
+    raw_load(0).start()
+    right_load(0).start()
+    raw_load(1).start()
+    produce(0)
     for t in range(n + length + 3):
+        if t + 1 < n:
+            produce(t + 1)
         if t < n:
             first_add(t)
-            if t + slots < n:
-                pl.semaphore_wait(credit, 1)
-                to_core(t + slots).start()
         if 0 <= t - 1 < n:
             second_add(t - 1)
         for j in range(length):
@@ -339,51 +437,120 @@
         if 0 <= t - 2 - length < n:
             finish_late(t - 2 - length)
     for i in range(n):
-        to_core(i).wait_send()
+        if i >= n - slots:
+            to_core(i).wait_send()
         across(i).wait_send()
         result(i).wait()
         for bb in rows_of(i):
             for here in range(length):
 
-                def sent():
+                def gone():
                     for dest in range(here + 1, length):
                         up(i, here, dest, bb).wait_send()
                     for dest in range(0, here):
                         down(i, here, dest, bb).wait_send()
 
-                when(a == here, sent)
-
-
-def scatter_all(grads, plan, length):
-    count, n = len(grads), len(plan)
-    slots = 3
-    rows = grads[0].shape[3]
-    width = plan[0][2]
-    dtype = grads[0].dtype
-    flows = sum((length - 1) * (1 if p[3] == "pair" else 2) for p in plan)
+                when(a == here, gone)
+
+
+def scatter_all(lefts, rights, shard_shapes, plan, length):
+    n = len(plan)
+    slots, pair_slots = 2, 4
+    total_rows = lefts[0].shape[0]
+    rows, width = shard_shapes[0][0], plan[0][2]
+    late = sum(p[3] != "pair" for p in plan)
+    flows = (length - 1) * (n + late)
+    lead = shard_shapes[-1][0]
     dma = pltpu.SemaphoreType.DMA
-    anywhere = [pl.BlockSpec(memory_space=pl.ANY)] * count
+    anywhere = pl.BlockSpec(memory_space=pl.ANY)
     slab = (rows, width)
     return pl.pallas_call(
-        functools.partial(scatter_kernel, length, plan, count, slots),
-        out_shape=tuple(jax.ShapeDtypeStruct(g.shape[3:], dtype) for g in grads),
-        in_specs=anywhere,
-        out_specs=anywhere,
+        functools.partial(scatter_kernel, length, plan, slots, pair_slots),
+        out_shape=tuple(jax.ShapeDtypeStruct(s, BF16) for s in shard_shapes),
+        in_specs=[anywhere] * 8,
+        out_specs=[anywhere] * 4,
         scratch_shapes=[
-            pltpu.VMEM((n, length, 2) + slab, dtype),
-            pltpu.VMEM((slots, length, 2) + slab, dtype),
-            pltpu.VMEM((n, length) + slab, dtype),
-            pltpu.VMEM((flows,) + slab, dtype),
-            pltpu.VMEM((flows,) + slab, dtype),
-            dma((n,)), dma((n,)), dma((n,)), dma((n,)), dma((n,)),
+            pltpu.VMEM((2, total_rows, width), BF16),
+            pltpu.VMEM((2, total_rows, width), BF16),
+            pltpu.VMEM((2 * lead, 2 * length * rows, total_rows), BF16),
+            pltpu.VMEM((n, length, 2) + slab, BF16),
+            pltpu.VMEM((slots, length, 2) + slab, BF16),
+            pltpu.VMEM((slots, length, 2) + slab, BF16),
+            pltpu.VMEM((pair_slots, length) + slab, BF16),
+            pltpu.VMEM((late,) + slab, BF16),
+            pltpu.VMEM((flows,) + slab, BF16),
+            pltpu.VMEM((flows,) + slab, BF16),
+            dma((lead + 3,)), dma((n,)), dma((n,)), dma((n,)), dma((n,)), dma((n,)),
             dma((flows,)), dma((flows,)), dma((flows,)), dma((flows,)), dma((n,)),
-            pltpu.SemaphoreType.REGULAR,
+            pltpu.SemaphoreType.REGULAR, pltpu.SemaphoreType.REGULAR,
         ],
         compiler_params=pltpu.CompilerParams(
-            collective_id=1, has_side_effects=True, vmem_limit_bytes=60 * 1024 * 1024
+            collective_id=1, has_side_effects=True, vmem_limit_bytes=62 * 1024 * 1024
         ),
         name="scatter_grads",
-    )(*grads)
+    )(*lefts, *rights)
+
+
+def small_gather_kernel(length, sum_sections, own_ref, out_ref, other, *sems):
+    line_s, line_r, pair_s, pair_r, core_s, core_r, side_s, side_r = sems
+    a, b, c = position()
+    partner = {"section": 1 - lax.axis_index("section")}
+    barrier = pltpu.get_barrier_semaphore()
+
+    def tell(target):
+        pl.semaphore_signal(barrier, inc=1, device_id=target, device_id_type=MESH)
+
+    tell(at(a, 1 - b, c))
+    tell(at(a, b, 1 - c))
+    for k in range(1, length):
+        tell(at(lax.rem(a + k, length), b, c))
+    if sum_sections:
+        tell(partner)
+    pl.semaphore_wait(barrier, length + 1 + int(sum_sections))
+    value = own_ref[...]
+    if sum_sections:
+        side = remote(own_ref, other, side_s, side_r, partner)
+        side.start()
+        side.wait()
+        value = value + other[...]
+    out_ref[a, b, c] = value
+    mine = out_ref.at[a, b, c]
+    copies = []
+    for k in range(1, length):
+        to = lax.rem(a + k, length)
+        copy = remote(mine, mine, line_s.at[k - 1], line_r.at[k - 1], at(to, b, c))
+        copy.start()
+        copies.append(copy)
+    for k in range(1, length):
+        source = lax.rem(a + length - k, length)
+        slab = out_ref.at[source, b, c]
+        remote(slab, slab, line_s.at[k - 1], line_r.at[k - 1], at(a, 1 - b, c)).wait_recv()
+        copies[k - 1].wait_send()
+    for go, come, s, r, to in (
+        (out_ref.at[:, b, c], out_ref.at[:, 1 - b, c], pair_s, pair_r, at(a, 1 - b, c)),
+        (out_ref.at[:, :, c], out_ref.at[:, :, 1 - c], core_s, core_r, at(a, b, 1 - c)),
+    ):
+        copy = remote(go, go, s, r, to)
+        copy.start()
+        remote(come, come, s, r, to).wait_recv()
+        copy.wait_send()
+
+
+def small_gather(own, length, sum_sections, collective_id):
+    dma = pltpu.SemaphoreType.DMA
+    vmem = pl.BlockSpec(memory_space=pltpu.VMEM)
+    shape = (length, 2, 2) + own.shape
+    return pl.pallas_call(
+        functools.partial(small_gather_kernel, length, sum_sections),
+        out_shape=jax.ShapeDtypeStruct(shape, own.dtype),
+        in_specs=[vmem],
+        out_specs=vmem,
+        scratch_shapes=[
+            pltpu.VMEM(own.shape, own.dtype), dma((length - 1,)), dma((length - 1,)), dma, dma, dma, dma, dma, dma,
+        ],
+        compiler_params=pltpu.CompilerParams(collective_id=collective_id, has_side_effects=True),
+        name="small_gather",
+    )(own).reshape((4 * length,) + own.shape)
 
 
 def head_window(h):
@@ -528,23 +695,20 @@
     grad_gate2 = jnp.sum(grad_out * mlp, axis=1)
     _, pull = jax.vjp(lambda h: jax.nn.gelu(h, approximate=True), hidden)
     grad_hidden = pull(dot_back(grad_mlp, down_weight))[0].astype(BF16)
-    down_grad = dot_rows(active, grad_mlp).astype(BF16)
     grad_second = dot_back(grad_hidden, up_weight).reshape(shape)
-    up_grad = dot_rows(second_in, grad_hidden).astype(BF16)
     grad_middle, grad_shift2, grad_scale2 = norm_back(grad_second, middle, scale2)
     grad_middle = grad_middle + grad_out
     grad_gate1 = jnp.sum(grad_middle * branch, axis=1)
     grad_branch = flat((gate1 * grad_middle).astype(BF16))
     grad_attended = dot_back(grad_branch, proj_weight).astype(BF16)
-    proj_grad = dot_rows(attended, grad_branch).astype(BF16)
     grad_qkv = attention_call(attend_back_kernel, (qkv, grad_attended), segments, 3 * width, 5)
     grad_first = dot_back(grad_qkv, qkv_weight).reshape(shape)
-    qkv_grad = dot_rows(first_in, grad_qkv).astype(BF16)
     grad_x, grad_shift1, grad_scale1 = norm_back(grad_first, x, scale1)
     grad_modulation = jnp.concatenate(
         [grad_shift1, grad_scale1, grad_gate1, grad_shift2, grad_scale2, grad_gate2], axis=-1
     )
-    return grad_x + grad_middle, grad_modulation, (qkv_grad, proj_grad, up_grad, down_grad)
+    operands = ((first_in, attended, second_in, active), (grad_qkv, grad_branch, grad_hidden, grad_mlp))
+    return grad_x + grad_middle, grad_modulation, operands
 
 
 def plan_of(widths, lead, unit, other, last, names):
@@ -578,10 +742,14 @@
     quarters = micro * SMALL_PER
     ada = ada_weight[0]
 
-    ids = jnp.stack([timesteps, labels])
-    ids = lax.all_gather(ids, "dp", axis=0)
-    times = ids[:, 0].reshape(devices * images)
-    classes = ids[:, 1].reshape(devices * images)
+    length = devices // 4
+    ids = jnp.concatenate([timesteps.reshape(1, images), labels.reshape(1, images)])
+    if length == 4:
+        ids = small_gather(jnp.pad(ids, ((0, 6), (0, 128 - images))), length, False, 2)
+    else:
+        ids = lax.all_gather(ids, "dp", axis=0)
+    times = ids[:, 0, :images].reshape(devices * images)
+    classes = ids[:, 1, :images].reshape(devices * images)
     half = time_weight.shape[0] // 2
     frequencies = jnp.exp(-math.log(10000.0) * jnp.arange(half, dtype=F32) / half)
     angles = times.astype(F32)[:, None] * frequencies[None, :]
@@ -600,7 +768,6 @@
     shards = (qkv_weight[0], proj_weight[0], up_weight[0])
     lead = down_weight.shape[1] // qkv_weight.shape[1]
     down_shard = down_weight[0].reshape(lead, own_width, width)
-    length = devices // 4
     widths = [s.shape[1] for s in shards]
     if length == 4:
         plan = plan_of(widths, lead, width, 2, True, ("line", "pair"))
@@ -657,6 +824,7 @@
         grad = received.astype(F32).reshape(enc_rows)
         grad_x, grad_mod, grads = block_backward(x, enc_segments, modulation, weights, kept, grad)
         grad_x = grad_x.astype(BF16).reshape(micro, kept_count, width)
+        grads = jax.tree.map(lambda g: jnp.pad(g, ((0, micro * (slot - kept_count)), (0, 0))), grads)
         return to_slots(grad_x).astype(BF16), grad_mod, grads
 
     token_grad, grad_mod, grads = lax.cond(
@@ -682,25 +850,31 @@
     )
     grad_lifted = dot_back(every_mod, ada)
     _, pull = jax.vjp(jax.nn.silu, cond)
-    grad_cond = pull(grad_lifted)[0].astype(BF16)
-    every_cond = lax.all_gather(grad_cond.T, ("section", "dp"), axis=0)
-    every_cond = every_cond.reshape(2, width, devices * images)
+    grad_cond = pull(grad_lifted)[0]
+    mask_rows = mask_part.reshape(-1, devices * images) if length == 4 else None
+    if length == 4:
+        payload = jnp.concatenate([grad_cond.T, mask_rows])
+        extra = -payload.shape[0] % 8
+        payload = small_gather(jnp.pad(payload, ((0, extra), (0, 0))), length, True, 3)
+        every_cond = payload[:, :own_width].reshape(width, devices * images)
+        mask_grad = jnp.sum(payload[:, own_width : own_width + mask_rows.shape[0]], axis=0).reshape(width)
+    else:
+        every_cond = lax.psum(lax.all_gather(grad_cond.T, "dp", axis=0, tiled=True), "section")
+        mask_grad = lax.psum(mask_part, ("section", "dp"))
     inputs = jnp.concatenate([embedding, onehot], axis=1)
     shared = lax.dot_general(
-        jnp.concatenate([inputs, inputs], axis=0),
-        jnp.concatenate([every_cond[0], every_cond[1]], axis=1),
-        (((0,), (1,)), ((), ())),
-        preferred_element_type=F32,
+        inputs, every_cond.astype(BF16), (((0,), (1,)), ((), ())), preferred_element_type=F32
     )
     time_grad, table_grad = shared[: time_weight.shape[0]], shared[time_weight.shape[0] :]
-    mask_grad = lax.psum(mask_part, ("section", "dp"))
-
-    split = tuple(g.reshape((devices,) + s.shape) for g, s in zip(grads, shards + (down_shard,)))
+
+    shapes = tuple(x.shape for x in shards + (down_shard,))
+    lefts, rights = grads
     if length == 4:
-        plan = plan_of(widths, lead, width, 2, False, ("pair", "line"))
-        split = tuple(g.reshape((length, 2, 2) + g.shape[1:]) for g in split)
-        mine = scatter_all(split, plan, length)
+        names = ("pair", "line")
+        plan = plan_of(widths, lead, width, 2, False, names)
+        mine = scatter_all(lefts, rights, shapes, plan, length)
     else:
+        split = (dot_rows(x, y).astype(BF16).reshape((devices,) + s) for x, y, s in zip(lefts, rights, shapes))
         mine = tuple(lax.psum_scatter(g, "dp", scatter_dimension=0) for g in split)
     qkv_grad, proj_grad, up_grad, down_grad = (g.astype(F32) for g in mine)
     return (

time: 922 us -> 781 us (0.85)
  blocking collectives: 108 us -> 0 us
  Pallas kernels: 390 us -> 426 us
  starting transfers between devices: 164 us -> 136 us
  local copies, waits for them, and re-layouts: 81.5 us -> 54.1 us
  matrix products: 86.9 us -> 60.4 us
  waiting for transfers between devices: 16 us -> 27.3 us
    all_gather x2 -> x0, blocking collectives: 64 us -> none  [the longest x1 40.7 us: on_device(): every_cond = lax.all_gather(grad_cond.T, ('section', 'dp'), axis=0)]
    cond x61, local copies, waits for them, and re-layouts: 48.7 us -> 3.2 us  [the longest x4 45.4 us: on_device(): lax.cond(section == 0, encode_back, lambda: (jnp.zeros_like(decoded), gra...]
    psum x1 -> x0, blocking collectives: 43.8 us -> none  [on_device(): mask_grad = lax.psum(mask_part, ('section', 'dp'))]
    pallas_call x1 -> x3, Pallas kernels: 201 us -> 236 us  [the longest x1 202 us: scatter_all(): pl.pallas_call(functools.partial(scatter_kernel, length, plan, slots, pai...]
    ppermute x3, starting transfers between devices: 164 us -> 136 us  [swap_sections(): return lax.ppermute(x, 'section', [(0, 1), (1, 0)])]
    dot_general x5 -> x1, matrix products: 28.1 us -> 1.7 us  [dot_rows(): lax.dot_general(x, y, (((0,), (0,)), ((), ())), preferred_element_type=F32)]
    pad x0 -> x9, local copies, waits for them, and re-layouts: none -> 18.1 us  [the longest x8 17.5 us: encode_back(): jnp.pad(g, ((0, micro * (slot - kept_count)), (0, 0)))]
    ppermute x3, waiting for transfers between devices: 15.9 us -> 27.3 us  [swap_sections(): return lax.ppermute(x, 'section', [(0, 1), (1, 0)])]
  transfers between devices with their start and end apart: 5 -> 5, of which waited for: 1 -> 2; matrix products, arithmetic and copies ran while one was open for 1% -> 2% of each run, Pallas kernels for 41% -> 49%
where the time goes in v2:
time: 781 us; the launch traced here: 772 us
  Pallas kernels  426 us (55%)
  starting transfers between devices  136 us (17%)
  matrix products  60.4 us (8%)
  local copies, waits for them, and re-layouts  54.1 us (7%)
  other arithmetic  49.6 us (6%)
  waiting for transfers between devices  27.3 us (3%)
  between operations  15 us (2%)
    pallas_call x1, Pallas kernels, scatter_all(): pl.pallas_call(functools.partial(scatter_kernel, length, plan, slots, pai...  202 us
    pallas_call x1, Pallas kernels, gather_all(): pl.pallas_call(functools.partial(gather_kernel, length, plan, count), out...  174 us
    ppermute x3, starting transfers between devices, swap_sections(): return lax.ppermute(x, 'section', [(0, 1), (1, 0)])  136 us
    pallas_call x2, Pallas kernels, small_gather(): pl.pallas_call(functools.partial(small_gather_kernel, length, sum_section...  33.8 us
    dot_general x7, matrix products, dot(): return jnp.dot(x, y, preferred_element_type=F32)  32 us
    ppermute x3, waiting for transfers between devices, swap_sections(): return lax.ppermute(x, 'section', [(0, 1), (1, 0)])  27.3 us
    dot_general x5, matrix products, dot_back(): lax.dot_general(x, y, (((1,), (1,)), ((), ())), preferred_element_type=F32)  22.4 us
    pad x8, local copies, waits for them, and re-layouts, encode_back(): jnp.pad(g, ((0, micro * (slot - kept_count)), (0, 0)))  17.5 us
  transfers between devices with their start and end apart: 5, of which 2 were waited for; matrix products, arithmetic and copies ran while one was open for 2% of the time, Pallas kernels for 49%

profile of v2, /device:TPU:0, one launch (start us, length us, event | category | flops | bytes accessed | tf_op | source)
XLA Modules:
  0.0 772.5 jit_solution(13525027697780716719)
XLA Ops:
  9.5 12.7 %small_gather.2 = s32[4,2,2,8,128]{4,3,2,1,0:T(8,128)} custom-call(s32[8,128]{1,0:T(8,128)} %pad.43.own_ref), custom_call_target="tpu_custom_call" | custom-call | tf_op jit(solution)/shard_map/small_gather/pallas_call | solution.py:543
  24.4 2.7 fusion.76
  28.7 1.9 fusion.71
  31.2 174.2 %gather_weights.1 = (bf16[4,2,2,72,3456]{4,3,2,1,0:T(8,128)(2,1)}, bf16[4,2,2,72,1152]{4,3,2,1,0:T(8,128)(2,1)}, bf16[4,2,2,72,4608]{4,3,2,1,0:T(8,128)(2,1)}, bf16[4,2,2,4,72,1152]{5,4,3,2,1,0:T(8,128)(2,1)}) custom-call(bf16[72,3456]{1,0:T(8,128)(2,1)} %bitcast.361, bf16[72,1152]{1,0:T(8,128)(2,1)} %bitcast.363, bf16[72,4608]{1,0:T(8,128)(2,1)} %bitcast.358, ...), custom_call_target="tpu_custom_call" | custom-call | tf_op jit(solution)/shard_map/gather_weights/pallas_call | solution.py:189
  208.3 50.3 %conditional.3 = (bf16[8,32,1152]{2,1,0:T(8,128)(2,1)}, f32[8,32,1152]{2,1,0:T(8,128)}, bf16[256,1152]{1,0:T(8,128)(2,1)}, bf16[256,3456]{1,0:T(8,128)(2,1)}, bf...) conditional(s32[]{:T(128)} %convert_element_type.179, () %tuple.49, ...), branch_computations={%region_1.2_spmd, %region_2.7_spmd} | conditional | flops 9398536192 | bytes 114876640 | solution.py:804
  208.8 2.7 fusion.103
  211.5 1.5 multiply_reduce_fusion.1
  213.6 2.4 fusion.13
  216.0 7.2 convolution_convert_fusion.qkv_ref
  223.4 5.0 branch_1_fun.7
  228.4 3.1 fusion.109
  231.6 1.9 fusion.15
  233.6 2.0 multiply_reduce_fusion
  235.6 3.0 fusion.8
  238.5 10.9 %fusion.7 = (bf16[256,4608]{1,0:T(8,128)(2,1)}, f32[256,4608]{1,0:T(8,128)}) fusion(bf16[256,1152]{1,0:T(8,128)(2,1)} %fusion.8, bf16[1152,4608]{1,0:T(8,128)(2,1)} %get-tuple-element.187), kind=kOutput, calls=%fused_computation.9 | convolution fusion | flops 2728525824 | bytes 18284544 | tf_op jit(solution)/shard_map/cond/branch_1_fun/dot_general | solution.py:639
  249.5 5.9 fusion.110
  255.4 3.1 add_convert_fusion
  258.7 16.0 %collective-permute-done = bf16[8,32,1152]{2,1,0:T(8,128)(2,1)} collective-permute-done((bf16[8,32,1152]{2,1,0:T(8,128)(2,1)}, bf16[8,32,1152]{2,1,0:T(8,128)(2,1)}, u32[]{:S(2)}, u32[]{:S(2)}) %collective-permute-start) | collective-permute-done | bytes 589856 | tf_op jit(solution)/shard_map/ppermute | solution.py:728
  274.7 19.0 %conditional.4 = (bf16[2,128,1152]{1,2,0:T(8,128)(2,1)}, f32[8,6912]{1,0:T(8,128)}, bf16[512,1152]{1,0:T(8,128)(2,1)}, bf16[512,1152]{1,0:T(8,128)(2,1)}, bf16[5...) conditional(s32[]{:T(128)} %convert_element_type.180, () %tuple.48, ...), branch_computations={%region_7.8_spmd, %region_8.25_spmd} | conditional | flops 40542011392 | bytes 414672032 | solution.py:819
  274.7 2.4 broadcast.495
  277.1 2.6 broadcast.495.clone
  279.7 2.0 broadcast.496
  281.7 1.1 broadcast.494
  282.9 1.1 broadcast.494.clone
  284.0 1.1 broadcast.494.clone.1
  285.1 1.1 broadcast.494.clone.2
  286.2 1.1 broadcast.494.clone.3
  293.7 1.4 copy.46
  295.1 135.6 %collective-permute-start.1 = (bf16[2,128,1152]{2,1,0:T(8,128)(2,1)S(1)}, bf16[2,128,1152]{2,1,0:T(8,128)(2,1)S(1)}, u32[]{:S(2)}, u32[]{:S(2)}) collective-permute-start(bf16[2,128,1152]{2,1,0:T(8,128)(2,1)S(1)} %copy.46), channel_id=1, source_target_pairs={{0,16},{16,0},{1,17},{17,1},{2,18},{18,2},{3,19},{19,3},{4,20},{20... | collective-permute-start | bytes 1769480 | tf_op jit(solution)/shard_map/ppermute | solution.py:728
  431.3 1.4 fusion.75
  432.6 11.3 %collective-permute-done.1 = bf16[2,128,1152]{2,1,0:T(8,128)(2,1)S(1)} collective-permute-done((bf16[2,128,1152]{2,1,0:T(8,128)(2,1)S(1)}, bf16[2,128,1152]{2,1,0:T(8,128)(2,1)S(1)}, u32[]{:S(2)}, u32[]{:S(2)}) %collective-permute-start.1) | collective-permute-done | bytes 589856 | tf_op jit(solution)/shard_map/ppermute | solution.py:728
  444.0 71.7 %conditional.5 = (f32[8,6912]{1,0:T(8,128)}, bf16[512,1152]{1,0:T(8,128)(2,1)}, bf16[512,1152]{1,0:T(8,128)(2,1)}, bf16[512,1152]{1,0:T(8,128)(2,1)}, bf16[512,4...) conditional(s32[]{:T(128)} %convert_element_type.179, ...), branch_computations={%region_25.26_spmd, %region_26.41_spmd} | conditional | flops 11029737472 | bytes 217606944 | solution.py:830
  444.0 1.6 slice_add_fusion.4
  445.7 8.7 %fusion.62 = bf16[256,4608]{1,0:T(8,128)(2,1)S(1)} fusion(f32[256,4608]{1,0:T(8,128)} %get-tuple-element.213, bf16[256,1152]{1,0:T(8,128)(2,1)S(1)} %fusion.67, bf16[4608,1152]{1,0:T(8,128)(2,1)} %get-tuple-element.212), kind=kOutput, calls=%fused_computation.133 | convolution fusion | flops 2741501952 | bytes 18284544 | tf_op jit(solution)/shard_map/cond/branch_1_fun/dot_general | solution.py:643
  454.5 3.9 fusion.66
  458.8 3.8 fusion.68
  464.0 3.0 multiply_reduce_fusion.11
  468.4 10.7 %branch_1_fun.10 = bf16[256,3456]{1,0:T(8,128)(2,1)S(1)} custom-call(bf16[256,3456]{1,0:T(8,128)(2,1)} %get-tuple-element.208.qkv_ref, bf16[256,1152]{1,0:T(8,128)(2,1)S(1)} %convolution_convert_fusion.5.grad_ref, s32[256,1]{1,0:T(8,128)S(1)} %reshape_reshape.19.row_ref, s32[1,1,256]{2,1,0:T(1,128)S(1)} %reshape_reshape.17.column_ref), custom_call_target="tpu_custom_call" | custom-call | flops 2684354560 | bytes 4128768 | tf_op jit(solution)/shard_map/cond/branch_1_fun/pallas_call | solution.py:621
  479.1 6.5 bitcast_multiply_fusion.18
  485.9 1.4 reduce_sum.357
  487.3 1.6 multiply_reduce_fusion.12
  488.9 1.9 multiply_reduce_fusion.9
  490.8 1.7 add_convert_fusion.1
  497.9 2.0 pad.37
  500.0 1.1 pad.38
  501.1 2.5 pad.39
  503.7 1.1 pad.40
  504.8 4.1 pad.36
  508.9 2.2 pad.33
  511.1 2.2 pad.34
  513.3 2.2 pad.35
  516.8 1.7 select_convert_fusion
  518.5 2.0 broadcast_select_fusion.2
  520.5 202.4 %scatter_grads.1 = (bf16[72,3456]{1,0:T(8,128)(2,1)}, bf16[72,1152]{1,0:T(8,128)(2,1)}, bf16[72,4608]{1,0:T(8,128)(2,1)}, bf16[4,72,1152]{2,1,0:T(8,128)(2,1)}) custom-call(bf16[512,1152]{1,0:T(8,128)(2,1)} %get-tuple-element.311.refs_0_, bf16[512,1152]{1,0:T(8,128)(2,1)} %get-tuple-element.312.refs_1_, bf16[512,1152]{1,0:T(8,128)(2,1)} %get-tuple-element.313.refs_2_, ...), custom_call_target="tpu_custom_call" | custom-call | tf_op jit(solution)/shard_map/scatter_grads/pallas_call | solution.py:467
  722.9 2.1 bitcast_convert_fusion.2
  725.0 2.3 bitcast_convert_fusion.1
  728.0 1.1 bitcast_convert_fusion
  729.2 2.2 broadcast_select_fusion
  731.4 2.3 fusion.93
  734.3 21.1 %small_gather.3 = f32[4,2,2,88,128]{4,3,2,1,0:T(8,128)} custom-call(f32[88,128]{1,0:T(8,128)} %select_maximum_fusion.own_ref), custom_call_target="tpu_custom_call" | custom-call | tf_op jit(solution)/shard_map/small_gather/pallas_call | solution.py:543
  755.4 1.1 slice.81
  757.6 2.4 slice.76
  761.2 1.5 slice_reduce_fusion
  762.7 1.7 convolution_bitcast_fusion
  (197 shorter events, 28.6 us)
Async XLA Ops:
  7.2 21.5 %copy-start = (bf16[1,72,6912]{2,1,0:T(8,128)(2,1)S(1)}, bf16[1,72,6912]{2,1,0:T(8,128)(2,1)}, u32[]{:S(2)}) copy-start(bf16[1,72,6912]{2,1,0:T(8,128)(2,1)} %param.30) | copy-start | bytes 2985988
  7.2 20.0 %copy-start.38 = (bf16[256,1152]{1,0:T(8,128)(2,1)S(1)}, bf16[256,1152]{1,0:T(8,128)(2,1)}, u32[]{:S(2)}) copy-start(bf16[256,1152]{1,0:T(8,128)(2,1)} %param.28) | copy-start | bytes 1769476
  7.2 198.3 %reduce-scatter.2.cloned.1.call-start = ((), (), s32[]{:S(2)}) async-start(), calls=%async_computation.1 | async-start | bytes 1880064 | tf_op jit(solution)/shard_map/reduce_scatter | solution.py:766
  23.4 7.2 copy-start.72
  24.4 6.2 copy-start.44
  24.4 6.1 copy-start.46
  27.2 3.4 copy-start.36
  27.5 0.8 copy-start.35
  28.4 2.3 copy-start.80
  28.4 177.0 %copy-start.48 = (bf16[128,72]{0,1:T(8,128)(2,1)}, bf16[128,72]{0,1:T(8,128)(2,1)S(1)}, u32[]{:S(2)}) copy-start(bf16[128,72]{0,1:T(8,128)(2,1)S(1)} %multiply_convert_fusion.2) | copy-start | bytes 55300
  30.6 174.9 %copy-start.75 = (s32[2,128]{1,0:T(2,128)S(1)}, s32[2,128]{1,0:T(2,128)}, u32[]{:S(2)}) copy-start(s32[2,128]{1,0:T(2,128)} %param.22) | copy-start | bytes 3076
  30.6 700.8 %all-gather.2.cloned.1.call-start = ((), (), s32[]{:S(2)}) async-start(), calls=%async_computation.2 | async-start | bytes 1880064 | tf_op jit(solution)/shard_map/all_gather | solution.py:846
  30.9 176.9 %copy-start.68 = (pred[8]{0:T(512)(128)(4,1)}, pred[8]{0:T(512)(128)(4,1)S(1)}, u32[]{:S(2)}) copy-start(pred[8]{0:T(512)(128)(4,1)S(1)} %broadcast_in_dim.175) | copy-start | bytes 28
  31.2 176.5 %copy-start.70 = (s32[8]{0:T(128)}, s32[8]{0:T(128)S(1)}, u32[]{:S(2)}) copy-start(s32[8]{0:T(128)S(1)} %select_n.47) | copy-start | bytes 100
  207.6 0.7 copy-start.25
  207.7 67.0 %copy-start.17 = (bf16[2,256,1152]{2,1,0:T(8,128)(2,1)S(1)}, bf16[2,256,1152]{2,1,0:T(8,128)(2,1)}, u32[]{:S(2)}) copy-start(bf16[2,256,1152]{2,1,0:T(8,128)(2,1)} %param.26) | copy-start | bytes 3538948
  207.7 67.0 %copy-start.74 = (bf16[1152]{0:T(1024)(128)(2,1)S(1)}, bf16[1152]{0:T(1024)(128)(2,1)}, u32[]{:S(2)}) copy-start(bf16[1152]{0:T(1024)(128)(2,1)} %param.27) | copy-start | bytes 6916
  223.4 5.0 copy-start.76
  235.6 13.9 %slice-start.3 = ((s8[10616832]{0:T(1024)(128)(4,1)}), s8[4194304]{0:T(1024)(128)(4,1)S(1)}, s32[]{:S(2)}) async-start(s8[10616832]{0:T(1024)(128)(4,1)} %bitcast.345), calls=%async_computation.6 | async-start | bytes 8388608 | tf_op jit(solution)/shard_map/cond
  238.5 10.9 %slice-start.4 = ((s8[10616832]{0:T(1024)(128)(4,1)}), s8[4194304]{0:T(1024)(128)(4,1)S(1)}, s32[]{:S(2)}) async-start(s8[10616832]{0:T(1024)(128)(4,1)} %bitcast.345), calls=%async_computation.7 | async-start | bytes 8388608 | tf_op jit(solution)/shard_map/cond
  238.5 10.9 %slice-start.5 = ((s8[10616832]{0:T(1024)(128)(4,1)}), s8[2228224]{0:T(1024)(128)(4,1)S(1)}, s32[]{:S(2)}) async-start(s8[10616832]{0:T(1024)(128)(4,1)} %bitcast.345), calls=%async_computation.8 | async-start | bytes 4456448 | tf_op jit(solution)/shard_map/cond
  249.5 5.9 copy-start.52
  258.6 16.1 %copy-start.9 = (f32[8,32,1152]{2,1,0:T(8,128)}, f32[8,32,1152]{2,1,0:T(8,128)S(1)}, u32[]{:S(2)}) copy-start(f32[8,32,1152]{2,1,0:T(8,128)S(1)} %get-tuple-element.294) | copy-start | bytes 3538948
  258.6 16.0 %collective-permute-start = (bf16[8,32,1152]{2,1,0:T(8,128)(2,1)}, bf16[8,32,1152]{2,1,0:T(8,128)(2,1)}, u32[]{:S(2)}, u32[]{:S(2)}) collective-permute-start(bf16[8,32,1152]{2,1,0:T(8,128)(2,1)} %get-tuple-element.284), channel_id=1, source_target_pairs={{0,16},{16,0},{1,17},{17,1},{2,18},{18,2},{3,19},{19,3},{4,20},{20... | collective-permute-start | bytes 1769480 | tf_op jit(solution)/shard_map/ppermute | solution.py:728
  295.1 148.9 %collective-permute-start.1 = (bf16[2,128,1152]{2,1,0:T(8,128)(2,1)S(1)}, bf16[2,128,1152]{2,1,0:T(8,128)(2,1)S(1)}, u32[]{:S(2)}, u32[]{:S(2)}) collective-permute-start(bf16[2,128,1152]{2,1,0:T(8,128)(2,1)S(1)} %copy.46), channel_id=1, source_target_pairs={{0,16},{16,0},{1,17},{17,1},{2,18},{18,2},{3,19},{19,3},{4,20},{20... | collective-permute-start | bytes 1769480 | tf_op jit(solution)/shard_map/ppermute | solution.py:728
  443.9 72.9 %copy-start.69 = (pred[8]{0:T(512)(128)(4,1)S(1)}, pred[8]{0:T(512)(128)(4,1)}, u32[]{:S(2)}) copy-start(pred[8]{0:T(512)(128)(4,1)} %copy-done.68) | copy-start | bytes 28
  444.0 10.4 %copy-start.27 = (bf16[2,128,1152]{2,1,0:T(8,128)(2,1)}, bf16[2,128,1152]{2,1,0:T(8,128)(2,1)S(1)}, u32[]{:S(2)}) copy-start(bf16[2,128,1152]{2,1,0:T(8,128)(2,1)S(1)} %get-tuple-element.211) | copy-start | bytes 1769476 | tf_op jit(solution)/shard_map/cond
  445.5 8.9 %copy-start.41 = (f32[8,1152]{1,0:T(8,128)}, f32[8,1152]{1,0:T(8,128)S(1)}, u32[]{:S(2)}) copy-start(f32[8,1152]{1,0:T(8,128)S(1)} %get-tuple-element.418) | copy-start | bytes 110596 | tf_op jit(solution)/shard_map/cond
  445.6 8.7 %copy-start.30 = (bf16[256,1152]{1,0:T(8,128)(2,1)}, bf16[256,1152]{1,0:T(8,128)(2,1)S(1)}, u32[]{:S(2)}) copy-start(bf16[256,1152]{1,0:T(8,128)(2,1)S(1)} %fusion.67) | copy-start | bytes 1769476 | tf_op jit(solution)/shard_map/cond
  445.7 8.8 %slice-start = ((s8[10616832]{0:T(1024)(128)(4,1)}), s8[4194304]{0:T(1024)(128)(4,1)S(1)}, s32[]{:S(2)}) async-start(s8[10616832]{0:T(1024)(128)(4,1)} %bitcast.340), calls=%async_computation.3 | async-start | bytes 8388608 | tf_op jit(solution)/shard_map/cond
  445.7 8.8 %slice-start.1 = ((s8[10616832]{0:T(1024)(128)(4,1)}), s8[4194304]{0:T(1024)(128)(4,1)S(1)}, s32[]{:S(2)}) async-start(s8[10616832]{0:T(1024)(128)(4,1)} %bitcast.340), calls=%async_computation.4 | async-start | bytes 8388608 | tf_op jit(solution)/shard_map/cond
  445.7 8.8 %slice-start.2 = ((s8[10616832]{0:T(1024)(128)(4,1)}), s8[2228224]{0:T(1024)(128)(4,1)S(1)}, s32[]{:S(2)}) async-start(s8[10616832]{0:T(1024)(128)(4,1)} %bitcast.340), calls=%async_computation.5 | async-start | bytes 4456448 | tf_op jit(solution)/shard_map/cond
  454.4 4.0 copy-start.21
  454.5 3.9 copy-start.10
  458.8 3.9 copy-start.73
  464.0 3.0 copy-start.51
  464.0 3.1 copy-start.79
  467.0 1.2 copy-start.19
  467.1 1.1 copy-start.28
  479.1 6.5 copy-start.1
  487.3 3.5 copy-start.20
  492.6 2.9 copy-start.56
  492.6 3.5 copy-start.55
  492.6 4.1 copy-start.54
  492.6 4.7 copy-start.53
  492.6 5.3 copy-start.2
  497.9 2.0 copy-start.29
  497.9 3.2 copy-start.22
  501.1 2.6 copy-start.31
  520.5 208.7 %collective-permute-start.2 = (bf16[2,256,576]{1,2,0:T(8,128)(2,1)}, bf16[2,256,576]{1,2,0:T(8,128)(2,1)S(1)}, u32[]{:S(2)}, u32[]{:S(2)}) collective-permute-start(bf16[2,256,576]{1,2,0:T(8,128)(2,1)} %broadcast_select_fusion.2), channel_id=1, source_target_pairs={{0,16},{16,0},{1,17},{17,1},{2,18},{18,2},{3,19},{19,3},{4,20},{20... | collective-permute-start | bytes 1769480 | tf_op jit(solution)/shard_map/ppermute | solution.py:728
  722.9 4.4 copy-start.50
  722.9 5.1 copy-start.37
  731.4 25.2 %copy-start.32 = (bf16[128,1000]{1,0:T(8,128)(2,1)S(1)}, bf16[128,1000]{1,0:T(8,128)(2,1)}, u32[]{:S(2)}) copy-start(bf16[128,1000]{1,0:T(8,128)(2,1)} %fusion.75) | copy-start | bytes 768004
  731.4 25.2 %copy-start.45 = (bf16[128,128]{1,0:T(8,128)(2,1)S(1)}, bf16[128,128]{1,0:T(8,128)(2,1)}, u32[]{:S(2)}) copy-start(bf16[128,128]{1,0:T(8,128)(2,1)} %copy-done.44) | copy-start | bytes 98308
  731.4 25.2 %copy-start.47 = (bf16[128,128]{1,0:T(8,128)(2,1)S(1)}, bf16[128,128]{1,0:T(8,128)(2,1)}, u32[]{:S(2)}) copy-start(bf16[128,128]{1,0:T(8,128)(2,1)} %copy-done.46) | copy-start | bytes 98308
  760.1 2.6 copy-start.23
  760.1 2.6 copy-start.49
Sparse Core Ops, SparseCore 0:
  30.7 68.0 reduce-scatter.1
  518.6 43.7 all-gather.1

commit v3 on v2

--- a/solution.py
+++ b/solution.py
@@ -65,12 +65,9 @@
     return ref.at[lead + (slice(None), pl.ds(low, size))]
 
 
-def gather_kernel(length, plan, count, *refs):
-    sources = refs[:count]
-    outs = refs[count : 2 * count]
-    up_s, up_r, down_s, down_r, pair_s, pair_r, core_s, core_r, own_sem = refs[2 * count :]
-    a, b, c = position()
-    has_up, has_down = greet(length, a, b, c)
+def gather_moves(length, plan, sources, outs, sems, a, b, c):
+    up_s, up_r, down_s, down_r, pair_s, pair_r, core_s, core_r, own_sem = sems
+    has_up, has_down = a < length - 1, a > 0
     chunks = range(len(plan))
     line_first = [plan[i][3] == "line" for i in chunks]
 
@@ -119,55 +116,58 @@
         across_arrival(i, aa).wait_recv()
         to_core(i, aa, 1 - b).start()
 
-    for i in chunks:
+    def issue(i):
         src = own(i)
         pltpu.make_async_copy(src, slot(i, a, b, c), own_sem.at[i]).start()
         across(i, a, src).start()
         when(has_up, lambda: up(i, 0, b, src).start())
         when(has_down, lambda: down(i, 0, b, src).start())
         to_core(i, a, b, src).start()
-    for i in chunks:
+
+    def pair_step(i):
+        across_arrival(i, a).wait_recv()
+        when(has_up, lambda: up(i, 0, 1 - b).start())
+        when(has_down, lambda: down(i, 0, 1 - b).start())
+        to_core(i, a, 1 - b).start()
+
+    def line_step(i, k):
+        for bb in rows_of(i):
+
+            def from_below():
+                up_arrival(i, k - 1, bb).wait_recv()
+                when(has_up, lambda: up(i, k, bb).start())
+                if line_first[i]:
+                    across(i, a - k).start()
+                to_core(i, a - k, bb).start()
+
+            def from_above():
+                down_arrival(i, k - 1, bb).wait_recv()
+                when(has_down, lambda: down(i, k, bb).start())
+                if line_first[i]:
+                    across(i, a + k).start()
+                to_core(i, a + k, bb).start()
+
+            when(a - k >= 0, from_below)
+            when(a + k <= length - 1, from_above)
+
+    def across_step(i, k):
         if not line_first[i]:
-            across_arrival(i, a).wait_recv()
-            when(has_up, lambda: up(i, 0, 1 - b).start())
-            when(has_down, lambda: down(i, 0, 1 - b).start())
-            to_core(i, a, 1 - b).start()
-    for k in range(1, length):
-        for i in chunks:
-            for bb in rows_of(i):
-
-                def from_below():
-                    up_arrival(i, k - 1, bb).wait_recv()
-                    when(has_up, lambda: up(i, k, bb).start())
-                    if line_first[i]:
-                        across(i, a - k).start()
-                    to_core(i, a - k, bb).start()
-
-                def from_above():
-                    down_arrival(i, k - 1, bb).wait_recv()
-                    when(has_down, lambda: down(i, k, bb).start())
-                    if line_first[i]:
-                        across(i, a + k).start()
-                    to_core(i, a + k, bb).start()
-
-                when(a - k >= 0, from_below)
-                when(a + k <= length - 1, from_above)
-            if line_first[i]:
-                if k == 1:
-                    after_across(i, a)
-                else:
-                    when(a - k + 1 >= 0, lambda: after_across(i, a - k + 1))
-                    when(a + k - 1 <= length - 1, lambda: after_across(i, a + k - 1))
-    for i in chunks:
-        if line_first[i]:
-            k = length - 1
+            return
+        if k == 0:
+            after_across(i, a)
+        else:
             when(a - k >= 0, lambda: after_across(i, a - k))
             when(a + k <= length - 1, lambda: after_across(i, a + k))
-    for i in chunks:
+
+    def complete(i):
         pltpu.make_async_copy(own(i), slot(i, a, b, c), own_sem.at[i]).wait()
         for aa in range(length):
             for bb in range(2):
                 core_arrival(i, aa, bb).wait_recv()
+
+    def drain(i):
+        for aa in range(length):
+            for bb in range(2):
                 to_core(i, aa, bb).wait_send()
             if line_first[i]:
                 across(i, aa).wait_send()
@@ -181,23 +181,22 @@
                     lambda: down(i, k, bb).wait_send(),
                 )
 
-
-def gather_all(shards, plan, length):
-    count, n = len(shards), len(plan)
-    dma = pltpu.SemaphoreType.DMA
-    anywhere = [pl.BlockSpec(memory_space=pl.ANY)] * count
-    return pl.pallas_call(
-        functools.partial(gather_kernel, length, plan, count),
-        out_shape=tuple(jax.ShapeDtypeStruct((length, 2, 2) + s.shape, s.dtype) for s in shards),
-        in_specs=anywhere,
-        out_specs=anywhere,
-        scratch_shapes=[dma((n, length, 2))] * 4
-        + [dma((n, length))] * 2
-        + [dma((n, length, 2))] * 2
-        + [dma((n,))],
-        compiler_params=pltpu.CompilerParams(collective_id=0, has_side_effects=True),
-        name="gather_weights",
-    )(*shards)
+    def move(t, ahead):
+        n = len(plan)
+        if t + ahead < n:
+            issue(t + ahead)
+        if t < n and not line_first[t]:
+            pair_step(t)
+        for k in range(1, length):
+            i = t - k + 1
+            if 0 <= i < n:
+                line_step(i, k)
+        for k in range(length):
+            i = t - k
+            if 0 <= i < n:
+                across_step(i, k)
+
+    return issue, move, complete, drain
 
 
 def scatter_kernel(length, plan, slots, pair_slots, *refs):
@@ -215,6 +214,8 @@
     n = len(plan)
     rows, width = held.shape[3:]
     total_rows = raw.shape[1]
+    encoder = lax.axis_index("section") == 0
+    used_rows = jnp.where(encoder, total_rows // 2, total_rows)
     pair_first = [p[3] == "pair" for p in plan]
     order = [sum(pair_first[:i]) if pair_first[i] else i - sum(pair_first[:i]) for i in range(n)]
     base, total = [], 0
@@ -273,7 +274,7 @@
                             ] = part.astype(BF16)
                 return carry
 
-            lax.fori_loop(0, total_rows // 128, body, 0)
+            lax.fori_loop(0, used_rows // 128, body, 0)
             if x + 2 < len(raw_jobs):
                 raw_load(x + 2).start()
 
@@ -286,9 +287,14 @@
 
         def body(k, carry):
             columns = pl.ds(pl.multiple_of(k * tile, 128), tile)
-            result = jnp.dot(left_t[row_set], right[slot, :, columns], preferred_element_type=F32)
-            for s in range(groups):
-                put(s, columns, result[s * rows : (s + 1) * rows].astype(BF16))
+
+            def multiply(depth):
+                result = dot(left_t[row_set, :, :depth], right[slot, :depth, columns])
+                for s in range(groups):
+                    put(s, columns, result[s * rows : (s + 1) * rows].astype(BF16))
+
+            when(encoder, lambda: multiply(total_rows // 2))
+            when(jnp.logical_not(encoder), lambda: multiply(total_rows))
             return carry
 
         lax.fori_loop(0, 3, body, 0)
@@ -423,10 +429,10 @@
     raw_load(1).start()
     produce(0)
     for t in range(n + length + 3):
+        if t < n:
+            first_add(t)
         if t + 1 < n:
             produce(t + 1)
-        if t < n:
-            first_add(t)
         if 0 <= t - 1 < n:
             second_add(t - 1)
         for j in range(length):
@@ -563,12 +569,12 @@
     return lax.dot_general(x, y, ((dims[0], dims[1]), ((), ())), preferred_element_type=F32)
 
 
-def head_operands(qkv_ref, h):
+def head_operands(qkv_ref, rows, h):
     width = qkv_ref.shape[1] // 3
     low, high, start, stop = head_window(h)
     lane = lax.broadcasted_iota(jnp.int32, (1, stop - start), 1) + start
     inside = jnp.logical_and(lane >= low, lane < high)
-    parts = [qkv_ref[:, j * width + start : j * width + stop] for j in range(3)]
+    parts = [qkv_ref[rows, j * width + start : j * width + stop] for j in range(3)]
     return inside, slice(start, stop), parts
 
 
@@ -582,25 +588,24 @@
     return weights * (1.0 / jnp.sum(weights, axis=-1, keepdims=True))
 
 
-def attend_kernel(qkv_ref, row_ref, column_ref, out_ref, total):
-    allowed = row_ref[...] == column_ref[0]
-    total[...] = jnp.zeros_like(total)
+def attend(qkv_ref, rows, allowed, total, out_ref):
+    width = out_ref.shape[1]
+    total[:, :width] = jnp.zeros((total.shape[0], width), F32)
     for h in range(HEADS):
-        inside, window, (query, key, value) = head_operands(qkv_ref, h)
+        inside, window, (query, key, value) = head_operands(qkv_ref, rows, h)
         probs = softmax_of(only(inside, query), key, allowed).astype(BF16)
         mixed = contract(probs, value, ((1,), (0,)))
         total[:, window] += only(inside, mixed)
-    out_ref[...] = total[...].astype(BF16)
-
-
-def attend_back_kernel(qkv_ref, grad_ref, row_ref, column_ref, out_ref, total):
-    allowed = row_ref[...] == column_ref[0]
+    out_ref[rows, :] = total[:, :width].astype(BF16)
+
+
+def attend_back(qkv_ref, grad_ref, rows, allowed, total, out_ref):
     width = grad_ref.shape[1]
     total[...] = jnp.zeros_like(total)
     for h in range(HEADS):
-        inside, window, (query, key, value) = head_operands(qkv_ref, h)
+        inside, window, (query, key, value) = head_operands(qkv_ref, rows, h)
         query, key = only(inside, query), only(inside, key)
-        grad = only(inside, grad_ref[:, window])
+        grad = only(inside, grad_ref[rows, window])
         probs = softmax_of(query, key, allowed)
         grad_probs = contract(grad, value, ((1,), (1,)))
         centre = jnp.sum(probs * grad_probs, axis=-1, keepdims=True)
@@ -609,30 +614,7 @@
         total[:, start:stop] += contract(grad_scores, key, ((1,), (0,))) * HD**-0.5
         total[:, width + start : width + stop] += contract(grad_scores, query, ((0,), (0,))) * HD**-0.5
         total[:, 2 * width + start : 2 * width + stop] += contract(probs.astype(BF16), grad, ((0,), (0,)))
-    out_ref[...] = total[...].astype(BF16)
-
-
-def attention_call(kernel, operands, segments, out_width, matmuls):
-    rows = operands[0].shape[0]
-    blocks = rows // ATT_ROWS
-    row_ids = segments.reshape(rows, 1)
-    column_ids = segments.reshape(blocks, 1, ATT_ROWS)
-    wide = lambda n: pl.BlockSpec((ATT_ROWS, n), lambda i: (i, 0))
-    return pl.pallas_call(
-        kernel,
-        grid=(blocks,),
-        out_shape=jax.ShapeDtypeStruct((rows, out_width), BF16),
-        in_specs=[wide(x.shape[1]) for x in operands]
-        + [wide(1), pl.BlockSpec((1, 1, ATT_ROWS), lambda i: (i, 0, 0))],
-        out_specs=wide(out_width),
-        scratch_shapes=[pltpu.VMEM((ATT_ROWS, out_width), F32)],
-        compiler_params=pltpu.CompilerParams(vmem_limit_bytes=32 * 1024 * 1024),
-        cost_estimate=pl.CostEstimate(
-            flops=matmuls * blocks * HEADS * 2 * ATT_ROWS**3,
-            bytes_accessed=2 * rows * (out_width + sum(x.shape[1] for x in operands)),
-            transcendentals=blocks * HEADS * ATT_ROWS**2,
-        ),
-    )(*operands, row_ids, column_ids)
+    out_ref[rows, :] = total[...].astype(BF16)
 
 
 def dot(x, y):
@@ -645,10 +627,6 @@
 
 def dot_rows(x, y):
     return lax.dot_general(x, y, (((0,), (0,)), ((), ())), preferred_element_type=F32)
-
-
-def flat(x):
-    return x.reshape(-1, x.shape[-1])
 
 
 def normal(x):
@@ -657,71 +635,789 @@
     return centred * scale, scale
 
 
-def pieces_of(modulation):
-    return [p[:, None, :] for p in jnp.split(modulation, 6, axis=-1)]
-
-
-def block_forward(x, segments, modulation, weights):
-    qkv_weight, proj_weight, up_weight, down_weight = weights
-    shape, width = x.shape, x.shape[-1]
-    shift1, scale1, gate1, shift2, scale2, gate2 = pieces_of(modulation)
-    first_in = flat((normal(x)[0] * (1.0 + scale1) + shift1).astype(BF16))
-    qkv = dot(first_in, qkv_weight).astype(BF16)
-    attended = attention_call(attend_kernel, (qkv,), segments, width, 2)
-    branch = dot(attended, proj_weight).reshape(shape)
-    middle = x + gate1 * branch
-    second_in = flat((normal(middle)[0] * (1.0 + scale2) + shift2).astype(BF16))
-    hidden = dot(second_in, up_weight)
-    active = jax.nn.gelu(hidden, approximate=True).astype(BF16)
-    mlp = dot(active, down_weight).reshape(shape)
-    output = middle + gate2 * mlp
-    return output, (first_in, qkv, attended, branch, middle, second_in, hidden, active, mlp)
-
-
-def norm_back(grad, x, scale):
+TILE = 384
+DEPTH = 3
+GELU = math.sqrt(2.0 / math.pi)
+
+
+def columns_of(t):
+    if isinstance(t, int):
+        return pl.ds(t * TILE, TILE)
+    return pl.ds(pl.multiple_of(t * TILE, 128), TILE)
+
+
+class Stream:
+    def __init__(self, wide, tall, sems, width):
+        self.wide, self.tall, self.sems, self.width = wide, tall, sems, width
+        self.stages = []
+
+    def add(self, weight, back, inner, outer):
+        self.stages.append((weight, back, inner, outer))
+
+    def tile(self, stage, n, k):
+        weight, back, inner, _ = self.stages[stage]
+        t = n * inner + k
+        slot = lax.rem(t, DEPTH) if not isinstance(t, int) else t % DEPTH
+        deep = pl.ds(pl.multiple_of(k * self.width, 128), self.width)
+        side = columns_of(n)
+        ring = self.tall if back else self.wide
+        src = weight.at[side, deep] if back else weight.at[deep, side]
+        buffer = ring.at[stage % 2, slot]
+        return pltpu.make_async_copy(src, buffer, self.sems.at[stage % 2, slot]), buffer
+
+    def begin(self, stage):
+        if stage < len(self.stages):
+            _, _, inner, outer = self.stages[stage]
+            for t in range(min(DEPTH, inner * outer)):
+                self.tile(stage, t // inner, t % inner)[0].start()
+
+    def run(self, stage, use, ahead=True):
+        _, _, inner, outer = self.stages[stage]
+        if ahead:
+            self.begin(stage + 1)
+        count = inner * outer
+
+        def body(n, carry):
+            def product(k, left, back):
+                copy, buffer = self.tile(stage, n, k)
+                copy.wait()
+                result = (dot_back if back else dot)(left, buffer[...])
+                t = n * inner + k + DEPTH
+
+                def refill():
+                    self.tile(stage, lax.div(t, inner), lax.rem(t, inner))[0].start()
+
+                when(t < count, refill)
+                return result
+
+            use(n, product)
+            return carry
+
+        lax.fori_loop(0, outer, body, 0)
+
+
+def each_quarter(rows, run):
+    def body(q, carry):
+        run(q, pl.ds(pl.multiple_of(q * rows, rows), rows))
+        return carry
+
+    lax.fori_loop(0, 8, body, 0)
+
+
+def piece_of(mod_ref, q, p, width, columns=None):
+    if columns is None:
+        return mod_ref[q, :, p * width : (p + 1) * width]
+    return mod_ref[q, :, pl.ds(p * width + columns.start, columns.size)]
+
+
+def modulate(x_ref, mod_ref, out_ref, first, quarter_rows):
+    width = x_ref.shape[1]
+
+    def run(q, rows):
+        hat = normal(x_ref[rows, :])[0]
+        shift, scale = piece_of(mod_ref, q, first, width), piece_of(mod_ref, q, first + 1, width)
+        out_ref[rows, :] = (hat * (1.0 + scale) + shift).astype(BF16)
+
+    each_quarter(quarter_rows, run)
+
+
+def modulate_back(grad, x, scale):
     hat, inverse = normal(x)
     inner = grad * (1.0 + scale)
     along = jnp.mean(inner * hat, axis=-1, keepdims=True)
     grad_x = inverse * (inner - jnp.mean(inner, axis=-1, keepdims=True) - hat * along)
-    return grad_x, jnp.sum(grad, axis=1), jnp.sum(grad * hat, axis=1)
-
-
-def block_backward(x, segments, modulation, weights, kept, grad_out):
-    qkv_weight, proj_weight, up_weight, down_weight = weights
-    first_in, qkv, attended, branch, middle, second_in, hidden, active, mlp = kept
-    shape, width = x.shape, x.shape[-1]
-    shift1, scale1, gate1, shift2, scale2, gate2 = pieces_of(modulation)
-    grad_mlp = flat((gate2 * grad_out).astype(BF16))
-    grad_gate2 = jnp.sum(grad_out * mlp, axis=1)
-    _, pull = jax.vjp(lambda h: jax.nn.gelu(h, approximate=True), hidden)
-    grad_hidden = pull(dot_back(grad_mlp, down_weight))[0].astype(BF16)
-    grad_second = dot_back(grad_hidden, up_weight).reshape(shape)
-    grad_middle, grad_shift2, grad_scale2 = norm_back(grad_second, middle, scale2)
-    grad_middle = grad_middle + grad_out
-    grad_gate1 = jnp.sum(grad_middle * branch, axis=1)
-    grad_branch = flat((gate1 * grad_middle).astype(BF16))
-    grad_attended = dot_back(grad_branch, proj_weight).astype(BF16)
-    grad_qkv = attention_call(attend_back_kernel, (qkv, grad_attended), segments, 3 * width, 5)
-    grad_first = dot_back(grad_qkv, qkv_weight).reshape(shape)
-    grad_x, grad_shift1, grad_scale1 = norm_back(grad_first, x, scale1)
-    grad_modulation = jnp.concatenate(
-        [grad_shift1, grad_scale1, grad_gate1, grad_shift2, grad_scale2, grad_gate2], axis=-1
+    return grad_x, jnp.sum(grad, axis=0, keepdims=True), jnp.sum(grad * hat, axis=0, keepdims=True)
+
+
+def split_quarters(quarter_rows, run):
+    for q in range(8):
+        run(q, slice(q * quarter_rows, (q + 1) * quarter_rows))
+
+
+def allowed_of(row_ref, column_ref, block):
+    rows = pl.ds(pl.multiple_of(block * ATT_ROWS, ATT_ROWS), ATT_ROWS)
+    return rows, row_ref[rows, :] == column_ref[block]
+
+
+def each_block(total_rows, run):
+    def body(block, carry):
+        run(block)
+        return carry
+
+    lax.fori_loop(0, total_rows // ATT_ROWS, body, 0)
+
+
+def forward_stages(stream, weights):
+    width = weights[0].shape[0]
+    qkv, proj, up, down = weights
+    stream.add(qkv, False, 1, qkv.shape[1] // TILE)
+    stream.add(proj, False, 1, width // TILE)
+    stream.add(up, False, 1, up.shape[1] // TILE)
+    stream.add(down, False, down.shape[0] // width, width // TILE)
+
+
+def backward_stages(stream, weights):
+    width = weights[0].shape[0]
+    qkv, proj, up, down = weights
+    stream.add(down, True, 1, down.shape[0] // TILE)
+    stream.add(up, True, up.shape[1] // width, width // TILE)
+    stream.add(proj, True, 1, width // TILE)
+    stream.add(qkv, True, qkv.shape[1] // width, width // TILE)
+
+
+def proj_tile(r, mod_ref, quarter_rows, columns, branch):
+    width = r["x"].shape[1]
+    r["branch"][:, columns] = branch.astype(BF16)
+
+    def gated(q, rows):
+        gate = piece_of(mod_ref, q, 2, width, columns)
+        r["x2"][rows, columns] = r["x"][rows, columns] + gate * branch[rows]
+
+    split_quarters(quarter_rows, gated)
+
+
+def up_tile(r, columns, h):
+    square = h * h
+    t = jnp.tanh(h * (GELU + (GELU * 0.044715) * square))
+    half = 0.5 + 0.5 * t
+    r["act"][:, columns] = (h * half).astype(BF16)
+    slope = half + (0.5 * h) * (1.0 - t * t) * (GELU + (3.0 * GELU * 0.044715) * square)
+    r["slope"][:, columns] = slope.astype(BF16)
+
+
+def out_tile(r, mod_ref, quarter_rows, columns, mlp):
+    width = r["x"].shape[1]
+    r["mlp"][:, columns] = mlp.astype(BF16)
+
+    def gated(q, rows):
+        gate = piece_of(mod_ref, q, 5, width, columns)
+        r["out"][rows, columns] = (r["x2"][rows, columns] + gate * mlp[rows]).astype(BF16)
+
+    split_quarters(quarter_rows, gated)
+
+
+def run_forward(stream, r, mod_ref, segments, quarter_rows, finish_tile, done):
+    width = r["x"].shape[1]
+    total_rows = r["x"].shape[0]
+    modulate(r["x"], mod_ref, r["a1"], 0, quarter_rows)
+
+    def qkv(n, product):
+        r["qkv"][:, columns_of(n)] = product(0, r["a1"][...], False).astype(BF16)
+
+    stream.run(0, qkv)
+    done("a1")
+
+    def mix(block):
+        rows, allowed = allowed_of(*segments, block)
+        attend(r["qkv"], rows, allowed, r["total"], r["att"])
+
+    each_block(total_rows, mix)
+
+    def proj(n, product):
+        proj_tile(r, mod_ref, quarter_rows, columns_of(n), product(0, r["att"][...], False))
+
+    stream.run(1, proj)
+    done("att")
+    modulate(r["x2"], mod_ref, r["a2"], 3, quarter_rows)
+
+    def up(n, product):
+        up_tile(r, columns_of(n), product(0, r["a2"][...], False))
+
+    stream.run(2, up)
+    done("a2")
+
+    def down(n, product):
+        mlp = None
+        for k in range(r["act"].shape[1] // width):
+            part = product(k, r["act"][:, k * width : (k + 1) * width], False)
+            mlp = part if mlp is None else mlp + part
+        finish_tile(n, columns_of(n), mlp)
+
+    stream.run(3, down)
+    done("act")
+
+
+def run_backward(stream, first, r, mod_ref, segments, quarter_rows, grad_of, finish, done):
+    width = r["x"].shape[1]
+    total_rows = r["x"].shape[0]
+
+    def down(n, product):
+        columns = columns_of(n)
+        grad = product(0, r["dmlp"][...], True)
+        r["slope"][:, columns] = (grad * r["slope"][:, columns].astype(F32)).astype(BF16)
+
+    stream.run(first, down)
+    done("dmlp")
+    done("slope")
+
+    def up(n, product):
+        grad = None
+        for k in range(r["slope"].shape[1] // width):
+            part = product(k, r["slope"][:, k * width : (k + 1) * width], True)
+            grad = part if grad is None else grad + part
+        r["dx2"][:, columns_of(n)] = grad
+
+    stream.run(first + 1, up)
+
+    def middle(q, rows):
+        scale, gate = piece_of(mod_ref, q, 4, width), piece_of(mod_ref, q, 2, width)
+        grad, shift_grad, scale_grad = modulate_back(r["dx2"][rows, :], r["x2"][rows, :], scale)
+        grad = grad + grad_of(rows)
+        r["dx2"][rows, :] = grad
+        r["dmod"][q, :, 3 * width : 4 * width] = shift_grad
+        r["dmod"][q, :, 4 * width : 5 * width] = scale_grad
+        r["dmod"][q, :, 2 * width : 3 * width] = jnp.sum(
+            grad * r["branch"][rows, :].astype(F32), axis=0, keepdims=True
+        )
+        r["dbranch"][rows, :] = (gate * grad).astype(BF16)
+
+    each_quarter(quarter_rows, middle)
+
+    def proj(n, product):
+        r["datt"][:, columns_of(n)] = product(0, r["dbranch"][...], True).astype(BF16)
+
+    stream.run(first + 2, proj)
+    done("dbranch")
+
+    def mix(block):
+        rows, allowed = allowed_of(*segments, block)
+        attend_back(r["qkv"], r["datt"], rows, allowed, r["total"], r["dqkv"])
+
+    each_block(total_rows, mix)
+    done("dqkv")
+
+    def qkv(n, product):
+        grad = None
+        for k in range(3):
+            part = product(k, r["dqkv"][:, k * width : (k + 1) * width], True)
+            grad = part if grad is None else grad + part
+        r["da1"][:, columns_of(n)] = grad
+
+    stream.run(first + 3, qkv, ahead=False)
+
+    def outer(q, rows):
+        scale = piece_of(mod_ref, q, 1, width)
+        grad, shift_grad, scale_grad = modulate_back(r["da1"][rows, :], r["x"][rows, :], scale)
+        r["dmod"][q, :, :width] = shift_grad
+        r["dmod"][q, :, width : 2 * width] = scale_grad
+        finish(q, rows, grad + r["dx2"][rows, :])
+
+    each_quarter(quarter_rows, outer)
+    done("dmod")
+
+
+def placed(kept_ref, m, slot):
+    kept = kept_ref[m]
+    positions = lax.broadcasted_iota(jnp.int32, (slot, kept.shape[1]), 0)
+    return jnp.where(positions == kept, 1.0, 0.0).astype(BF16)
+
+
+class Copies:
+    def __init__(self, sems):
+        self.sems, self.count, self.pending = sems, 0, []
+
+    def start(self, src, dst):
+        copy = pltpu.make_async_copy(src, dst, self.sems.at[self.count])
+        self.count += 1
+        copy.start()
+        self.pending.append(copy)
+        return copy
+
+    def finish(self):
+        for copy in self.pending:
+            copy.wait()
+        self.pending = []
+
+
+def encode_kernel(names, tokens, kept_ref, mod_ref, row_ref, column_ref, wq, wp, wu, wd, *rest):
+    outs, scratch = rest[: len(names)], rest[len(names) :]
+    r = dict(zip(names + ("total",), scratch[: len(names) + 1]))
+    loaded, wide, tall, stream_sems, sems = scratch[len(names) + 1 :]
+    width = loaded.shape[2]
+    slot = loaded.shape[1]
+
+    def work():
+        stream = Stream(wide, tall, stream_sems, width)
+        forward_stages(stream, (wq, wp, wu, wd))
+        copies = Copies(sems)
+        copies.start(tokens, loaded)
+        stream.begin(0)
+        copies.finish()
+        kept = kept_ref.shape[2]
+        for m in range(2):
+            r["x"][m * kept : (m + 1) * kept, :] = dot_rows(placed(kept_ref, m, slot), loaded[m])
+        total_rows = r["x"].shape[0]
+        out_of = dict(zip(names, outs))
+
+        def done(name):
+            copies.start(r[name], out_of[name].at[pl.ds(0, total_rows)])
+
+        def finish_tile(n, columns, mlp):
+            out_tile(r, mod_ref, total_rows // 8, columns, mlp)
+
+        run_forward(stream, r, mod_ref, (row_ref, column_ref), total_rows // 8, finish_tile, done)
+        for name in ("x", "x2", "qkv", "branch", "slope", "mlp", "out"):
+            done(name)
+        copies.finish()
+
+    when(lax.axis_index("section") == 0, work)
+
+
+def decode_kernel(
+    names, rights, received, cotangent, kept_ref, mask_ref, mod_ref, row_ref, column_ref, wq, wp, wu, wd,
+    a1, att, a2, act, *rest,
+):
+    outs, scratch = rest[: 4 + len(rights) + 4], rest[4 + len(rights) + 4 :]
+    lefts = dict(zip(("a1", "att", "a2", "act"), outs[:4]))
+    right_outs = dict(zip(rights, outs[4 : 4 + len(rights)]))
+    dmod_out, decoded, back, mask_out = outs[4 + len(rights) :]
+    r = dict(zip(names, scratch[: len(names)]))
+    got, wide, tall, stream_sems, sems = scratch[len(names) :]
+    width = got.shape[2]
+
+    def work():
+        stream = Stream(wide, tall, stream_sems, width)
+        forward_stages(stream, (wq, wp, wu, wd))
+        backward_stages(stream, (wq, wp, wu, wd))
+        copies = Copies(sems)
+        copies.start(received, got)
+        copies.start(cotangent, r["dy"])
+        stream.begin(0)
+        copies.finish()
+        total_rows = r["x"].shape[0]
+        slot, kept = total_rows // 2, kept_ref.shape[2]
+        for m in range(2):
+            place = placed(kept_ref, m, slot)
+            flags = jnp.sum(place.astype(F32), axis=1, keepdims=True)
+            r["free"][m * slot : (m + 1) * slot, :] = jnp.broadcast_to(1.0 - flags, (slot, 128))
+            filled = dot(place, got[m]) + (1.0 - flags) * mask_ref[...].astype(F32)
+            r["x"][m * slot : (m + 1) * slot, :] = filled
+        out_of = {**lefts, **right_outs, "dmod": dmod_out, "slope": right_outs["dhid"]}
+
+        def done(name):
+            copies.start(r[name], out_of[name])
+
+        def finish_tile(n, columns, mlp):
+            def gated(q, rows):
+                gate = piece_of(mod_ref, q, 5, width, columns)
+                dy = r["dy"][rows, columns].astype(F32)
+                part = mlp[rows]
+                r["out"][rows, columns] = (r["x2"][rows, columns] + gate * part).astype(BF16)
+                r["dmlp"][rows, columns] = (gate * dy).astype(BF16)
+                r["dmod"][q, :, pl.ds(5 * width + columns.start, TILE)] = jnp.sum(
+                    dy * part, axis=0, keepdims=True
+                )
+
+            split_quarters(total_rows // 8, gated)
+
+        segments = (row_ref, column_ref)
+        run_forward(stream, r, mod_ref, segments, total_rows // 8, finish_tile, done)
+        copies.start(r["out"], decoded)
+        r["mask"][...] = jnp.zeros_like(r["mask"])
+
+        def finish(q, rows, grad):
+            r["mask"][...] += jnp.sum(grad * r["free"][rows, :1], axis=0, keepdims=True)
+            r["dbranch"][rows, :] = grad.astype(BF16)
+
+        def grad_of(rows):
+            return r["dy"][rows, :].astype(F32)
+
+        def done_back(name):
+            if name == "dbranch":
+                copies.start(r[name], out_of[name]).wait()
+                copies.pending.pop()
+            else:
+                done(name)
+
+        run_backward(stream, 4, r, mod_ref, segments, total_rows // 8, grad_of, finish, done_back)
+        for m in range(2):
+            place = placed(kept_ref, m, slot)
+            got[m] = dot_rows(place, r["dbranch"][m * slot : (m + 1) * slot, :]).astype(BF16)
+        copies.start(got, back)
+        copies.start(r["mask"], mask_out)
+        copies.finish()
+
+    when(lax.axis_index("section") == 1, work)
+
+
+def encode_back_kernel(
+    names, rights, saved, received, kept_ref, mod_ref, row_ref, column_ref, wq, wp, wu, wd, *rest
+):
+    kept_in = dict(zip(saved, rest[: len(saved)]))
+    rest = rest[len(saved) + len(rights) + 1 :]
+    right_outs = dict(zip(rights, rest[: len(rights)]))
+    dmod_out, token_out = rest[len(rights) : len(rights) + 2]
+    scratch = rest[len(rights) + 2 :]
+    r = dict(zip(names, scratch[: len(names)]))
+    wide, tall, stream_sems, sems = scratch[len(names) :]
+    width = r["x"].shape[1]
+
+    def work():
+        stream = Stream(wide, tall, stream_sems, width)
+        backward_stages(stream, (wq, wp, wu, wd))
+        copies = Copies(sems)
+        copies.start(received, r["dy"])
+        for name in saved:
+            copies.start(kept_in[name], r[name])
+        stream.begin(0)
+        copies.finish()
+        total_rows = r["x"].shape[0]
+        out_of = {**right_outs, "dmod": dmod_out, "slope": right_outs["dhid"]}
+
+        def done(name):
+            if name == "dmod":
+                copies.start(r[name], out_of[name])
+            else:
+                copies.start(r[name], out_of[name].at[pl.ds(0, total_rows)])
+
+        def start(q, rows):
+            gate = piece_of(mod_ref, q, 5, width)
+            dy = r["dy"][rows, :].astype(F32)
+            r["dmlp"][rows, :] = (gate * dy).astype(BF16)
+            r["dmod"][q, :, 5 * width :] = jnp.sum(dy * r["mlp"][rows, :].astype(F32), axis=0, keepdims=True)
+
+        each_quarter(total_rows // 8, start)
+
+        def finish(q, rows, grad):
+            r["mlp"][rows, :] = grad.astype(BF16)
+
+        def grad_of(rows):
+            return r["dy"][rows, :].astype(F32)
+
+        segments = (row_ref, column_ref)
+        run_backward(stream, 0, r, mod_ref, segments, total_rows // 8, grad_of, finish, done)
+        kept = kept_ref.shape[2]
+        slot = token_out.shape[1]
+        for m in range(2):
+            place = placed(kept_ref, m, slot)
+            r["tokens"][m] = dot(place, r["mlp"][m * kept : (m + 1) * kept, :]).astype(BF16)
+        copies.start(r["tokens"], token_out)
+        copies.finish()
+
+    when(lax.axis_index("section") == 0, work)
+
+
+VMEM_BYTES = 60 * 1024 * 1024
+LEFTS = ("a1", "att", "a2", "act")
+RIGHTS = ("dqkv", "dbranch", "dhid", "dmlp")
+SAVED = ("x", "x2", "qkv", "branch", "slope", "mlp")
+anywhere = pl.BlockSpec(memory_space=pl.ANY)
+in_vmem = pl.BlockSpec(memory_space=pltpu.VMEM)
+
+
+def buffer_shapes(rows, width, wide_width):
+    full, broad = lambda t: ((rows, width), t), lambda n, t: ((rows, n), t)
+    return {
+        "x": full(F32), "x2": full(F32), "dx2": full(F32), "da1": full(F32), "a1": full(BF16),
+        "att": full(BF16), "a2": full(BF16), "branch": full(BF16), "mlp": full(BF16), "out": full(BF16),
+        "dy": full(BF16), "dmlp": full(BF16), "dbranch": full(BF16), "datt": full(BF16),
+        "qkv": broad(3 * width, BF16), "dqkv": broad(3 * width, BF16), "act": broad(wide_width, BF16),
+        "slope": broad(wide_width, BF16), "dhid": broad(wide_width, BF16),
+        "dmod": ((8, 1, 6 * width), F32), "mask": ((1, width), F32), "free": ((rows, 128), F32),
+        "total": ((ATT_ROWS, 3 * width), F32),
+    }
+
+
+def rings(width, forward, backward):
+    dma = pltpu.SemaphoreType.DMA
+    none = (2, 1, 8, 128)
+    return [
+        pltpu.VMEM((2, DEPTH, width, TILE) if forward else none, BF16),
+        pltpu.VMEM((2, DEPTH, TILE, width) if backward else none, BF16),
+        dma((2, DEPTH)),
+        dma((24,)),
+    ]
+
+
+def encode(tokens, kept, modulation, segments, weights, rows, all_rows):
+    width, wide_width = weights[0].shape[0], weights[2].shape[1]
+    shapes = buffer_shapes(rows, width, wide_width)
+    names = LEFTS + SAVED + ("out",)
+    outs = [jax.ShapeDtypeStruct(((all_rows if n in LEFTS else rows), shapes[n][0][1]), shapes[n][1]) for n in names]
+    results = pl.pallas_call(
+        functools.partial(encode_kernel, names),
+        out_shape=outs,
+        in_specs=[anywhere] + [in_vmem] * 4 + [anywhere] * 4,
+        out_specs=[anywhere] * len(names),
+        scratch_shapes=[pltpu.VMEM(*shapes[n]) for n in names + ("total",)]
+        + [pltpu.VMEM(tokens.shape, BF16)]
+        + rings(width, True, False),
+        compiler_params=pltpu.CompilerParams(vmem_limit_bytes=VMEM_BYTES),
+        name="encode",
+    )(tokens, kept, modulation, *segments, *weights)
+    return results[:4], results[4:-1], results[-1]
+
+
+def decode(received, cotangent, kept, mask_token, modulation, segments, weights, lefts):
+    width, wide_width = weights[0].shape[0], weights[2].shape[1]
+    rows = cotangent.shape[0]
+    shapes = buffer_shapes(rows, width, wide_width)
+    names = LEFTS + (
+        "x", "x2", "qkv", "branch", "slope", "out", "dy", "dmlp", "dbranch", "datt", "dqkv", "dmod",
+        "mask", "free", "total",
     )
-    operands = ((first_in, attended, second_in, active), (grad_qkv, grad_branch, grad_hidden, grad_mlp))
-    return grad_x + grad_middle, grad_modulation, operands
-
-
-def plan_of(widths, lead, unit, other, last, names):
-    plan = []
-    for w, width in enumerate(widths):
-        for low in range(0, width, unit):
-            plan.append([w, low, unit, names[0]])
-    for j in range(lead):
-        plan.append([len(widths), j, 0, names[0]])
-    chosen = range(len(plan) - other, len(plan)) if last else range(other)
-    for j in chosen:
-        plan[j][3] = names[1]
-    return tuple(tuple(p) for p in plan)
+    scratch = [pltpu.VMEM(*shapes[n]) for n in names]
+    names += ("dx2", "da1")
+    scratch += [pltpu.VMEM(*shapes["dx2"]), pltpu.VMEM(*shapes["da1"])]
+    outs = [jax.ShapeDtypeStruct(*shapes[n]) for n in LEFTS + RIGHTS + ("dmod", "out")]
+    outs += [jax.ShapeDtypeStruct(received.shape, BF16), jax.ShapeDtypeStruct((1, width), F32)]
+    results = pl.pallas_call(
+        functools.partial(decode_kernel, names, RIGHTS),
+        out_shape=outs,
+        in_specs=[anywhere] * 2 + [in_vmem] * 5 + [anywhere] * 8,
+        out_specs=[anywhere] * len(outs),
+        scratch_shapes=scratch + [pltpu.VMEM(received.shape, BF16)] + rings(width, True, True),
+        input_output_aliases={11 + j: j for j in range(4)},
+        compiler_params=pltpu.CompilerParams(vmem_limit_bytes=VMEM_BYTES),
+        name="decode",
+    )(received, cotangent, kept, mask_token, modulation, *segments, *weights, *lefts)
+    return results[:4], results[4:8], results[8:]
+
+
+def encode_back(received, kept, modulation, segments, weights, saved, rights, grad_mod, token_shape):
+    width, wide_width = weights[0].shape[0], weights[2].shape[1]
+    rows = received.shape[0]
+    shapes = buffer_shapes(rows, width, wide_width)
+    names = SAVED + ("dy", "dmlp", "dbranch", "datt", "dqkv", "dmod", "dx2", "da1", "total", "tokens")
+    shapes["tokens"] = (token_shape, BF16)
+    outs = [jax.ShapeDtypeStruct(x.shape, x.dtype) for x in tuple(rights) + (grad_mod,)]
+    outs.append(jax.ShapeDtypeStruct(token_shape, BF16))
+    before = 9 + len(saved)
+    results = pl.pallas_call(
+        functools.partial(encode_back_kernel, names, RIGHTS, SAVED),
+        out_shape=outs,
+        in_specs=[anywhere] + [in_vmem] * 4 + [anywhere] * (4 + len(saved) + 5),
+        out_specs=[anywhere] * len(outs),
+        scratch_shapes=[pltpu.VMEM(*shapes[n]) for n in names] + rings(width, False, True),
+        input_output_aliases={before + j: j for j in range(5)},
+        compiler_params=pltpu.CompilerParams(vmem_limit_bytes=VMEM_BYTES),
+        name="encode_back",
+    )(received, kept, modulation, *segments, *weights, *saved, *rights, grad_mod)
+    return results[:4], results[4], results[5]
+
+
+def gather_encode_kernel(length, plan, names, *refs):
+    sources, (partial, big_ref, tokens, kept_ref, row_ref, column_ref) = refs[:4], refs[4:10]
+    outs, (mod_out, received) = refs[10:14], refs[14:16]
+    saved_outs = refs[16 : 16 + len(names)]
+    rest = refs[16 + len(names) :]
+    r = dict(zip(names + ("out", "total"), rest[: len(names) + 2]))
+    (
+        loaded, mod_ref, tiles, last_tile, part_held, part_core, part_pair, part_line,
+    ) = rest[len(names) + 2 : len(names) + 10]
+    sems = rest[len(names) + 10 : len(names) + 19]
+    part_sems, line_sems, tile_sems, out_sems, copy_sems = rest[len(names) + 19 :]
+    a, b, c = position()
+    encoder = lax.axis_index("section") == 0
+    other = {"section": 1 - lax.axis_index("section")}
+    barrier = pltpu.get_barrier_semaphore()
+
+    def tell(target):
+        pl.semaphore_signal(barrier, inc=1, device_id=target, device_id_type=MESH)
+
+    tell(at(a, 1 - b, c))
+    tell(at(a, b, 1 - c))
+    tell(other)
+    for k in range(1, length):
+        tell(at(lax.rem(a + k, length), b, c))
+    pl.semaphore_wait(barrier, length + 2)
+
+    n = len(plan)
+    width = r["x"].shape[1]
+    total_rows = r["x"].shape[0]
+    quarter_rows = total_rows // 8
+    issue, move, complete, drain = gather_moves(length, plan, sources, outs, sems, a, b, c)
+    copies = Copies(copy_sems)
+    out_of = dict(zip(names, saved_outs))
+
+    part_load = pltpu.make_async_copy(partial.at[:, :, c], part_held, part_sems.at[0])
+    part_to_core = remote(partial.at[:, :, 1 - c], part_core, part_sems.at[1], part_sems.at[2], at(a, b, 1 - c))
+    part_across = remote(part_held.at[:, 1 - b], part_pair, part_sems.at[3], part_sems.at[4], at(a, 1 - b, c))
+
+    def part_to_line(k):
+        to = lax.rem(a + k, length)
+        return remote(
+            part_held.at[to, b], part_line.at[k - 1], line_sems.at[0, k - 1], line_sems.at[1, k - 1], at(to, b, c)
+        )
+
+    def add_part(where, got):
+        part_held[where] = part_held[where] + got
+
+    def part_first():
+        part_to_core.wait_recv()
+        part_load.wait()
+        for s in range(2 * length):
+            add_part((s // 2, s % 2), part_core[s // 2, s % 2])
+        part_across.start()
+
+    def part_second():
+        part_across.wait()
+        for aa in range(length):
+            add_part((aa, b), part_pair[aa])
+        for k in range(1, length):
+            part_to_line(k).start()
+
+    def part_last():
+        total = part_held[a, b].astype(F32)
+        for k in range(1, length):
+            part_to_line(k).wait_recv()
+            total = total + part_line[k - 1].astype(F32)
+        for q in range(8):
+            first = q // SMALL_PER * SMALL_PER
+            mod_ref[q] = jnp.where(big_ref[q] > 0, total[first : first + 1], total[q : q + 1])
+        copies.start(mod_ref, mod_out)
+
+    def load_tile(w, low, t):
+        src = outs[w].at[:, :, :, :, pl.ds(low + t * TILE, TILE)]
+        return pltpu.make_async_copy(src, tiles.at[t % 2], tile_sems.at[t % 2])
+
+    def products(w, low, left, put):
+        count = width // TILE
+        for t in range(min(2, count)):
+            load_tile(w, low, t).start()
+        for t in range(count):
+            load_tile(w, low, t).wait()
+            tile = tiles[t % 2].astype(F32).reshape(width, TILE).astype(BF16)
+            result = dot(r[left][...], tile)
+            if t + 2 < count:
+                load_tile(w, low, t + 2).start()
+            put(columns_of(low // TILE + t), result)
+
+    def done(name):
+        copies.start(r[name], out_of[name].at[pl.ds(0, total_rows)])
+
+    def start_encode():
+        fetch = pltpu.make_async_copy(tokens, loaded, tile_sems.at[2])
+        fetch.start()
+        fetch.wait()
+        kept, slot = kept_ref.shape[2], loaded.shape[1]
+        for m in range(2):
+            r["x"][m * kept : (m + 1) * kept, :] = dot_rows(placed(kept_ref, m, slot), loaded[m])
+
+    def put_qkv(columns, result):
+        r["qkv"][:, columns] = result.astype(BF16)
+
+    def put_proj(columns, result):
+        proj_tile(r, mod_ref, quarter_rows, columns, result)
+
+    def put_up(columns, result):
+        up_tile(r, columns, result)
+
+    def send_out(t):
+        columns = columns_of(t)
+        return remote(
+            r["out"].at[:, columns], received.at[:, columns], out_sems.at[0, t], out_sems.at[1, t], other
+        )
+
+    def encode_chunk(i):
+        w, low, _, _ = plan[i]
+        if w == 0:
+            if i == 0:
+                modulate(r["x"], mod_ref, r["a1"], 0, quarter_rows)
+            products(w, low, "a1", put_qkv)
+        elif w == 1:
+            rows, allowed = slice(0, total_rows), row_ref[...] == column_ref[0]
+            attend(r["qkv"], rows, allowed, r["total"], r["att"])
+            products(w, low, "att", put_proj)
+            modulate(r["x2"], mod_ref, r["a2"], 3, quarter_rows)
+        elif w == 2:
+            products(w, low, "a2", put_up)
+        else:
+            src = outs[w].at[:, :, :, :, pl.ds(low, TILE)]
+            fetch = pltpu.make_async_copy(src, last_tile, tile_sems.at[2])
+            fetch.start()
+            fetch.wait()
+            tile = last_tile[...].reshape(r["act"].shape[1], TILE)
+            out_tile(r, mod_ref, quarter_rows, columns_of(low // TILE), dot(r["act"][...], tile))
+            send_out(low // TILE).start()
+
+    part_load.start()
+    part_to_core.start()
+    issue(0)
+    when(encoder, start_encode)
+    part_first()
+    for i in range(1, AHEAD):
+        issue(i)
+    for t in range(n + length - 1):
+        move(t, AHEAD)
+        if t == 0:
+            part_second()
+        if t == 1:
+            part_last()
+        i = t - length + 1
+        if i >= 0:
+            complete(i)
+            when(encoder, lambda: encode_chunk(i))
+    for i in range(n):
+        drain(i)
+    part_to_core.wait_send()
+    for k in range(1, length):
+        part_to_line(k).wait_send()
+
+    def close():
+        for name in names:
+            done(name)
+        for copy in copies.pending[1:]:
+            copy.wait()
+        for t in range(width // TILE):
+            send_out(t).wait_send()
+
+    when(encoder, close)
+    copies.pending[0].wait()
+
+    def arrive():
+        for t in range(width // TILE):
+            send_out(t).wait_recv()
+
+    when(jnp.logical_not(encoder), arrive)
+
+
+AHEAD = 4
+
+
+def gather_encode(shards, partial, big, tokens, kept, segments, plan, length, rows, all_rows):
+    n = len(plan)
+    width, wide_width = shards[1].shape[1], shards[2].shape[1]
+    shapes = buffer_shapes(rows, width, wide_width)
+    names = LEFTS + SAVED
+    quarters = partial.shape[3]
+    part_slab = partial.shape[3:]
+    dma = pltpu.SemaphoreType.DMA
+    outs = [jax.ShapeDtypeStruct((length, 2, 2) + s.shape, BF16) for s in shards]
+    outs += [jax.ShapeDtypeStruct((quarters, 1, 6 * width), F32), jax.ShapeDtypeStruct((rows, width), BF16)]
+    outs += [jax.ShapeDtypeStruct(((all_rows if m in LEFTS else rows), shapes[m][0][1]), shapes[m][1]) for m in names]
+    results = pl.pallas_call(
+        functools.partial(gather_encode_kernel, length, plan, names),
+        out_shape=outs,
+        in_specs=[anywhere] * 5 + [in_vmem, anywhere] + [in_vmem] * 3,
+        out_specs=[anywhere] * len(outs),
+        scratch_shapes=[pltpu.VMEM(*shapes[m]) for m in names + ("out", "total")]
+        + [
+            pltpu.VMEM(tokens.shape, BF16),
+            pltpu.VMEM((quarters, 1, 6 * width), F32),
+            pltpu.VMEM((2, length, 2, 2, shards[0].shape[0], TILE), BF16),
+            pltpu.VMEM((length, 2, 2, shards[3].shape[0], TILE), BF16),
+            pltpu.VMEM((length, 2) + part_slab, BF16),
+            pltpu.VMEM((length, 2) + part_slab, BF16),
+            pltpu.VMEM((length,) + part_slab, BF16),
+            pltpu.VMEM((length - 1,) + part_slab, BF16),
+        ]
+        + [dma((n, length, 2))] * 4
+        + [dma((n, length))] * 2
+        + [dma((n, length, 2))] * 2
+        + [dma((n,)), dma((5,)), dma((2, length - 1)), dma((3,)), dma((2, width // TILE)), dma((len(names) + 1,))],
+        compiler_params=pltpu.CompilerParams(
+            collective_id=0, has_side_effects=True, vmem_limit_bytes=VMEM_BYTES
+        ),
+        name="gather_encode",
+    )(*shards, partial, big, tokens, kept, *segments)
+    return results[:4], results[4], results[5], results[6:10], results[10:]
+
+
+def plan_of(widths, lead, unit, line_first):
+    plan = [(w, low, unit) for w, width in enumerate(widths) for low in range(0, width, unit)]
+    plan += [(len(widths), j, 0) for j in range(lead)]
+    return tuple(p + ("line" if i in line_first else "pair",) for i, p in enumerate(plan))
 
 
 def swap_sections(x):
@@ -763,73 +1459,53 @@
         jnp.zeros((1, 6 * width), F32), ada_bias.astype(F32), me * bias_width, axis=1
     )
     partial = (dot(lifted, ada) + bias).astype(BF16).reshape(devices, images, 6 * width)
-    modulation = lax.psum_scatter(partial, "dp", scatter_dimension=0, tiled=False).astype(F32)
+
+    big = big_image[:, :1] > 0
+    quarter_ids = jnp.arange(quarters, dtype=jnp.int32).reshape(micro, SMALL_PER)
+    segment_of = jnp.where(big, quarter_ids[:, :1], quarter_ids).reshape(quarters)
+    kept = kept_index.reshape(micro, 1, kept_count)
+
+    def segments(quarter_rows):
+        ids = jnp.repeat(segment_of, quarter_rows)
+        return ids.reshape(-1, 1), ids.reshape(-1, 1, ATT_ROWS)
+
+    enc_rows, dec_rows = micro * kept_count, micro * slot
+    enc_segments = segments(enc_rows // quarters)
+    dec_segments = segments(dec_rows // quarters)
 
     shards = (qkv_weight[0], proj_weight[0], up_weight[0])
     lead = down_weight.shape[1] // qkv_weight.shape[1]
-    down_shard = down_weight[0].reshape(lead, own_width, width)
-    widths = [s.shape[1] for s in shards]
+    widths = [x.shape[1] for x in shards]
     if length == 4:
-        plan = plan_of(widths, lead, width, 2, True, ("line", "pair"))
-        whole = gather_all(shards + (down_shard,), plan, length)
+        plan = [(w, low, width, "line") for w in range(3) for low in range(0, widths[w], width)]
+        plan += [(3, low, TILE, "line") for low in range(0, width, TILE)]
+        plan = tuple(p[:3] + ("pair" if i in (1, 7) else "line",) for i, p in enumerate(plan))
+        flags = jnp.repeat(big[:, 0], SMALL_PER).astype(jnp.int32).reshape(quarters, 1, 1)
+        whole, modulation, received, lefts, saved = gather_encode(
+            shards + (down_weight[0],), partial.reshape((length, 2, 2) + partial.shape[1:]), flags, tokens, kept,
+            enc_segments, plan, length, enc_rows, dec_rows,
+        )
+        weights = tuple(w.reshape(-1, w.shape[-1]) for w in whole)
+        received = received.reshape(micro, kept_count, width)
     else:
-        whole = tuple(lax.all_gather(s, "dp", axis=0) for s in shards + (down_shard,))
-    weights = tuple(w.reshape(-1, w.shape[-1]) for w in whole)
-
-    big = big_image[:, :1] > 0
-    modulation = modulation.reshape(micro, SMALL_PER, 6 * width)
-    modulation = jnp.where(big[:, :, None], modulation[:, :1], modulation).reshape(quarters, 6 * width)
-    quarter_ids = jnp.arange(quarters, dtype=jnp.int32).reshape(micro, SMALL_PER)
-    segment_of = jnp.where(big, quarter_ids[:, :1], quarter_ids).reshape(quarters)
-    positions = jnp.arange(slot, dtype=jnp.int32)
-    placement = (positions[None, :, None] == kept_index[:, None, :]).astype(BF16)
-    enc_segments = jnp.repeat(segment_of, kept_count // SMALL_PER)
-    dec_segments = jnp.repeat(segment_of, slot // SMALL_PER)
-
-    def to_kept(rows):
-        return jnp.einsum("msk,msd->mkd", placement, rows, preferred_element_type=F32)
-
-    def to_slots(rows):
-        return jnp.einsum("msk,mkd->msd", placement, rows, preferred_element_type=F32)
-
-    enc_rows = (quarters, kept_count // SMALL_PER, width)
-    dec_rows = (quarters, slot // SMALL_PER, width)
-
-    def encode():
-        x = to_kept(tokens).reshape(enc_rows)
-        out, kept = block_forward(x, enc_segments, modulation, weights)
-        return out.astype(BF16), (x, kept)
-
-    idle = lambda f: jax.tree.map(lambda s: jnp.zeros(s.shape, s.dtype), jax.eval_shape(f))
-    encoded, enc_kept = lax.cond(section == 0, encode, lambda: idle(encode))
-    received = swap_sections(encoded).reshape(micro, kept_count, width)
-
-    def decode():
-        flags = jnp.sum(placement.astype(F32), axis=2)[:, :, None]
-        x = to_slots(received) + (1.0 - flags) * mask_token.astype(F32)[None, None, :]
-        x = x.reshape(dec_rows)
-        out, kept = block_forward(x, dec_segments, modulation, weights)
-        grad = cotangent.astype(F32).reshape(dec_rows)
-        grad_x, grad_mod, grads = block_backward(x, dec_segments, modulation, weights, kept, grad)
-        grad_x = grad_x.reshape(micro, slot, width)
-        mask_part = jnp.sum((1.0 - flags) * grad_x, axis=(0, 1))
-        back = to_kept(grad_x.astype(BF16)).astype(BF16)
-        return out.astype(BF16).reshape(micro, slot, width), mask_part, back, grad_mod, grads
-
-    decoded, mask_part, back, grad_mod, grads = lax.cond(section == 1, decode, lambda: idle(decode))
-    received = swap_sections(back)
-
-    def encode_back():
-        x, kept = enc_kept
-        grad = received.astype(F32).reshape(enc_rows)
-        grad_x, grad_mod, grads = block_backward(x, enc_segments, modulation, weights, kept, grad)
-        grad_x = grad_x.astype(BF16).reshape(micro, kept_count, width)
-        grads = jax.tree.map(lambda g: jnp.pad(g, ((0, micro * (slot - kept_count)), (0, 0))), grads)
-        return to_slots(grad_x).astype(BF16), grad_mod, grads
-
-    token_grad, grad_mod, grads = lax.cond(
-        section == 0, encode_back, lambda: (jnp.zeros_like(decoded), grad_mod, grads)
+        whole = (lax.all_gather(x, "dp", axis=0, tiled=True) for x in shards + (down_weight[0],))
+        weights = tuple(whole)
+        modulation = lax.psum_scatter(partial, "dp", scatter_dimension=0, tiled=False).astype(F32)
+        modulation = modulation.reshape(micro, SMALL_PER, 6 * width)
+        modulation = jnp.where(big[:, :, None], modulation[:, :1], modulation).reshape(quarters, 1, 6 * width)
+        lefts, saved, encoded = encode(tokens, kept, modulation, enc_segments, weights, enc_rows, dec_rows)
+        received = swap_sections(encoded).reshape(micro, kept_count, width)
+
+    lefts, rights, (grad_mod, decoded, back, mask_part) = decode(
+        received, cotangent.reshape(dec_rows, width), kept, mask_token.reshape(1, width), modulation,
+        dec_segments, weights, lefts,
     )
+    received = swap_sections(back).reshape(enc_rows, width)
+    rights, grad_mod, token_grad = encode_back(
+        received, kept, modulation, enc_segments, weights, saved, rights, grad_mod, (micro, slot, width)
+    )
+    decoded = decoded.reshape(micro, slot, width)
+    mask_part = jnp.where(section == 1, mask_part, 0.0).reshape(width)
 
     half_width = width // 2
     outgoing = jnp.where(section == 0, token_grad[:, :, half_width:], decoded[:, :, :half_width])
@@ -867,13 +1543,13 @@
     )
     time_grad, table_grad = shared[: time_weight.shape[0]], shared[time_weight.shape[0] :]
 
-    shapes = tuple(x.shape for x in shards + (down_shard,))
-    lefts, rights = grads
+    shapes = tuple(x.shape for x in shards) + ((lead, own_width, width),)
+    half_rows = jnp.arange(dec_rows)[:, None] < jnp.where(section == 0, enc_rows, dec_rows)
     if length == 4:
-        names = ("pair", "line")
-        plan = plan_of(widths, lead, width, 2, False, names)
+        plan = plan_of(widths, lead, width, (0, 6))
         mine = scatter_all(lefts, rights, shapes, plan, length)
     else:
+        lefts, rights = ([jnp.where(half_rows, x, jnp.zeros_like(x)) for x in xs] for xs in (lefts, rights))
         split = (dot_rows(x, y).astype(BF16).reshape((devices,) + s) for x, y, s in zip(lefts, rights, shapes))
         mine = tuple(lax.psum_scatter(g, "dp", scatter_dimension=0) for g in split)
     qkv_grad, proj_grad, up_grad, down_grad = (g.astype(F32) for g in mine)

time: 781 us -> 658 us (0.84)
  matrix products: 60.4 us -> 9.93 us
  Pallas kernels: 426 us -> 473 us
  other arithmetic: 49.6 us -> 15.4 us
  starting transfers between devices: 136 us -> 102 us
  local copies, waits for them, and re-layouts: 54.1 us -> 20.4 us
  waiting for transfers between devices: 27.3 us -> 13.6 us
    pallas_call x3, Pallas kernels: 190 us -> 246 us  [the longest x1 193 us: gather_encode(): pl.pallas_call(functools.partial(gather_encode_kernel, length, plan, name...]
    ppermute x3 -> x2, starting transfers between devices: 136 us -> 102 us  [swap_sections(): return lax.ppermute(x, 'section', [(0, 1), (1, 0)])]
    dot_general x7 -> x3, matrix products: 32 us -> 4.94 us  [dot(): return jnp.dot(x, y, preferred_element_type=F32)]
    dot_general x5 -> x1, matrix products: 22.4 us -> 2.24 us  [dot_back(): lax.dot_general(x, y, (((1,), (1,)), ((), ())), preferred_element_type=F32)]
    reduce_sum x11 -> x0, other arithmetic: 17.8 us -> none  [the longest x4 5.41 us: normal(): scale = lax.rsqrt(jnp.mean(centred * centred, axis=-1, keepdims=True) + EPS)]
    pad x8 -> x0, local copies, waits for them, and re-layouts: 17.5 us -> none  [encode_back(): jnp.pad(g, ((0, micro * (slot - kept_count)), (0, 0)))]
    ppermute x3 -> x2, waiting for transfers between devices: 27.3 us -> 13.6 us  [swap_sections(): return lax.ppermute(x, 'section', [(0, 1), (1, 0)])]
    another operation x14 -> x3, local copies, waits for them, and re-layouts: 14.6 us -> 2.36 us  [segments(): return (ids.reshape(-1, 1), ids.reshape(-1, 1, ATT_ROWS))]
  transfers between devices with their start and end apart: 5 -> 3, of which waited for: 2 -> 1; matrix products, arithmetic and copies ran while one was open for 2% -> 2% of each run, Pallas kernels for 49% -> 30%
where the time goes in v3:
time: 658 us; the launch traced here: 648 us
  Pallas kernels  473 us (72%)
  starting transfers between devices  102 us (16%)
  local copies, waits for them, and re-layouts  20.4 us (3%)
  other arithmetic  15.4 us (2%)
  between operations  14.5 us (2%)
  waiting for transfers between devices  13.6 us (2%)
  matrix products  9.93 us (2%)
    pallas_call x1, Pallas kernels, scatter_all(): pl.pallas_call(functools.partial(scatter_kernel, length, plan, slots, pai...  197 us
    pallas_call x1, Pallas kernels, gather_encode(): pl.pallas_call(functools.partial(gather_encode_kernel, length, plan, name...  193 us
    ppermute x2, starting transfers between devices, swap_sections(): return lax.ppermute(x, 'section', [(0, 1), (1, 0)])  102 us
    pallas_call x1, Pallas kernels, encode_back(): pl.pallas_call(functools.partial(encode_back_kernel, names, RIGHTS, SAVED...  42.5 us
    pallas_call x2, Pallas kernels, small_gather(): pl.pallas_call(functools.partial(small_gather_kernel, length, sum_section...  30.1 us
    ppermute x2, waiting for transfers between devices, swap_sections(): return lax.ppermute(x, 'section', [(0, 1), (1, 0)])  13.6 us
  transfers between devices with their start and end apart: 3, of which 1 were waited for; matrix products, arithmetic and copies ran while one was open for 2% of the time, Pallas kernels for 30%

profile of v3, /device:TPU:0, one launch (start us, length us, event | category | flops | bytes accessed | tf_op | source)
XLA Modules:
  0.0 648.5 jit_solution(9413423270658482178)
XLA Ops:
  7.3 0.1 slice_reduce_fusion.1
  7.4 0.1 reshape.162
  7.5 0.7 compare_bitcast_fusion
  8.2 0.1 broadcast_in_dim.109
  8.2 0.1 broadcast_in_dim.110
  8.3 0.1 broadcast_in_dim.112
  8.4 0.1 broadcast_in_dim.113
  8.5 0.1 broadcast_in_dim.114
  8.6 0.8 reshape_reshape.22.refs_8_.row_ref
  9.3 0.7 reshape_reshape.18.refs_9_.column_ref
  10.0 0.1 broadcast_select_fusion.1
  10.1 0.8 reshape.155
  10.8 0.8 reshape.156
  11.6 0.6 pad.8.own_ref
  12.2 12.8 %small_gather.2 = s32[4,2,2,8,128]{4,3,2,1,0:T(8,128)} custom-call(s32[8,128]{1,0:T(8,128)} %pad.8.own_ref), custom_call_target="tpu_custom_call" | custom-call | tf_op jit(solution)/shard_map/small_gather/pallas_call | solution.py:549
  25.0 0.9 fusion.30
  25.9 0.1 convert_element_type.52
  26.0 0.1 eq.31
  26.1 0.7 add.47
  26.8 0.1 broadcast_in_dim.108
  26.9 0.7 convert_element_type.61.refs_5_
  27.5 0.1 broadcast_in_dim.115
  27.6 0.9 reshape_reshape.21.row_ref
  28.5 0.1 broadcast_in_dim.116
  28.6 0.7 broadcast_in_dim.117.column_ref
  29.3 1.3 reshape.165.mask_ref
  30.5 0.3 fusion.15
  30.9 2.7 fusion.6
  33.6 0.3 fusion.17
  33.9 0.8 copy-done.4
  34.8 0.3 dynamic_update_slice.4
  35.1 1.9 fusion.1
  37.0 192.9 %gather_encode.1 = (bf16[4,2,2,72,3456]{4,3,2,1,0:T(8,128)(2,1)}, bf16[4,2,2,72,1152]{4,3,2,1,0:T(8,128)(2,1)}, bf16[4,2,2,72,4608]{4,3,2,1,0:T(8,128)(2,1)}, bf...) custom-call(bf16[72,3456]{1,0:T(8,128)(2,1)} %bitcast.87, ...), custom_call_target="tpu_custom_call" | custom-call | tf_op jit(solution)/shard_map/gather_encode/pallas_call | solution.py:1389
  229.9 10.3 %decode.1 = (bf16[512,1152]{1,0:T(8,128)(2,1)}, bf16[512,1152]{1,0:T(8,128)(2,1)}, bf16[512,1152]{1,0:T(8,128)(2,1)}, bf16[512,4608]{1,0:T(8,128)(2,1)}, bf16[51...) custom-call(bf16[2,128,1152]{2,1,0:T(8,128)(2,1)} %bitcast.86, ...), custom_call_target="tpu_custom_call", output_to_operand_aliasing={{0}: (11, {}), {1}: (12, {}), {2}: (13, {}), {3}: (14, {})} | custom-call | tf_op jit(solution)/shard_map/decode/pallas_call | solution.py:1164
  240.2 101.7 %collective-permute-start = (bf16[2,128,1152]{2,1,0:T(8,128)(2,1)}, bf16[2,128,1152]{2,1,0:T(8,128)(2,1)S(1)}, u32[]{:S(2)}, u32[]{:S(2)}) collective-permute-start(bf16[2,128,1152]{2,1,0:T(8,128)(2,1)} %get-tuple-element.59), channel_id=1, source_target_pairs={{0,16},{16,0},{1,17},{17,1},{2,18},{18,2},{3,19},{19,3},{4,20},{20... | collective-permute-start | bytes 1769480 | tf_op jit(solution)/shard_map/ppermute | solution.py:1424
  341.8 0.1 broadcast_in_dim.120
  342.0 0.1 fusion.5
  342.1 13.6 %collective-permute-done = bf16[2,128,1152]{2,1,0:T(8,128)(2,1)S(1)} collective-permute-done((bf16[2,128,1152]{2,1,0:T(8,128)(2,1)}, bf16[2,128,1152]{2,1,0:T(8,128)(2,1)S(1)}, u32[]{:S(2)}, u32[]{:S(2)}) %collective-permute-start) | collective-permute-done | bytes 589856 | tf_op jit(solution)/shard_map/ppermute | solution.py:1424
  355.6 0.8 copy-done.9
  356.5 42.5 %encode_back.1 = (bf16[512,3456]{1,0:T(8,128)(2,1)}, bf16[512,1152]{1,0:T(8,128)(2,1)}, bf16[512,4608]{1,0:T(8,128)(2,1)}, bf16[512,1152]{1,0:T(8,128)(2,1)}, f3...) custom-call(bf16[256,1152]{1,0:T(8,128)(2,1)} %bitcast.85, ...), custom_call_target="tpu_custom_call", output_to_operand_aliasing={{0}: (15, {}), {1}: (16, {}), {2}: (17, {}), {3}: (18, {}),... | custom-call | tf_op jit(solution)/shard_map/encode_back/pallas_call | solution.py:1186
  399.0 1.6 reduce.1
  400.7 0.1 fusion
  400.8 0.7 fusion.14
  401.6 1.4 slice_select_fusion.1
  403.0 1.1 copy.54
  404.0 197.2 %scatter_grads.1 = (bf16[72,3456]{1,0:T(8,128)(2,1)}, bf16[72,1152]{1,0:T(8,128)(2,1)}, bf16[72,4608]{1,0:T(8,128)(2,1)}, bf16[4,72,1152]{2,1,0:T(8,128)(2,1)}) custom-call(bf16[512,1152]{1,0:T(8,128)(2,1)} %get-tuple-element.75.refs_0_, bf16[512,1152]{1,0:T(8,128)(2,1)} %get-tuple-element.76.refs_1_, bf16[512,1152]{1,0:T(8,128)(2,1)} %get-tuple-element.77.refs_2_, ...), custom_call_target="tpu_custom_call" | custom-call | tf_op jit(solution)/shard_map/scatter_grads/pallas_call | solution.py:473
  601.2 2.2 bitcast_convert_fusion.2
  603.4 1.2 bitcast_convert_fusion.1
  604.6 0.7 bitcast_convert_fusion.3
  605.3 1.1 bitcast_convert_fusion
  606.5 1.4 copy.55
  607.8 1.6 slice_select_fusion.2
  609.4 1.1 copy.57
  610.5 1.1 copy.58
  611.6 2.2 fusion.23
  613.8 0.6 select_maximum_fusion.own_ref
  614.4 17.4 %small_gather.3 = f32[4,2,2,88,128]{4,3,2,1,0:T(8,128)} custom-call(f32[88,128]{1,0:T(8,128)} %select_maximum_fusion.own_ref), custom_call_target="tpu_custom_call" | custom-call | tf_op jit(solution)/shard_map/small_gather/pallas_call | solution.py:549
  631.8 1.1 slice.62
  632.9 1.1 fusion.7
  634.0 2.4 slice.54
  636.4 1.1 slice.53
  637.5 1.5 slice_reduce_fusion
  639.1 1.7 convolution_bitcast_fusion
  640.8 0.7 convert_reduce_fusion
  (37 shorter events, 0.3 us)
Async XLA Ops:
  7.2 27.9 %copy-start = (bf16[1,72,6912]{2,1,0:T(8,128)(2,1)S(1)}, bf16[1,72,6912]{2,1,0:T(8,128)(2,1)}, u32[]{:S(2)}) copy-start(bf16[1,72,6912]{2,1,0:T(8,128)(2,1)} %param.24) | copy-start | bytes 2985988
  7.2 604.4 %all-gather.2.cloned.1.call-start = ((), (), s32[]{:S(2)}) async-start(), calls=%async_computation | async-start | bytes 1880064 | tf_op jit(solution)/shard_map/all_gather | solution.py:1522
  8.6 25.0 %copy-start.8 = (bf16[256,1152]{1,0:T(8,128)(2,1)S(1)}, bf16[256,1152]{1,0:T(8,128)(2,1)}, u32[]{:S(2)}) copy-start(bf16[256,1152]{1,0:T(8,128)(2,1)} %param.22) | copy-start | bytes 1769476
  33.6 3.4 copy-start.5
  33.9 0.8 copy-start.4
  240.2 115.5 %collective-permute-start = (bf16[2,128,1152]{2,1,0:T(8,128)(2,1)}, bf16[2,128,1152]{2,1,0:T(8,128)(2,1)S(1)}, u32[]{:S(2)}, u32[]{:S(2)}) collective-permute-start(bf16[2,128,1152]{2,1,0:T(8,128)(2,1)} %get-tuple-element.59), channel_id=1, source_target_pairs={{0,16},{16,0},{1,17},{17,1},{2,18},{18,2},{3,19},{19,3},{4,20},{20... | collective-permute-start | bytes 1769480 | tf_op jit(solution)/shard_map/ppermute | solution.py:1424
  355.6 0.8 copy-start.9
  399.0 1.8 copy-start.2
  399.0 2.6 copy-start.3
  404.0 202.4 %collective-permute-start.1 = (bf16[2,256,576]{1,2,0:T(8,128)(2,1)}, bf16[2,256,576]{1,2,0:T(8,128)(2,1)}, u32[]{:S(2)}, u32[]{:S(2)}) collective-permute-start(bf16[2,256,576]{1,2,0:T(8,128)(2,1)} %copy.54), channel_id=1, source_target_pairs={{0,16},{16,0},{1,17},{17,1},{2,18},{18,2},{3,19},{19,3},{4,20},{20... | collective-permute-start | bytes 1769480 | tf_op jit(solution)/shard_map/ppermute | solution.py:1424
  601.2 2.2 copy-start.7
  601.2 3.3 copy-start.10
  601.2 4.1 copy-start.6
  636.4 2.6 copy-start.1
Sparse Core Ops, SparseCore 0:
  401.7 40.9 all-gather.1

commit v4 on v3

--- a/solution.py
+++ b/solution.py
@@ -17,6 +17,10 @@
 MESH = pl.DeviceIdType.MESH
 F32 = jnp.float32
 BF16 = jnp.bfloat16
+
+
+anywhere = pl.BlockSpec(memory_space=pl.ANY)
+in_vmem = pl.BlockSpec(memory_space=pltpu.VMEM)
 
 
 def remote(src, dst, send_sem, recv_sem, target):
@@ -199,18 +203,133 @@
     return issue, move, complete, drain
 
 
+SIDE_TIMES = (2, 4, 5, 6, 8, 10)
+
+
+def greet_all(length, a, b, c):
+    barrier = pltpu.get_barrier_semaphore()
+
+    def tell(target):
+        pl.semaphore_signal(barrier, inc=1, device_id=target, device_id_type=MESH)
+
+    tell(at(a, 1 - b, c))
+    tell(at(a, b, 1 - c))
+    tell({"section": 1 - lax.axis_index("section")})
+    for k in range(1, length):
+        tell(at(lax.rem(a + k, length), b, c))
+    pl.semaphore_wait(barrier, length + 2)
+
+
+def spread(length, buffer, sems, a, b, c):
+    line_s, line_r, pair_core = sems
+
+    def to_line(k):
+        mine = buffer.at[a, b, c]
+        return remote(mine, mine, line_s.at[k - 1], line_r.at[k - 1], at(lax.rem(a + k, length), b, c))
+
+    def from_line(k):
+        slab = buffer.at[lax.rem(a + length - k, length), b, c]
+        return remote(slab, slab, line_s.at[k - 1], line_r.at[k - 1], at(a, 1 - b, c))
+
+    def across(bb):
+        part = buffer.at[:, bb, c]
+        return remote(part, part, pair_core.at[0], pair_core.at[1], at(a, 1 - b, c))
+
+    def to_core(cc):
+        part = buffer.at[:, :, cc]
+        return remote(part, part, pair_core.at[2], pair_core.at[3], at(a, b, 1 - c))
+
+    def start():
+        for k in range(1, length):
+            to_line(k).start()
+
+    def second():
+        for k in range(1, length):
+            from_line(k).wait_recv()
+            to_line(k).wait_send()
+        across(b).start()
+
+    def third():
+        across(1 - b).wait_recv()
+        across(b).wait_send()
+        to_core(c).start()
+
+    def end():
+        to_core(1 - c).wait_recv()
+        to_core(c).wait_send()
+
+    return start, second, third, end
+
+
+def conditioning_steps(length, inputs, outputs, scratch, a, b, c):
+    grad_mod, lifted_t, slope_t, ada, mask_rows = inputs
+    ada_grad, bias_sum, shared = outputs
+    every, stage, payload, other = scratch[:4]
+    mod_sems, shared_sems, side_sems, stage_sems = scratch[4:7], scratch[7:10], scratch[10], scratch[11]
+    mod_start, mod_second, mod_third, mod_end = spread(length, every, mod_sems, a, b, c)
+    shared_start, shared_second, shared_third, shared_end = spread(length, shared, shared_sems, a, b, c)
+    own_rows, images = lifted_t.shape
+    mask_count = mask_rows.shape[0]
+    width = stage.shape[2]
+    count = grad_mod.shape[1] // width
+    side = remote(payload, other, side_sems.at[0], side_sems.at[1], {"section": 1 - lax.axis_index("section")})
+
+    def save(j):
+        return pltpu.make_async_copy(
+            stage.at[j % 2], ada_grad.at[:, pl.ds(j * width, width)], stage_sems.at[j % 2]
+        )
+
+    def begin():
+        every[a, b, c] = grad_mod[...]
+        mod_start()
+
+    def compute():
+        mod_end()
+        total = None
+        for j in range(count):
+            columns = slice(j * width, (j + 1) * width)
+            rows = every[:, :, :, :, columns].astype(F32).reshape(images, width)
+            bias_sum[:, columns] = jnp.sum(rows, axis=0, keepdims=True)
+            rows = rows.astype(BF16)
+            if j >= 2:
+                save(j - 2).wait()
+            stage[j % 2] = dot(lifted_t[...], rows)
+            save(j).start()
+            part = dot_back(ada[:, columns], rows)
+            total = part if total is None else total + part
+        payload[...] = jnp.zeros_like(payload)
+        payload[:own_rows, :] = total * slope_t[...]
+        payload[own_rows : own_rows + mask_count, :] = mask_rows[...]
+        side.start()
+
+    def add():
+        side.wait()
+        shared[a, b, c] = payload[...] + other[...]
+        shared_start()
+
+    def end():
+        shared_end()
+        for j in range(count - 2, count):
+            save(j).wait()
+
+    return begin, mod_second, mod_third, compute, add, shared_second, shared_third, end
+
+
 def scatter_kernel(length, plan, slots, pair_slots, *refs):
     lefts, rights = refs[:4], refs[4:8]
-    outs = refs[8:12]
+    extras = refs[8:13]
+    outs = refs[13:17]
+    extra_outs = refs[17:20]
     (
         raw, right, left_t, held, sent, core_in, pair_in, pair_late, up_in, down_in,
-    ) = refs[12:22]
+    ) = refs[20:30]
     (
         raw_sem, right_sem, core_s, core_r, pair_s, pair_r, up_s, up_r, down_s, down_r, out_sem,
         core_credit, pair_credit,
-    ) = refs[22:]
+    ) = refs[30:43]
     a, b, c = position()
-    greet(length, a, b, c)
+    greet_all(length, a, b, c)
+    side_steps = conditioning_steps(length, extras, extra_outs, refs[43:], a, b, c)
     n = len(plan)
     rows, width = held.shape[3:]
     total_rows = raw.shape[1]
@@ -424,11 +543,14 @@
             add(held.at[i, a, b], pair_late.at[order[i]])
             result(i).start()
 
+    side_steps[0]()
     raw_load(0).start()
     right_load(0).start()
     raw_load(1).start()
     produce(0)
     for t in range(n + length + 3):
+        if t in SIDE_TIMES:
+            side_steps[SIDE_TIMES.index(t) + 1]()
         if t < n:
             first_add(t)
         if t + 1 < n:
@@ -442,6 +564,7 @@
             finish(t - 1 - length)
         if 0 <= t - 2 - length < n:
             finish_late(t - 2 - length)
+    side_steps[-1]()
     for i in range(n):
         if i >= n - slots:
             to_core(i).wait_send()
@@ -459,7 +582,7 @@
                 when(a == here, gone)
 
 
-def scatter_all(lefts, rights, shard_shapes, plan, length):
+def scatter_all(lefts, rights, extras, shard_shapes, plan, length):
     n = len(plan)
     slots, pair_slots = 2, 4
     total_rows = lefts[0].shape[0]
@@ -468,13 +591,21 @@
     flows = (length - 1) * (n + late)
     lead = shard_shapes[-1][0]
     dma = pltpu.SemaphoreType.DMA
-    anywhere = pl.BlockSpec(memory_space=pl.ANY)
+    grad_mod, lifted_t, slope_t, ada, mask_rows = extras
+    images = lifted_t.shape[1]
+    payload = (-(-(rows + mask_rows.shape[0]) // 8) * 8, images)
+    small = [dma((length - 1,)), dma((length - 1,)), dma((4,))]
     slab = (rows, width)
     return pl.pallas_call(
         functools.partial(scatter_kernel, length, plan, slots, pair_slots),
-        out_shape=tuple(jax.ShapeDtypeStruct(s, BF16) for s in shard_shapes),
-        in_specs=[anywhere] * 8,
-        out_specs=[anywhere] * 4,
+        out_shape=tuple(jax.ShapeDtypeStruct(s, BF16) for s in shard_shapes)
+        + (
+            jax.ShapeDtypeStruct(ada.shape, F32),
+            jax.ShapeDtypeStruct((1, ada.shape[1]), F32),
+            jax.ShapeDtypeStruct((length, 2, 2) + payload, F32),
+        ),
+        in_specs=[anywhere] * 8 + [in_vmem] * 5,
+        out_specs=[anywhere] * 5 + [in_vmem] * 2,
         scratch_shapes=[
             pltpu.VMEM((2, total_rows, width), BF16),
             pltpu.VMEM((2, total_rows, width), BF16),
@@ -489,12 +620,19 @@
             dma((lead + 3,)), dma((n,)), dma((n,)), dma((n,)), dma((n,)), dma((n,)),
             dma((flows,)), dma((flows,)), dma((flows,)), dma((flows,)), dma((n,)),
             pltpu.SemaphoreType.REGULAR, pltpu.SemaphoreType.REGULAR,
-        ],
+            pltpu.VMEM((length, 2, 2) + grad_mod.shape, BF16),
+            pltpu.VMEM((2, rows, width), F32),
+            pltpu.VMEM(payload, F32),
+            pltpu.VMEM(payload, F32),
+        ]
+        + small
+        + small
+        + [dma((2,)), dma((2,))],
         compiler_params=pltpu.CompilerParams(
             collective_id=1, has_side_effects=True, vmem_limit_bytes=62 * 1024 * 1024
         ),
         name="scatter_grads",
-    )(*lefts, *rights)
+    )(*lefts, *rights, *extras)
 
 
 def small_gather_kernel(length, sum_sections, own_ref, out_ref, other, *sems):
@@ -636,7 +774,7 @@
 
 
 TILE = 384
-DEPTH = 3
+DEPTH = 2
 GELU = math.sqrt(2.0 / math.pi)
 
 
@@ -646,9 +784,15 @@
     return pl.ds(pl.multiple_of(t * TILE, 128), TILE)
 
 
+def unit_of(t, width):
+    if isinstance(t, int):
+        return pl.ds(t * width, width)
+    return pl.ds(pl.multiple_of(t * width, 128), width)
+
+
 class Stream:
-    def __init__(self, wide, tall, sems, width):
-        self.wide, self.tall, self.sems, self.width = wide, tall, sems, width
+    def __init__(self, ring, sems, width):
+        self.ring, self.sems, self.width = ring, sems, width
         self.stages = []
 
     def add(self, weight, back, inner, outer):
@@ -657,12 +801,10 @@
     def tile(self, stage, n, k):
         weight, back, inner, _ = self.stages[stage]
         t = n * inner + k
-        slot = lax.rem(t, DEPTH) if not isinstance(t, int) else t % DEPTH
-        deep = pl.ds(pl.multiple_of(k * self.width, 128), self.width)
-        side = columns_of(n)
-        ring = self.tall if back else self.wide
+        slot = t % DEPTH if isinstance(t, int) else lax.rem(t, DEPTH)
+        deep, side = unit_of(k, self.width), unit_of(n, self.width)
         src = weight.at[side, deep] if back else weight.at[deep, side]
-        buffer = ring.at[stage % 2, slot]
+        buffer = self.ring.at[stage % 2, slot]
         return pltpu.make_async_copy(src, buffer, self.sems.at[stage % 2, slot]), buffer
 
     def begin(self, stage):
@@ -677,7 +819,7 @@
             self.begin(stage + 1)
         count = inner * outer
 
-        def body(n, carry):
+        def group(n):
             def product(k, left, back):
                 copy, buffer = self.tile(stage, n, k)
                 copy.wait()
@@ -687,13 +829,22 @@
                 def refill():
                     self.tile(stage, lax.div(t, inner), lax.rem(t, inner))[0].start()
 
-                when(t < count, refill)
+                if not isinstance(t, int):
+                    when(t < count, refill)
+                elif t < count:
+                    self.tile(stage, t // inner, t % inner)[0].start()
                 return result
 
             use(n, product)
+
+        def body(n, carry):
+            group(n)
             return carry
 
-        lax.fori_loop(0, outer, body, 0)
+        if outer == 1:
+            group(0)
+        else:
+            lax.fori_loop(0, outer, body, 0)
 
 
 def each_quarter(rows, run):
@@ -707,7 +858,7 @@
 def piece_of(mod_ref, q, p, width, columns=None):
     if columns is None:
         return mod_ref[q, :, p * width : (p + 1) * width]
-    return mod_ref[q, :, pl.ds(p * width + columns.start, columns.size)]
+    return mod_ref[q, :, pl.ds(p * width + columns.start, TILE)]
 
 
 def modulate(x_ref, mod_ref, out_ref, first, quarter_rows):
@@ -750,19 +901,27 @@
 def forward_stages(stream, weights):
     width = weights[0].shape[0]
     qkv, proj, up, down = weights
-    stream.add(qkv, False, 1, qkv.shape[1] // TILE)
-    stream.add(proj, False, 1, width // TILE)
-    stream.add(up, False, 1, up.shape[1] // TILE)
-    stream.add(down, False, down.shape[0] // width, width // TILE)
+    stream.add(qkv, False, 1, qkv.shape[1] // width)
+    stream.add(proj, False, 1, 1)
+    stream.add(up, False, 1, up.shape[1] // width)
+    stream.add(down, False, down.shape[0] // width, 1)
 
 
 def backward_stages(stream, weights):
     width = weights[0].shape[0]
     qkv, proj, up, down = weights
-    stream.add(down, True, 1, down.shape[0] // TILE)
-    stream.add(up, True, up.shape[1] // width, width // TILE)
-    stream.add(proj, True, 1, width // TILE)
-    stream.add(qkv, True, qkv.shape[1] // width, width // TILE)
+    stream.add(down, True, 1, down.shape[0] // width)
+    stream.add(up, True, up.shape[1] // width, 1)
+    stream.add(proj, True, 1, 1)
+    stream.add(qkv, True, qkv.shape[1] // width, 1)
+
+
+def by_parts(quarter_rows, width, run):
+    def one(q, rows):
+        for t in range(width // TILE):
+            run(q, rows, slice(t * TILE, (t + 1) * TILE))
+
+    each_quarter(quarter_rows, one)
 
 
 def proj_tile(r, mod_ref, quarter_rows, columns, branch):
@@ -776,12 +935,16 @@
     split_quarters(quarter_rows, gated)
 
 
-def up_tile(r, columns, h):
+def gelu_parts(h):
     square = h * h
     t = jnp.tanh(h * (GELU + (GELU * 0.044715) * square))
     half = 0.5 + 0.5 * t
-    r["act"][:, columns] = (h * half).astype(BF16)
-    slope = half + (0.5 * h) * (1.0 - t * t) * (GELU + (3.0 * GELU * 0.044715) * square)
+    return h * half, half + (0.5 * h) * (1.0 - t * t) * (GELU + (3.0 * GELU * 0.044715) * square)
+
+
+def up_tile(r, columns, h):
+    act, slope = gelu_parts(h)
+    r["act"][:, columns] = act.astype(BF16)
     r["slope"][:, columns] = slope.astype(BF16)
 
 
@@ -796,13 +959,13 @@
     split_quarters(quarter_rows, gated)
 
 
-def run_forward(stream, r, mod_ref, segments, quarter_rows, finish_tile, done):
+def run_forward(stream, r, mod_ref, segments, quarter_rows, finish_part, done):
     width = r["x"].shape[1]
     total_rows = r["x"].shape[0]
     modulate(r["x"], mod_ref, r["a1"], 0, quarter_rows)
 
     def qkv(n, product):
-        r["qkv"][:, columns_of(n)] = product(0, r["a1"][...], False).astype(BF16)
+        r["qkv"][:, unit_of(n, width)] = product(0, r["a1"][...], False).astype(BF16)
 
     stream.run(0, qkv)
     done("a1")
@@ -814,27 +977,45 @@
     each_block(total_rows, mix)
 
     def proj(n, product):
-        proj_tile(r, mod_ref, quarter_rows, columns_of(n), product(0, r["att"][...], False))
+        r["acc"][...] = product(0, r["att"][...], False)
 
     stream.run(1, proj)
     done("att")
+
+    def gated(q, rows, columns):
+        branch = r["acc"][rows, columns]
+        r["branch"][rows, columns] = branch.astype(BF16)
+        gate = piece_of(mod_ref, q, 2, width, columns)
+        r["x2"][rows, columns] = r["x"][rows, columns] + gate * branch
+
+    by_parts(quarter_rows, width, gated)
     modulate(r["x2"], mod_ref, r["a2"], 3, quarter_rows)
 
     def up(n, product):
-        up_tile(r, columns_of(n), product(0, r["a2"][...], False))
+        r["acc"][...] = product(0, r["a2"][...], False)
+
+        def part(q, rows, columns):
+            into = pl.ds(pl.multiple_of(n * width + columns.start, 128), TILE)
+            act, slope = gelu_parts(r["acc"][rows, columns])
+            r["act"][rows, into] = act.astype(BF16)
+            r["slope"][rows, into] = slope.astype(BF16)
+
+        by_parts(quarter_rows, width, part)
 
     stream.run(2, up)
     done("a2")
 
     def down(n, product):
-        mlp = None
         for k in range(r["act"].shape[1] // width):
             part = product(k, r["act"][:, k * width : (k + 1) * width], False)
-            mlp = part if mlp is None else mlp + part
-        finish_tile(n, columns_of(n), mlp)
+            if k == 0:
+                r["acc"][...] = part
+            else:
+                r["acc"][...] += part
 
     stream.run(3, down)
     done("act")
+    by_parts(quarter_rows, width, lambda q, rows, columns: finish_part(q, rows, columns, r["acc"][rows, columns]))
 
 
 def run_backward(stream, first, r, mod_ref, segments, quarter_rows, grad_of, finish, done):
@@ -842,7 +1023,7 @@
     total_rows = r["x"].shape[0]
 
     def down(n, product):
-        columns = columns_of(n)
+        columns = unit_of(n, width)
         grad = product(0, r["dmlp"][...], True)
         r["slope"][:, columns] = (grad * r["slope"][:, columns].astype(F32)).astype(BF16)
 
@@ -851,11 +1032,12 @@
     done("slope")
 
     def up(n, product):
-        grad = None
         for k in range(r["slope"].shape[1] // width):
             part = product(k, r["slope"][:, k * width : (k + 1) * width], True)
-            grad = part if grad is None else grad + part
-        r["dx2"][:, columns_of(n)] = grad
+            if k == 0:
+                r["dx2"][...] = part
+            else:
+                r["dx2"][...] += part
 
     stream.run(first + 1, up)
 
@@ -874,7 +1056,7 @@
     each_quarter(quarter_rows, middle)
 
     def proj(n, product):
-        r["datt"][:, columns_of(n)] = product(0, r["dbranch"][...], True).astype(BF16)
+        r["datt"][...] = product(0, r["dbranch"][...], True).astype(BF16)
 
     stream.run(first + 2, proj)
     done("dbranch")
@@ -887,17 +1069,18 @@
     done("dqkv")
 
     def qkv(n, product):
-        grad = None
         for k in range(3):
             part = product(k, r["dqkv"][:, k * width : (k + 1) * width], True)
-            grad = part if grad is None else grad + part
-        r["da1"][:, columns_of(n)] = grad
+            if k == 0:
+                r["acc"][...] = part
+            else:
+                r["acc"][...] += part
 
     stream.run(first + 3, qkv, ahead=False)
 
     def outer(q, rows):
         scale = piece_of(mod_ref, q, 1, width)
-        grad, shift_grad, scale_grad = modulate_back(r["da1"][rows, :], r["x"][rows, :], scale)
+        grad, shift_grad, scale_grad = modulate_back(r["acc"][rows, :], r["x"][rows, :], scale)
         r["dmod"][q, :, :width] = shift_grad
         r["dmod"][q, :, width : 2 * width] = scale_grad
         finish(q, rows, grad + r["dx2"][rows, :])
@@ -931,13 +1114,13 @@
 
 def encode_kernel(names, tokens, kept_ref, mod_ref, row_ref, column_ref, wq, wp, wu, wd, *rest):
     outs, scratch = rest[: len(names)], rest[len(names) :]
-    r = dict(zip(names + ("total",), scratch[: len(names) + 1]))
-    loaded, wide, tall, stream_sems, sems = scratch[len(names) + 1 :]
+    r = dict(zip(names + ("total", "acc"), scratch[: len(names) + 2]))
+    loaded, ring, stream_sems, sems = scratch[len(names) + 2 :]
     width = loaded.shape[2]
     slot = loaded.shape[1]
 
     def work():
-        stream = Stream(wide, tall, stream_sems, width)
+        stream = Stream(ring, stream_sems, width)
         forward_stages(stream, (wq, wp, wu, wd))
         copies = Copies(sems)
         copies.start(tokens, loaded)
@@ -952,10 +1135,12 @@
         def done(name):
             copies.start(r[name], out_of[name].at[pl.ds(0, total_rows)])
 
-        def finish_tile(n, columns, mlp):
-            out_tile(r, mod_ref, total_rows // 8, columns, mlp)
-
-        run_forward(stream, r, mod_ref, (row_ref, column_ref), total_rows // 8, finish_tile, done)
+        def finish_part(q, rows, columns, mlp):
+            r["mlp"][rows, columns] = mlp.astype(BF16)
+            gate = piece_of(mod_ref, q, 5, width, columns)
+            r["out"][rows, columns] = (r["x2"][rows, columns] + gate * mlp).astype(BF16)
+
+        run_forward(stream, r, mod_ref, (row_ref, column_ref), total_rows // 8, finish_part, done)
         for name in ("x", "x2", "qkv", "branch", "slope", "mlp", "out"):
             done(name)
         copies.finish()
@@ -972,11 +1157,11 @@
     right_outs = dict(zip(rights, outs[4 : 4 + len(rights)]))
     dmod_out, decoded, back, mask_out = outs[4 + len(rights) :]
     r = dict(zip(names, scratch[: len(names)]))
-    got, wide, tall, stream_sems, sems = scratch[len(names) :]
+    got, ring, stream_sems, sems = scratch[len(names) :]
     width = got.shape[2]
 
     def work():
-        stream = Stream(wide, tall, stream_sems, width)
+        stream = Stream(ring, stream_sems, width)
         forward_stages(stream, (wq, wp, wu, wd))
         backward_stages(stream, (wq, wp, wu, wd))
         copies = Copies(sems)
@@ -997,21 +1182,17 @@
         def done(name):
             copies.start(r[name], out_of[name])
 
-        def finish_tile(n, columns, mlp):
-            def gated(q, rows):
-                gate = piece_of(mod_ref, q, 5, width, columns)
-                dy = r["dy"][rows, columns].astype(F32)
-                part = mlp[rows]
-                r["out"][rows, columns] = (r["x2"][rows, columns] + gate * part).astype(BF16)
-                r["dmlp"][rows, columns] = (gate * dy).astype(BF16)
-                r["dmod"][q, :, pl.ds(5 * width + columns.start, TILE)] = jnp.sum(
-                    dy * part, axis=0, keepdims=True
-                )
-
-            split_quarters(total_rows // 8, gated)
+        def finish_part(q, rows, columns, part):
+            gate = piece_of(mod_ref, q, 5, width, columns)
+            dy = r["dy"][rows, columns].astype(F32)
+            r["out"][rows, columns] = (r["x2"][rows, columns] + gate * part).astype(BF16)
+            r["dmlp"][rows, columns] = (gate * dy).astype(BF16)
+            r["dmod"][q, :, 5 * width + columns.start : 5 * width + columns.stop] = jnp.sum(
+                dy * part, axis=0, keepdims=True
+            )
 
         segments = (row_ref, column_ref)
-        run_forward(stream, r, mod_ref, segments, total_rows // 8, finish_tile, done)
+        run_forward(stream, r, mod_ref, segments, total_rows // 8, finish_part, done)
         copies.start(r["out"], decoded)
         r["mask"][...] = jnp.zeros_like(r["mask"])
 
@@ -1049,11 +1230,11 @@
     dmod_out, token_out = rest[len(rights) : len(rights) + 2]
     scratch = rest[len(rights) + 2 :]
     r = dict(zip(names, scratch[: len(names)]))
-    wide, tall, stream_sems, sems = scratch[len(names) :]
+    ring, stream_sems, sems = scratch[len(names) :]
     width = r["x"].shape[1]
 
     def work():
-        stream = Stream(wide, tall, stream_sems, width)
+        stream = Stream(ring, stream_sems, width)
         backward_stages(stream, (wq, wp, wu, wd))
         copies = Copies(sems)
         copies.start(received, r["dy"])
@@ -1101,14 +1282,12 @@
 LEFTS = ("a1", "att", "a2", "act")
 RIGHTS = ("dqkv", "dbranch", "dhid", "dmlp")
 SAVED = ("x", "x2", "qkv", "branch", "slope", "mlp")
-anywhere = pl.BlockSpec(memory_space=pl.ANY)
-in_vmem = pl.BlockSpec(memory_space=pltpu.VMEM)
 
 
 def buffer_shapes(rows, width, wide_width):
     full, broad = lambda t: ((rows, width), t), lambda n, t: ((rows, n), t)
     return {
-        "x": full(F32), "x2": full(F32), "dx2": full(F32), "da1": full(F32), "a1": full(BF16),
+        "x": full(F32), "x2": full(F32), "dx2": full(F32), "acc": full(F32), "a1": full(BF16),
         "att": full(BF16), "a2": full(BF16), "branch": full(BF16), "mlp": full(BF16), "out": full(BF16),
         "dy": full(BF16), "dmlp": full(BF16), "dbranch": full(BF16), "datt": full(BF16),
         "qkv": broad(3 * width, BF16), "dqkv": broad(3 * width, BF16), "act": broad(wide_width, BF16),
@@ -1118,15 +1297,9 @@
     }
 
 
-def rings(width, forward, backward):
+def rings(width):
     dma = pltpu.SemaphoreType.DMA
-    none = (2, 1, 8, 128)
-    return [
-        pltpu.VMEM((2, DEPTH, width, TILE) if forward else none, BF16),
-        pltpu.VMEM((2, DEPTH, TILE, width) if backward else none, BF16),
-        dma((2, DEPTH)),
-        dma((24,)),
-    ]
+    return [pltpu.VMEM((2, DEPTH, width, width), BF16), dma((2, DEPTH)), dma((24,))]
 
 
 def encode(tokens, kept, modulation, segments, weights, rows, all_rows):
@@ -1139,9 +1312,9 @@
         out_shape=outs,
         in_specs=[anywhere] + [in_vmem] * 4 + [anywhere] * 4,
         out_specs=[anywhere] * len(names),
-        scratch_shapes=[pltpu.VMEM(*shapes[n]) for n in names + ("total",)]
+        scratch_shapes=[pltpu.VMEM(*shapes[n]) for n in names + ("total", "acc")]
         + [pltpu.VMEM(tokens.shape, BF16)]
-        + rings(width, True, False),
+        + rings(width),
         compiler_params=pltpu.CompilerParams(vmem_limit_bytes=VMEM_BYTES),
         name="encode",
     )(tokens, kept, modulation, *segments, *weights)
@@ -1157,8 +1330,8 @@
         "mask", "free", "total",
     )
     scratch = [pltpu.VMEM(*shapes[n]) for n in names]
-    names += ("dx2", "da1")
-    scratch += [pltpu.VMEM(*shapes["dx2"]), pltpu.VMEM(*shapes["da1"])]
+    names += ("dx2", "acc")
+    scratch += [pltpu.VMEM(*shapes["dx2"]), pltpu.VMEM(*shapes["acc"])]
     outs = [jax.ShapeDtypeStruct(*shapes[n]) for n in LEFTS + RIGHTS + ("dmod", "out")]
     outs += [jax.ShapeDtypeStruct(received.shape, BF16), jax.ShapeDtypeStruct((1, width), F32)]
     results = pl.pallas_call(
@@ -1166,7 +1339,7 @@
         out_shape=outs,
         in_specs=[anywhere] * 2 + [in_vmem] * 5 + [anywhere] * 8,
         out_specs=[anywhere] * len(outs),
-        scratch_shapes=scratch + [pltpu.VMEM(received.shape, BF16)] + rings(width, True, True),
+        scratch_shapes=scratch + [pltpu.VMEM(received.shape, BF16)] + rings(width),
         input_output_aliases={11 + j: j for j in range(4)},
         compiler_params=pltpu.CompilerParams(vmem_limit_bytes=VMEM_BYTES),
         name="decode",
@@ -1178,7 +1351,7 @@
     width, wide_width = weights[0].shape[0], weights[2].shape[1]
     rows = received.shape[0]
     shapes = buffer_shapes(rows, width, wide_width)
-    names = SAVED + ("dy", "dmlp", "dbranch", "datt", "dqkv", "dmod", "dx2", "da1", "total", "tokens")
+    names = SAVED + ("dy", "dmlp", "dbranch", "datt", "dqkv", "dmod", "dx2", "acc", "total", "tokens")
     shapes["tokens"] = (token_shape, BF16)
     outs = [jax.ShapeDtypeStruct(x.shape, x.dtype) for x in tuple(rights) + (grad_mod,)]
     outs.append(jax.ShapeDtypeStruct(token_shape, BF16))
@@ -1188,7 +1361,7 @@
         out_shape=outs,
         in_specs=[anywhere] + [in_vmem] * 4 + [anywhere] * (4 + len(saved) + 5),
         out_specs=[anywhere] * len(outs),
-        scratch_shapes=[pltpu.VMEM(*shapes[n]) for n in names] + rings(width, False, True),
+        scratch_shapes=[pltpu.VMEM(*shapes[n]) for n in names] + rings(width),
         input_output_aliases={before + j: j for j in range(5)},
         compiler_params=pltpu.CompilerParams(vmem_limit_bytes=VMEM_BYTES),
         name="encode_back",
@@ -1519,39 +1692,35 @@
         big[:, :, None], jnp.where(first_only, jnp.sum(grad_mod, axis=1, keepdims=True), 0.0), grad_mod
     )
     grad_mod = grad_mod.reshape(images, 6 * width).astype(BF16)
-    every_mod = lax.all_gather(grad_mod, "dp", axis=0, tiled=True)
-    ada_grad = dot_rows(lifted, every_mod)
-    bias_grad = jnp.sum(
-        lax.dynamic_slice_in_dim(every_mod, me * bias_width, bias_width, axis=1).astype(F32), axis=0
-    )
-    grad_lifted = dot_back(every_mod, ada)
-    _, pull = jax.vjp(jax.nn.silu, cond)
-    grad_cond = pull(grad_lifted)[0]
-    mask_rows = mask_part.reshape(-1, devices * images) if length == 4 else None
+    silu_slope = jax.vjp(jax.nn.silu, cond)[1](jnp.ones_like(cond))[0]
+    shapes = tuple(x.shape for x in shards) + ((lead, own_width, width),)
+    every_image = devices * images
     if length == 4:
-        payload = jnp.concatenate([grad_cond.T, mask_rows])
-        extra = -payload.shape[0] % 8
-        payload = small_gather(jnp.pad(payload, ((0, extra), (0, 0))), length, True, 3)
-        every_cond = payload[:, :own_width].reshape(width, devices * images)
-        mask_grad = jnp.sum(payload[:, own_width : own_width + mask_rows.shape[0]], axis=0).reshape(width)
+        mask_rows = mask_part.reshape(-1, every_image)
+        extras = (grad_mod, lifted.T, silu_slope.T, ada, mask_rows)
+        plan = plan_of(widths, lead, width, (0, 6))
+        *mine, ada_grad, bias_sum, shared = scatter_all(lefts, rights, extras, shapes, plan, length)
+        shared = shared.reshape(devices, -1, every_image)
+        every_cond = shared[:, :own_width].reshape(width, every_image)
+        mask_grad = jnp.sum(shared[:, own_width : own_width + mask_rows.shape[0]], axis=0).reshape(width)
+        bias_grad = lax.dynamic_slice_in_dim(bias_sum, me * bias_width, bias_width, axis=1)
     else:
+        every_mod = lax.all_gather(grad_mod, "dp", axis=0, tiled=True)
+        ada_grad = dot_rows(lifted, every_mod)
+        bias_sum = jnp.sum(every_mod.astype(F32), axis=0, keepdims=True)
+        bias_grad = lax.dynamic_slice_in_dim(bias_sum, me * bias_width, bias_width, axis=1)
+        grad_cond = dot_back(every_mod, ada) * silu_slope
         every_cond = lax.psum(lax.all_gather(grad_cond.T, "dp", axis=0, tiled=True), "section")
         mask_grad = lax.psum(mask_part, ("section", "dp"))
-    inputs = jnp.concatenate([embedding, onehot], axis=1)
-    shared = lax.dot_general(
-        inputs, every_cond.astype(BF16), (((0,), (1,)), ((), ())), preferred_element_type=F32
-    )
-    time_grad, table_grad = shared[: time_weight.shape[0]], shared[time_weight.shape[0] :]
-
-    shapes = tuple(x.shape for x in shards) + ((lead, own_width, width),)
-    half_rows = jnp.arange(dec_rows)[:, None] < jnp.where(section == 0, enc_rows, dec_rows)
-    if length == 4:
-        plan = plan_of(widths, lead, width, (0, 6))
-        mine = scatter_all(lefts, rights, shapes, plan, length)
-    else:
+        half_rows = jnp.arange(dec_rows)[:, None] < jnp.where(section == 0, enc_rows, dec_rows)
         lefts, rights = ([jnp.where(half_rows, x, jnp.zeros_like(x)) for x in xs] for xs in (lefts, rights))
         split = (dot_rows(x, y).astype(BF16).reshape((devices,) + s) for x, y, s in zip(lefts, rights, shapes))
         mine = tuple(lax.psum_scatter(g, "dp", scatter_dimension=0) for g in split)
+    inputs = jnp.concatenate([embedding, onehot], axis=1)
+    shared_grad = lax.dot_general(
+        inputs, every_cond.astype(BF16), (((0,), (1,)), ((), ())), preferred_element_type=F32
+    )
+    time_grad, table_grad = shared_grad[: time_weight.shape[0]], shared_grad[time_weight.shape[0] :]
     qkv_grad, proj_grad, up_grad, down_grad = (g.astype(F32) for g in mine)
     return (
         decoded_half,
@@ -1560,7 +1729,7 @@
         time_grad,
         table_grad,
         ada_grad[None],
-        bias_grad[None],
+        bias_grad,
         qkv_grad[None],
         proj_grad[None],
         up_grad[None],

time: 658 us -> 620 us (0.942)
  Pallas kernels: 473 us -> 457 us
  between operations: 14.5 us -> 1.38 us
  starting transfers between devices: 102 us -> 92.2 us
    pallas_call x2 -> x1, Pallas kernels: 30.1 us -> 12.7 us  [small_gather(): pl.pallas_call(functools.partial(small_gather_kernel, length, sum_section...]
    pallas_call x1, Pallas kernels: 197 us -> 209 us  [scatter_all(): pl.pallas_call(functools.partial(scatter_kernel, length, plan, slots, pai...]
    ppermute x2, starting transfers between devices: 102 us -> 92.2 us  [swap_sections(): return lax.ppermute(x, 'section', [(0, 1), (1, 0)])]
  transfers between devices with their start and end apart: 3 -> 2, of which waited for: 1 -> 2; matrix products, arithmetic and copies ran while one was open for 2% -> 1% of each run, Pallas kernels for 30% -> 0%
where the time goes in v4:
time: 620 us; the launch traced here: 611 us
  Pallas kernels  457 us (74%)
  starting transfers between devices  92.2 us (15%)
  local copies, waits for them, and re-layouts  22.2 us (4%)
  waiting for transfers between devices  18.2 us (3%)
  other arithmetic  14.2 us (2%)
    pallas_call x1, Pallas kernels, scatter_all(): pl.pallas_call(functools.partial(scatter_kernel, length, plan, slots, pai...  209 us
    pallas_call x1, Pallas kernels, gather_encode(): pl.pallas_call(functools.partial(gather_encode_kernel, length, plan, name...  193 us
    ppermute x2, starting transfers between devices, swap_sections(): return lax.ppermute(x, 'section', [(0, 1), (1, 0)])  92.2 us
    pallas_call x1, Pallas kernels, encode_back(): pl.pallas_call(functools.partial(encode_back_kernel, names, RIGHTS, SAVED...  37.4 us
    ppermute x2, waiting for transfers between devices, swap_sections(): return lax.ppermute(x, 'section', [(0, 1), (1, 0)])  18.2 us
    pallas_call x1, Pallas kernels, small_gather(): pl.pallas_call(functools.partial(small_gather_kernel, length, sum_section...  12.7 us
  transfers between devices with their start and end apart: 2, of which 2 were waited for; matrix products, arithmetic and copies ran while one was open for 1% of the time, Pallas kernels for 0%

profile of v4, /device:TPU:0, one launch (start us, length us, event | category | flops | bytes accessed | tf_op | source)
XLA Modules:
  0.0 611.5 jit_solution(11135855582130351777)
XLA Ops:
  0.7 0.1 slice_reduce_fusion.1
  0.8 0.1 reshape.162
  0.9 0.7 compare_bitcast_fusion
  1.5 0.1 broadcast_in_dim.107
  1.6 0.1 broadcast_in_dim.108
  1.7 0.1 broadcast_in_dim.110
  1.8 0.1 broadcast_in_dim.111
  1.9 0.1 broadcast_in_dim.112
  1.9 0.8 reshape_reshape.22.refs_8_.row_ref
  2.7 0.6 reshape_reshape.18.refs_9_.column_ref
  3.4 0.1 broadcast_select_fusion.1
  3.5 0.8 reshape.155
  4.2 0.8 reshape.156
  5.0 0.6 pad.4.own_ref
  5.6 12.7 %small_gather.1 = s32[4,2,2,8,128]{4,3,2,1,0:T(8,128)} custom-call(s32[8,128]{1,0:T(8,128)} %pad.4.own_ref), custom_call_target="tpu_custom_call" | custom-call | tf_op jit(solution)/shard_map/small_gather/pallas_call | solution.py:687
  18.3 0.9 fusion.26
  19.3 0.1 convert_element_type.47
  19.4 0.1 eq.31
  19.5 0.7 add.45
  20.2 0.1 broadcast_in_dim.106
  20.2 0.7 convert_element_type.55.refs_5_
  21.0 0.9 reshape_reshape.21.row_ref
  21.9 0.1 broadcast_in_dim.114
  21.9 0.7 broadcast_in_dim.115.column_ref
  22.6 1.3 reshape.165.mask_ref
  23.9 0.3 fusion.12
  24.2 2.8 fusion.3
  27.0 0.4 fusion.14
  27.4 0.7 fusion.20
  28.0 0.2 dynamic_update_slice.4
  28.3 1.9 fusion.1
  30.2 192.9 %gather_encode.1 = (bf16[4,2,2,72,3456]{4,3,2,1,0:T(8,128)(2,1)}, bf16[4,2,2,72,1152]{4,3,2,1,0:T(8,128)(2,1)}, bf16[4,2,2,72,4608]{4,3,2,1,0:T(8,128)(2,1)}, bf...) custom-call(bf16[72,3456]{1,0:T(8,128)(2,1)} %bitcast.79, ...), custom_call_target="tpu_custom_call" | custom-call | tf_op jit(solution)/shard_map/gather_encode/pallas_call | solution.py:1562
  223.1 5.3 decode.1
  228.5 92.1 %collective-permute-start = (bf16[2,128,1152]{2,1,0:T(8,128)(2,1)}, bf16[2,128,1152]{2,1,0:T(8,128)(2,1)S(1)}, u32[]{:S(2)}, u32[]{:S(2)}) collective-permute-start(bf16[2,128,1152]{2,1,0:T(8,128)(2,1)} %get-tuple-element.62), channel_id=1, source_target_pairs={{0,16},{16,0},{1,17},{17,1},{2,18},{18,2},{3,19},{19,3},{4,20},{20... | collective-permute-start | bytes 1769480 | tf_op jit(solution)/shard_map/ppermute | solution.py:1597
  320.6 0.1 broadcast_in_dim.118
  320.7 0.6 fusion.21
  321.3 0.1 fusion.2
  321.5 13.0 %collective-permute-done = bf16[2,128,1152]{2,1,0:T(8,128)(2,1)S(1)} collective-permute-done((bf16[2,128,1152]{2,1,0:T(8,128)(2,1)}, bf16[2,128,1152]{2,1,0:T(8,128)(2,1)S(1)}, u32[]{:S(2)}, u32[]{:S(2)}) %collective-permute-start) | collective-permute-done | bytes 589856 | tf_op jit(solution)/shard_map/ppermute | solution.py:1597
  334.4 0.8 copy-done.7
  335.2 37.4 %encode_back.1 = (bf16[512,3456]{1,0:T(8,128)(2,1)}, bf16[512,1152]{1,0:T(8,128)(2,1)}, bf16[512,4608]{1,0:T(8,128)(2,1)}, bf16[512,1152]{1,0:T(8,128)(2,1)}, f3...) custom-call(bf16[256,1152]{1,0:T(8,128)(2,1)} %bitcast.77, ...), custom_call_target="tpu_custom_call", output_to_operand_aliasing={{0}: (15, {}), {1}: (16, {}), {2}: (17, {}), {3}: (18, {}),... | custom-call | tf_op jit(solution)/shard_map/encode_back/pallas_call | solution.py:1359
  372.7 1.5 reduce.1
  374.2 0.1 fusion
  374.4 0.7 fusion.11.refs_8_
  375.1 208.7 %scatter_grads.1 = (bf16[72,3456]{1,0:T(8,128)(2,1)}, bf16[72,1152]{1,0:T(8,128)(2,1)}, bf16[72,4608]{1,0:T(8,128)(2,1)}, bf16[4,72,1152]{2,1,0:T(8,128)(2,1)}, ...) custom-call(bf16[512,1152]{1,0:T(8,128)(2,1)} %get-tuple-element.76.refs_0_, ...), custom_call_target="tpu_custom_call" | custom-call | tf_op jit(solution)/shard_map/scatter_grads/pallas_call | solution.py:599
  583.9 1.2 slice.62
  585.1 1.5 slice_reduce_fusion
  586.6 2.4 bitcast_convert_fusion.1
  589.0 1.0 bitcast_convert_fusion.2
  590.0 0.7 bitcast_convert_fusion.3
  590.8 0.3 slice_select_fusion.1
  591.0 0.2 copy.54
  591.3 0.1 collective-permute-start.1
  591.4 1.1 fusion.4
  592.4 1.3 constant_dynamic-slice_fusion
  593.8 2.4 slice.54
  596.2 1.1 slice.53
  597.3 0.3 copy-done.6
  597.6 1.1 bitcast_convert_fusion
  598.7 5.3 collective-permute-done.1
  604.0 0.3 copy.55
  604.3 1.6 slice_select_fusion.2
  605.8 1.1 copy.57
  606.9 1.1 copy.58
  608.0 3.0 copy.75
  (31 shorter events, 0.3 us)
Async XLA Ops:
  0.6 26.4 %copy-start = (bf16[256,1152]{1,0:T(8,128)(2,1)S(1)}, bf16[256,1152]{1,0:T(8,128)(2,1)}, u32[]{:S(2)}) copy-start(bf16[256,1152]{1,0:T(8,128)(2,1)} %param.22) | copy-start | bytes 1769476
  24.2 4.1 copy-start.2
  28.0 195.1 %copy-start.9 = (bf16[128,72]{0,1:T(8,128)(2,1)}, bf16[128,72]{0,1:T(8,128)(2,1)S(1)}, u32[]{:S(2)}) copy-start(bf16[128,72]{0,1:T(8,128)(2,1)S(1)} %get-tuple-element.127) | copy-start | bytes 55300
  228.5 106.0 %collective-permute-start = (bf16[2,128,1152]{2,1,0:T(8,128)(2,1)}, bf16[2,128,1152]{2,1,0:T(8,128)(2,1)S(1)}, u32[]{:S(2)}, u32[]{:S(2)}) collective-permute-start(bf16[2,128,1152]{2,1,0:T(8,128)(2,1)} %get-tuple-element.62), channel_id=1, source_target_pairs={{0,16},{16,0},{1,17},{17,1},{2,18},{18,2},{3,19},{19,3},{4,20},{20... | collective-permute-start | bytes 1769480 | tf_op jit(solution)/shard_map/ppermute | solution.py:1597
  334.4 0.8 copy-start.7
  372.6 1.8 copy-start.3
  583.9 5.1 copy-start.8
  586.6 3.4 copy-start.10
  586.6 4.2 copy-start.4
  586.6 4.2 copy-start.5
  591.3 12.7 %collective-permute-start.1 = (bf16[2,256,576]{1,2,0:T(8,128)(2,1)S(1)}, bf16[2,256,576]{1,2,0:T(8,128)(2,1)S(1)}, u32[]{:S(2)}, u32[]{:S(2)}) collective-permute-start(bf16[2,256,576]{1,2,0:T(8,128)(2,1)S(1)} %copy.54), channel_id=1, source_target_pairs={{0,16},{16,0},{1,17},{17,1},{2,18},{18,2},{3,19},{19,3},{4,20},{20... | collective-permute-start | bytes 1769480 | tf_op jit(solution)/shard_map/ppermute | solution.py:1597
  596.2 1.4 copy-start.6
  608.0 3.0 copy-start.1

commit v5 on v4

--- a/solution.py
+++ b/solution.py
@@ -1,5 +1,6 @@
 import functools
 import math
+from types import SimpleNamespace
 
 import jax
 import jax.numpy as jnp
@@ -317,19 +318,24 @@
 
 def scatter_kernel(length, plan, slots, pair_slots, *refs):
     lefts, rights = refs[:4], refs[4:8]
-    extras = refs[8:13]
-    outs = refs[13:17]
-    extra_outs = refs[17:20]
+    extras, outgoing = refs[8:13], refs[13]
+    outs = refs[14:18]
+    extra_outs, incoming = refs[18:21], refs[21]
     (
         raw, right, left_t, held, sent, core_in, pair_in, pair_late, up_in, down_in,
-    ) = refs[20:30]
+    ) = refs[22:32]
     (
         raw_sem, right_sem, core_s, core_r, pair_s, pair_r, up_s, up_r, down_s, down_r, out_sem,
         core_credit, pair_credit,
-    ) = refs[30:43]
+    ) = refs[32:45]
     a, b, c = position()
     greet_all(length, a, b, c)
-    side_steps = conditioning_steps(length, extras, extra_outs, refs[43:], a, b, c)
+    side_steps = conditioning_steps(length, extras, extra_outs, refs[45:-1], a, b, c)
+    swap_sem = refs[-1]
+    swap = remote(
+        outgoing, incoming, swap_sem.at[0], swap_sem.at[1], {"section": 1 - lax.axis_index("section")}
+    )
+    swap.start()
     n = len(plan)
     rows, width = held.shape[3:]
     total_rows = raw.shape[1]
@@ -565,6 +571,7 @@
         if 0 <= t - 2 - length < n:
             finish_late(t - 2 - length)
     side_steps[-1]()
+    swap.wait()
     for i in range(n):
         if i >= n - slots:
             to_core(i).wait_send()
@@ -582,7 +589,7 @@
                 when(a == here, gone)
 
 
-def scatter_all(lefts, rights, extras, shard_shapes, plan, length):
+def scatter_all(lefts, rights, extras, outgoing, shard_shapes, plan, length):
     n = len(plan)
     slots, pair_slots = 2, 4
     total_rows = lefts[0].shape[0]
@@ -603,9 +610,10 @@
             jax.ShapeDtypeStruct(ada.shape, F32),
             jax.ShapeDtypeStruct((1, ada.shape[1]), F32),
             jax.ShapeDtypeStruct((length, 2, 2) + payload, F32),
+            jax.ShapeDtypeStruct(outgoing.shape, BF16),
         ),
-        in_specs=[anywhere] * 8 + [in_vmem] * 5,
-        out_specs=[anywhere] * 5 + [in_vmem] * 2,
+        in_specs=[anywhere] * 8 + [in_vmem] * 5 + [anywhere],
+        out_specs=[anywhere] * 5 + [in_vmem] * 2 + [anywhere],
         scratch_shapes=[
             pltpu.VMEM((2, total_rows, width), BF16),
             pltpu.VMEM((2, total_rows, width), BF16),
@@ -627,12 +635,12 @@
         ]
         + small
         + small
-        + [dma((2,)), dma((2,))],
+        + [dma((2,)), dma((2,)), dma((2,))],
         compiler_params=pltpu.CompilerParams(
             collective_id=1, has_side_effects=True, vmem_limit_bytes=62 * 1024 * 1024
         ),
         name="scatter_grads",
-    )(*lefts, *rights, *extras)
+    )(*lefts, *rights, *extras, outgoing)
 
 
 def small_gather_kernel(length, sum_sections, own_ref, out_ref, other, *sems):
@@ -726,33 +734,33 @@
     return weights * (1.0 / jnp.sum(weights, axis=-1, keepdims=True))
 
 
-def attend(qkv_ref, rows, allowed, total, out_ref):
-    width = out_ref.shape[1]
-    total[:, :width] = jnp.zeros((total.shape[0], width), F32)
+def place(out_ref, rows, start, inside, value):
+    window = slice(start, start + value.shape[1])
+    out_ref[rows, window] = jnp.where(inside, value.astype(BF16), out_ref[rows, window])
+
+
+def attend(qkv_ref, rows, allowed, out_ref):
     for h in range(HEADS):
         inside, window, (query, key, value) = head_operands(qkv_ref, rows, h)
         probs = softmax_of(only(inside, query), key, allowed).astype(BF16)
-        mixed = contract(probs, value, ((1,), (0,)))
-        total[:, window] += only(inside, mixed)
-    out_ref[rows, :] = total[:, :width].astype(BF16)
-
-
-def attend_back(qkv_ref, grad_ref, rows, allowed, total, out_ref):
+        place(out_ref, rows, window.start, inside, contract(probs, value, ((1,), (0,))))
+
+
+def attend_back(qkv_ref, grad_ref, rows, allowed, out_ref):
     width = grad_ref.shape[1]
-    total[...] = jnp.zeros_like(total)
     for h in range(HEADS):
         inside, window, (query, key, value) = head_operands(qkv_ref, rows, h)
-        query, key = only(inside, query), only(inside, key)
-        grad = only(inside, grad_ref[rows, window])
-        probs = softmax_of(query, key, allowed)
-        grad_probs = contract(grad, value, ((1,), (1,)))
-        centre = jnp.sum(probs * grad_probs, axis=-1, keepdims=True)
+        query, grad = only(inside, query), only(inside, grad_ref[rows, window])
+        scores = jnp.where(allowed, contract(key, query, ((1,), (1,))) * HD**-0.5, MASKED)
+        weights = jnp.exp(scores - jnp.max(scores, axis=0, keepdims=True))
+        probs = weights * (1.0 / jnp.sum(weights, axis=0, keepdims=True))
+        grad_probs = contract(value, grad, ((1,), (1,)))
+        centre = jnp.sum(probs * grad_probs, axis=0, keepdims=True)
         grad_scores = (probs * (grad_probs - centre)).astype(BF16)
-        start, stop = window.start, window.stop
-        total[:, start:stop] += contract(grad_scores, key, ((1,), (0,))) * HD**-0.5
-        total[:, width + start : width + stop] += contract(grad_scores, query, ((0,), (0,))) * HD**-0.5
-        total[:, 2 * width + start : 2 * width + stop] += contract(probs.astype(BF16), grad, ((0,), (0,)))
-    out_ref[rows, :] = total[...].astype(BF16)
+        start = window.start
+        place(out_ref, rows, 2 * width + start, inside, contract(probs.astype(BF16), grad, ((1,), (0,))))
+        place(out_ref, rows, width + start, inside, contract(grad_scores, query, ((1,), (0,))) * HD**-0.5)
+        place(out_ref, rows, start, inside, contract(grad_scores, key, ((0,), (0,))) * HD**-0.5)
 
 
 def dot(x, y):
@@ -925,12 +933,12 @@
 
 
 def proj_tile(r, mod_ref, quarter_rows, columns, branch):
-    width = r["x"].shape[1]
-    r["branch"][:, columns] = branch.astype(BF16)
+    width = r.x.shape[1]
+    r.branch[:, columns] = branch.astype(BF16)
 
     def gated(q, rows):
         gate = piece_of(mod_ref, q, 2, width, columns)
-        r["x2"][rows, columns] = r["x"][rows, columns] + gate * branch[rows]
+        r.x2[rows, columns] = r.x[rows, columns] + gate * branch[rows]
 
     split_quarters(quarter_rows, gated)
 
@@ -944,61 +952,61 @@
 
 def up_tile(r, columns, h):
     act, slope = gelu_parts(h)
-    r["act"][:, columns] = act.astype(BF16)
-    r["slope"][:, columns] = slope.astype(BF16)
+    r.act[:, columns] = act.astype(BF16)
+    r.slope[:, columns] = slope.astype(BF16)
 
 
 def out_tile(r, mod_ref, quarter_rows, columns, mlp):
-    width = r["x"].shape[1]
-    r["mlp"][:, columns] = mlp.astype(BF16)
+    width = r.x.shape[1]
+    r.mlp[:, columns] = mlp.astype(BF16)
 
     def gated(q, rows):
         gate = piece_of(mod_ref, q, 5, width, columns)
-        r["out"][rows, columns] = (r["x2"][rows, columns] + gate * mlp[rows]).astype(BF16)
+        r.out[rows, columns] = (r.x2[rows, columns] + gate * mlp[rows]).astype(BF16)
 
     split_quarters(quarter_rows, gated)
 
 
 def run_forward(stream, r, mod_ref, segments, quarter_rows, finish_part, done):
-    width = r["x"].shape[1]
-    total_rows = r["x"].shape[0]
-    modulate(r["x"], mod_ref, r["a1"], 0, quarter_rows)
+    width = r.x.shape[1]
+    total_rows = r.x.shape[0]
+    modulate(r.x, mod_ref, r.a1, 0, quarter_rows)
 
     def qkv(n, product):
-        r["qkv"][:, unit_of(n, width)] = product(0, r["a1"][...], False).astype(BF16)
+        r.qkv[:, unit_of(n, width)] = product(0, r.a1[...], False).astype(BF16)
 
     stream.run(0, qkv)
     done("a1")
 
     def mix(block):
         rows, allowed = allowed_of(*segments, block)
-        attend(r["qkv"], rows, allowed, r["total"], r["att"])
+        attend(r.qkv, rows, allowed, r.att)
 
     each_block(total_rows, mix)
 
     def proj(n, product):
-        r["acc"][...] = product(0, r["att"][...], False)
+        r.acc[...] = product(0, r.att[...], False)
 
     stream.run(1, proj)
     done("att")
 
     def gated(q, rows, columns):
-        branch = r["acc"][rows, columns]
-        r["branch"][rows, columns] = branch.astype(BF16)
+        branch = r.acc[rows, columns]
+        r.branch[rows, columns] = branch.astype(BF16)
         gate = piece_of(mod_ref, q, 2, width, columns)
-        r["x2"][rows, columns] = r["x"][rows, columns] + gate * branch
+        r.x2[rows, columns] = r.x[rows, columns] + gate * branch
 
     by_parts(quarter_rows, width, gated)
-    modulate(r["x2"], mod_ref, r["a2"], 3, quarter_rows)
+    modulate(r.x2, mod_ref, r.a2, 3, quarter_rows)
 
     def up(n, product):
-        r["acc"][...] = product(0, r["a2"][...], False)
+        r.acc[...] = product(0, r.a2[...], False)
 
         def part(q, rows, columns):
             into = pl.ds(pl.multiple_of(n * width + columns.start, 128), TILE)
-            act, slope = gelu_parts(r["acc"][rows, columns])
-            r["act"][rows, into] = act.astype(BF16)
-            r["slope"][rows, into] = slope.astype(BF16)
+            act, slope = gelu_parts(r.acc[rows, columns])
+            r.act[rows, into] = act.astype(BF16)
+            r.slope[rows, into] = slope.astype(BF16)
 
         by_parts(quarter_rows, width, part)
 
@@ -1006,84 +1014,84 @@
     done("a2")
 
     def down(n, product):
-        for k in range(r["act"].shape[1] // width):
-            part = product(k, r["act"][:, k * width : (k + 1) * width], False)
+        for k in range(r.act.shape[1] // width):
+            part = product(k, r.act[:, k * width : (k + 1) * width], False)
             if k == 0:
-                r["acc"][...] = part
+                r.acc[...] = part
             else:
-                r["acc"][...] += part
+                r.acc[...] += part
 
     stream.run(3, down)
     done("act")
-    by_parts(quarter_rows, width, lambda q, rows, columns: finish_part(q, rows, columns, r["acc"][rows, columns]))
+    by_parts(quarter_rows, width, lambda q, rows, columns: finish_part(q, rows, columns, r.acc[rows, columns]))
 
 
 def run_backward(stream, first, r, mod_ref, segments, quarter_rows, grad_of, finish, done):
-    width = r["x"].shape[1]
-    total_rows = r["x"].shape[0]
+    width = r.x.shape[1]
+    total_rows = r.x.shape[0]
 
     def down(n, product):
         columns = unit_of(n, width)
-        grad = product(0, r["dmlp"][...], True)
-        r["slope"][:, columns] = (grad * r["slope"][:, columns].astype(F32)).astype(BF16)
+        grad = product(0, r.dmlp[...], True)
+        r.slope[:, columns] = (grad * r.slope[:, columns].astype(F32)).astype(BF16)
 
     stream.run(first, down)
     done("dmlp")
     done("slope")
 
     def up(n, product):
-        for k in range(r["slope"].shape[1] // width):
-            part = product(k, r["slope"][:, k * width : (k + 1) * width], True)
+        for k in range(r.slope.shape[1] // width):
+            part = product(k, r.slope[:, k * width : (k + 1) * width], True)
             if k == 0:
-                r["dx2"][...] = part
+                r.dx2[...] = part
             else:
-                r["dx2"][...] += part
+                r.dx2[...] += part
 
     stream.run(first + 1, up)
 
     def middle(q, rows):
         scale, gate = piece_of(mod_ref, q, 4, width), piece_of(mod_ref, q, 2, width)
-        grad, shift_grad, scale_grad = modulate_back(r["dx2"][rows, :], r["x2"][rows, :], scale)
+        grad, shift_grad, scale_grad = modulate_back(r.dx2[rows, :], r.x2[rows, :], scale)
         grad = grad + grad_of(rows)
-        r["dx2"][rows, :] = grad
-        r["dmod"][q, :, 3 * width : 4 * width] = shift_grad
-        r["dmod"][q, :, 4 * width : 5 * width] = scale_grad
-        r["dmod"][q, :, 2 * width : 3 * width] = jnp.sum(
-            grad * r["branch"][rows, :].astype(F32), axis=0, keepdims=True
+        r.dx2[rows, :] = grad
+        r.dmod[q, :, 3 * width : 4 * width] = shift_grad
+        r.dmod[q, :, 4 * width : 5 * width] = scale_grad
+        r.dmod[q, :, 2 * width : 3 * width] = jnp.sum(
+            grad * r.branch[rows, :].astype(F32), axis=0, keepdims=True
         )
-        r["dbranch"][rows, :] = (gate * grad).astype(BF16)
+        r.dbranch[rows, :] = (gate * grad).astype(BF16)
 
     each_quarter(quarter_rows, middle)
 
     def proj(n, product):
-        r["datt"][...] = product(0, r["dbranch"][...], True).astype(BF16)
+        r.datt[...] = product(0, r.dbranch[...], True).astype(BF16)
 
     stream.run(first + 2, proj)
     done("dbranch")
 
     def mix(block):
         rows, allowed = allowed_of(*segments, block)
-        attend_back(r["qkv"], r["datt"], rows, allowed, r["total"], r["dqkv"])
+        attend_back(r.qkv, r.datt, rows, allowed, r.dqkv)
 
     each_block(total_rows, mix)
     done("dqkv")
 
     def qkv(n, product):
         for k in range(3):
-            part = product(k, r["dqkv"][:, k * width : (k + 1) * width], True)
+            part = product(k, r.dqkv[:, k * width : (k + 1) * width], True)
             if k == 0:
-                r["acc"][...] = part
+                r.acc[...] = part
             else:
-                r["acc"][...] += part
+                r.acc[...] += part
 
     stream.run(first + 3, qkv, ahead=False)
 
     def outer(q, rows):
         scale = piece_of(mod_ref, q, 1, width)
-        grad, shift_grad, scale_grad = modulate_back(r["acc"][rows, :], r["x"][rows, :], scale)
-        r["dmod"][q, :, :width] = shift_grad
-        r["dmod"][q, :, width : 2 * width] = scale_grad
-        finish(q, rows, grad + r["dx2"][rows, :])
+        grad, shift_grad, scale_grad = modulate_back(r.acc[rows, :], r.x[rows, :], scale)
+        r.dmod[q, :, :width] = shift_grad
+        r.dmod[q, :, width : 2 * width] = scale_grad
+        finish(q, rows, grad + r.dx2[rows, :])
 
     each_quarter(quarter_rows, outer)
     done("dmod")
@@ -1114,8 +1122,8 @@
 
 def encode_kernel(names, tokens, kept_ref, mod_ref, row_ref, column_ref, wq, wp, wu, wd, *rest):
     outs, scratch = rest[: len(names)], rest[len(names) :]
-    r = dict(zip(names + ("total", "acc"), scratch[: len(names) + 2]))
-    loaded, ring, stream_sems, sems = scratch[len(names) + 2 :]
+    r = SimpleNamespace(**dict(zip(names + ("acc",), scratch[: len(names) + 1])))
+    loaded, ring, stream_sems, sems = scratch[len(names) + 1 :]
     width = loaded.shape[2]
     slot = loaded.shape[1]
 
@@ -1128,17 +1136,17 @@
         copies.finish()
         kept = kept_ref.shape[2]
         for m in range(2):
-            r["x"][m * kept : (m + 1) * kept, :] = dot_rows(placed(kept_ref, m, slot), loaded[m])
-        total_rows = r["x"].shape[0]
+            r.x[m * kept : (m + 1) * kept, :] = dot_rows(placed(kept_ref, m, slot), loaded[m])
+        total_rows = r.x.shape[0]
         out_of = dict(zip(names, outs))
 
         def done(name):
-            copies.start(r[name], out_of[name].at[pl.ds(0, total_rows)])
+            copies.start(getattr(r, name), out_of[name].at[pl.ds(0, total_rows)])
 
         def finish_part(q, rows, columns, mlp):
-            r["mlp"][rows, columns] = mlp.astype(BF16)
+            r.mlp[rows, columns] = mlp.astype(BF16)
             gate = piece_of(mod_ref, q, 5, width, columns)
-            r["out"][rows, columns] = (r["x2"][rows, columns] + gate * mlp).astype(BF16)
+            r.out[rows, columns] = (r.x2[rows, columns] + gate * mlp).astype(BF16)
 
         run_forward(stream, r, mod_ref, (row_ref, column_ref), total_rows // 8, finish_part, done)
         for name in ("x", "x2", "qkv", "branch", "slope", "mlp", "out"):
@@ -1156,7 +1164,7 @@
     lefts = dict(zip(("a1", "att", "a2", "act"), outs[:4]))
     right_outs = dict(zip(rights, outs[4 : 4 + len(rights)]))
     dmod_out, decoded, back, mask_out = outs[4 + len(rights) :]
-    r = dict(zip(names, scratch[: len(names)]))
+    r = SimpleNamespace(**dict(zip(names, scratch[: len(names)])))
     got, ring, stream_sems, sems = scratch[len(names) :]
     width = got.shape[2]
 
@@ -1166,46 +1174,46 @@
         backward_stages(stream, (wq, wp, wu, wd))
         copies = Copies(sems)
         copies.start(received, got)
-        copies.start(cotangent, r["dy"])
+        copies.start(cotangent, r.dy)
         stream.begin(0)
         copies.finish()
-        total_rows = r["x"].shape[0]
+        total_rows = r.x.shape[0]
         slot, kept = total_rows // 2, kept_ref.shape[2]
         for m in range(2):
             place = placed(kept_ref, m, slot)
             flags = jnp.sum(place.astype(F32), axis=1, keepdims=True)
-            r["free"][m * slot : (m + 1) * slot, :] = jnp.broadcast_to(1.0 - flags, (slot, 128))
+            r.free[m * slot : (m + 1) * slot, :] = jnp.broadcast_to(1.0 - flags, (slot, 128))
             filled = dot(place, got[m]) + (1.0 - flags) * mask_ref[...].astype(F32)
-            r["x"][m * slot : (m + 1) * slot, :] = filled
+            r.x[m * slot : (m + 1) * slot, :] = filled
         out_of = {**lefts, **right_outs, "dmod": dmod_out, "slope": right_outs["dhid"]}
 
         def done(name):
-            copies.start(r[name], out_of[name])
+            copies.start(getattr(r, name), out_of[name])
 
         def finish_part(q, rows, columns, part):
             gate = piece_of(mod_ref, q, 5, width, columns)
-            dy = r["dy"][rows, columns].astype(F32)
-            r["out"][rows, columns] = (r["x2"][rows, columns] + gate * part).astype(BF16)
-            r["dmlp"][rows, columns] = (gate * dy).astype(BF16)
-            r["dmod"][q, :, 5 * width + columns.start : 5 * width + columns.stop] = jnp.sum(
+            dy = r.dy[rows, columns].astype(F32)
+            r.out[rows, columns] = (r.x2[rows, columns] + gate * part).astype(BF16)
+            r.dmlp[rows, columns] = (gate * dy).astype(BF16)
+            r.dmod[q, :, 5 * width + columns.start : 5 * width + columns.stop] = jnp.sum(
                 dy * part, axis=0, keepdims=True
             )
 
         segments = (row_ref, column_ref)
         run_forward(stream, r, mod_ref, segments, total_rows // 8, finish_part, done)
-        copies.start(r["out"], decoded)
-        r["mask"][...] = jnp.zeros_like(r["mask"])
+        copies.start(r.out, decoded)
+        r.mask[...] = jnp.zeros_like(r.mask)
 
         def finish(q, rows, grad):
-            r["mask"][...] += jnp.sum(grad * r["free"][rows, :1], axis=0, keepdims=True)
-            r["dbranch"][rows, :] = grad.astype(BF16)
+            r.mask[...] += jnp.sum(grad * r.free[rows, :1], axis=0, keepdims=True)
+            r.dbranch[rows, :] = grad.astype(BF16)
 
         def grad_of(rows):
-            return r["dy"][rows, :].astype(F32)
+            return r.dy[rows, :].astype(F32)
 
         def done_back(name):
             if name == "dbranch":
-                copies.start(r[name], out_of[name]).wait()
+                copies.start(getattr(r, name), out_of[name]).wait()
                 copies.pending.pop()
             else:
                 done(name)
@@ -1213,9 +1221,9 @@
         run_backward(stream, 4, r, mod_ref, segments, total_rows // 8, grad_of, finish, done_back)
         for m in range(2):
             place = placed(kept_ref, m, slot)
-            got[m] = dot_rows(place, r["dbranch"][m * slot : (m + 1) * slot, :]).astype(BF16)
+            got[m] = dot_rows(place, r.dbranch[m * slot : (m + 1) * slot, :]).astype(BF16)
         copies.start(got, back)
-        copies.start(r["mask"], mask_out)
+        copies.start(r.mask, mask_out)
         copies.finish()
 
     when(lax.axis_index("section") == 1, work)
@@ -1229,41 +1237,41 @@
     right_outs = dict(zip(rights, rest[: len(rights)]))
     dmod_out, token_out = rest[len(rights) : len(rights) + 2]
     scratch = rest[len(rights) + 2 :]
-    r = dict(zip(names, scratch[: len(names)]))
+    r = SimpleNamespace(**dict(zip(names, scratch[: len(names)])))
     ring, stream_sems, sems = scratch[len(names) :]
-    width = r["x"].shape[1]
+    width = r.x.shape[1]
 
     def work():
         stream = Stream(ring, stream_sems, width)
         backward_stages(stream, (wq, wp, wu, wd))
         copies = Copies(sems)
-        copies.start(received, r["dy"])
+        copies.start(received, r.dy)
         for name in saved:
-            copies.start(kept_in[name], r[name])
+            copies.start(kept_in[name], getattr(r, name))
         stream.begin(0)
         copies.finish()
-        total_rows = r["x"].shape[0]
+        total_rows = r.x.shape[0]
         out_of = {**right_outs, "dmod": dmod_out, "slope": right_outs["dhid"]}
 
         def done(name):
             if name == "dmod":
-                copies.start(r[name], out_of[name])
+                copies.start(getattr(r, name), out_of[name])
             else:
-                copies.start(r[name], out_of[name].at[pl.ds(0, total_rows)])
+                copies.start(getattr(r, name), out_of[name].at[pl.ds(0, total_rows)])
 
         def start(q, rows):
             gate = piece_of(mod_ref, q, 5, width)
-            dy = r["dy"][rows, :].astype(F32)
-            r["dmlp"][rows, :] = (gate * dy).astype(BF16)
-            r["dmod"][q, :, 5 * width :] = jnp.sum(dy * r["mlp"][rows, :].astype(F32), axis=0, keepdims=True)
+            dy = r.dy[rows, :].astype(F32)
+            r.dmlp[rows, :] = (gate * dy).astype(BF16)
+            r.dmod[q, :, 5 * width :] = jnp.sum(dy * r.mlp[rows, :].astype(F32), axis=0, keepdims=True)
 
         each_quarter(total_rows // 8, start)
 
         def finish(q, rows, grad):
-            r["mlp"][rows, :] = grad.astype(BF16)
+            r.mlp[rows, :] = grad.astype(BF16)
 
         def grad_of(rows):
-            return r["dy"][rows, :].astype(F32)
+            return r.dy[rows, :].astype(F32)
 
         segments = (row_ref, column_ref)
         run_backward(stream, 0, r, mod_ref, segments, total_rows // 8, grad_of, finish, done)
@@ -1271,8 +1279,8 @@
         slot = token_out.shape[1]
         for m in range(2):
             place = placed(kept_ref, m, slot)
-            r["tokens"][m] = dot(place, r["mlp"][m * kept : (m + 1) * kept, :]).astype(BF16)
-        copies.start(r["tokens"], token_out)
+            r.tokens[m] = dot(place, r.mlp[m * kept : (m + 1) * kept, :]).astype(BF16)
+        copies.start(r.tokens, token_out)
         copies.finish()
 
     when(lax.axis_index("section") == 0, work)
@@ -1286,15 +1294,14 @@
 
 def buffer_shapes(rows, width, wide_width):
     full, broad = lambda t: ((rows, width), t), lambda n, t: ((rows, n), t)
-    return {
-        "x": full(F32), "x2": full(F32), "dx2": full(F32), "acc": full(F32), "a1": full(BF16),
-        "att": full(BF16), "a2": full(BF16), "branch": full(BF16), "mlp": full(BF16), "out": full(BF16),
-        "dy": full(BF16), "dmlp": full(BF16), "dbranch": full(BF16), "datt": full(BF16),
-        "qkv": broad(3 * width, BF16), "dqkv": broad(3 * width, BF16), "act": broad(wide_width, BF16),
-        "slope": broad(wide_width, BF16), "dhid": broad(wide_width, BF16),
-        "dmod": ((8, 1, 6 * width), F32), "mask": ((1, width), F32), "free": ((rows, 128), F32),
-        "total": ((ATT_ROWS, 3 * width), F32),
-    }
+    return dict(
+        x=full(F32), x2=full(F32), dx2=full(F32), acc=full(F32), a1=full(BF16),
+        att=full(BF16), a2=full(BF16), branch=full(BF16), mlp=full(BF16), out=full(BF16),
+        dy=full(BF16), dmlp=full(BF16), dbranch=full(BF16), datt=full(BF16),
+        qkv=broad(3 * width, BF16), dqkv=broad(3 * width, BF16), act=broad(wide_width, BF16),
+        slope=broad(wide_width, BF16), dhid=broad(wide_width, BF16),
+        dmod=((8, 1, 6 * width), F32), mask=((1, width), F32), free=((rows, 128), F32),
+    )
 
 
 def rings(width):
@@ -1312,7 +1319,7 @@
         out_shape=outs,
         in_specs=[anywhere] + [in_vmem] * 4 + [anywhere] * 4,
         out_specs=[anywhere] * len(names),
-        scratch_shapes=[pltpu.VMEM(*shapes[n]) for n in names + ("total", "acc")]
+        scratch_shapes=[pltpu.VMEM(*shapes[n]) for n in names + ("acc",)]
         + [pltpu.VMEM(tokens.shape, BF16)]
         + rings(width),
         compiler_params=pltpu.CompilerParams(vmem_limit_bytes=VMEM_BYTES),
@@ -1327,7 +1334,7 @@
     shapes = buffer_shapes(rows, width, wide_width)
     names = LEFTS + (
         "x", "x2", "qkv", "branch", "slope", "out", "dy", "dmlp", "dbranch", "datt", "dqkv", "dmod",
-        "mask", "free", "total",
+        "mask", "free",
     )
     scratch = [pltpu.VMEM(*shapes[n]) for n in names]
     names += ("dx2", "acc")
@@ -1351,7 +1358,7 @@
     width, wide_width = weights[0].shape[0], weights[2].shape[1]
     rows = received.shape[0]
     shapes = buffer_shapes(rows, width, wide_width)
-    names = SAVED + ("dy", "dmlp", "dbranch", "datt", "dqkv", "dmod", "dx2", "acc", "total", "tokens")
+    names = SAVED + ("dy", "dmlp", "dbranch", "datt", "dqkv", "dmod", "dx2", "acc", "tokens")
     shapes["tokens"] = (token_shape, BF16)
     outs = [jax.ShapeDtypeStruct(x.shape, x.dtype) for x in tuple(rights) + (grad_mod,)]
     outs.append(jax.ShapeDtypeStruct(token_shape, BF16))
@@ -1374,12 +1381,12 @@
     outs, (mod_out, received) = refs[10:14], refs[14:16]
     saved_outs = refs[16 : 16 + len(names)]
     rest = refs[16 + len(names) :]
-    r = dict(zip(names + ("out", "total"), rest[: len(names) + 2]))
+    r = SimpleNamespace(**dict(zip(names + ("out",), rest[: len(names) + 1])))
     (
         loaded, mod_ref, tiles, last_tile, part_held, part_core, part_pair, part_line,
-    ) = rest[len(names) + 2 : len(names) + 10]
-    sems = rest[len(names) + 10 : len(names) + 19]
-    part_sems, line_sems, tile_sems, out_sems, copy_sems = rest[len(names) + 19 :]
+    ) = rest[len(names) + 1 : len(names) + 9]
+    sems = rest[len(names) + 9 : len(names) + 18]
+    part_sems, line_sems, tile_sems, out_sems, copy_sems = rest[len(names) + 18 :]
     a, b, c = position()
     encoder = lax.axis_index("section") == 0
     other = {"section": 1 - lax.axis_index("section")}
@@ -1396,8 +1403,8 @@
     pl.semaphore_wait(barrier, length + 2)
 
     n = len(plan)
-    width = r["x"].shape[1]
-    total_rows = r["x"].shape[0]
+    width = r.x.shape[1]
+    total_rows = r.x.shape[0]
     quarter_rows = total_rows // 8
     issue, move, complete, drain = gather_moves(length, plan, sources, outs, sems, a, b, c)
     copies = Copies(copy_sems)
@@ -1451,13 +1458,13 @@
         for t in range(count):
             load_tile(w, low, t).wait()
             tile = tiles[t % 2].astype(F32).reshape(width, TILE).astype(BF16)
-            result = dot(r[left][...], tile)
+            result = dot(getattr(r, left)[...], tile)
             if t + 2 < count:
                 load_tile(w, low, t + 2).start()
             put(columns_of(low // TILE + t), result)
 
     def done(name):
-        copies.start(r[name], out_of[name].at[pl.ds(0, total_rows)])
+        copies.start(getattr(r, name), out_of[name].at[pl.ds(0, total_rows)])
 
     def start_encode():
         fetch = pltpu.make_async_copy(tokens, loaded, tile_sems.at[2])
@@ -1465,10 +1472,10 @@
         fetch.wait()
         kept, slot = kept_ref.shape[2], loaded.shape[1]
         for m in range(2):
-            r["x"][m * kept : (m + 1) * kept, :] = dot_rows(placed(kept_ref, m, slot), loaded[m])
+            r.x[m * kept : (m + 1) * kept, :] = dot_rows(placed(kept_ref, m, slot), loaded[m])
 
     def put_qkv(columns, result):
-        r["qkv"][:, columns] = result.astype(BF16)
+        r.qkv[:, columns] = result.astype(BF16)
 
     def put_proj(columns, result):
         proj_tile(r, mod_ref, quarter_rows, columns, result)
@@ -1479,20 +1486,20 @@
     def send_out(t):
         columns = columns_of(t)
         return remote(
-            r["out"].at[:, columns], received.at[:, columns], out_sems.at[0, t], out_sems.at[1, t], other
+            r.out.at[:, columns], received.at[:, columns], out_sems.at[0, t], out_sems.at[1, t], other
         )
 
     def encode_chunk(i):
         w, low, _, _ = plan[i]
         if w == 0:
             if i == 0:
-                modulate(r["x"], mod_ref, r["a1"], 0, quarter_rows)
+                modulate(r.x, mod_ref, r.a1, 0, quarter_rows)
             products(w, low, "a1", put_qkv)
         elif w == 1:
             rows, allowed = slice(0, total_rows), row_ref[...] == column_ref[0]
-            attend(r["qkv"], rows, allowed, r["total"], r["att"])
+            attend(r.qkv, rows, allowed, r.att)
             products(w, low, "att", put_proj)
-            modulate(r["x2"], mod_ref, r["a2"], 3, quarter_rows)
+            modulate(r.x2, mod_ref, r.a2, 3, quarter_rows)
         elif w == 2:
             products(w, low, "a2", put_up)
         else:
@@ -1500,8 +1507,8 @@
             fetch = pltpu.make_async_copy(src, last_tile, tile_sems.at[2])
             fetch.start()
             fetch.wait()
-            tile = last_tile[...].reshape(r["act"].shape[1], TILE)
-            out_tile(r, mod_ref, quarter_rows, columns_of(low // TILE), dot(r["act"][...], tile))
+            tile = last_tile[...].reshape(r.act.shape[1], TILE)
+            out_tile(r, mod_ref, quarter_rows, columns_of(low // TILE), dot(r.act[...], tile))
             send_out(low // TILE).start()
 
     part_load.start()
@@ -1564,7 +1571,7 @@
         out_shape=outs,
         in_specs=[anywhere] * 5 + [in_vmem, anywhere] + [in_vmem] * 3,
         out_specs=[anywhere] * len(outs),
-        scratch_shapes=[pltpu.VMEM(*shapes[m]) for m in names + ("out", "total")]
+        scratch_shapes=[pltpu.VMEM(*shapes[m]) for m in names + ("out",)]
         + [
             pltpu.VMEM(tokens.shape, BF16),
             pltpu.VMEM((quarters, 1, 6 * width), F32),
@@ -1682,9 +1689,6 @@
 
     half_width = width // 2
     outgoing = jnp.where(section == 0, token_grad[:, :, half_width:], decoded[:, :, :half_width])
-    incoming = swap_sections(outgoing)
-    decoded_half = jnp.where(section == 0, incoming, decoded[:, :, half_width:])
-    token_half = jnp.where(section == 0, token_grad[:, :, :half_width], incoming)
 
     grad_mod = grad_mod.reshape(micro, SMALL_PER, 6 * width)
     first_only = (jnp.arange(SMALL_PER) == 0)[None, :, None]
@@ -1699,12 +1703,15 @@
         mask_rows = mask_part.reshape(-1, every_image)
         extras = (grad_mod, lifted.T, silu_slope.T, ada, mask_rows)
         plan = plan_of(widths, lead, width, (0, 6))
-        *mine, ada_grad, bias_sum, shared = scatter_all(lefts, rights, extras, shapes, plan, length)
+        *mine, ada_grad, bias_sum, shared, incoming = scatter_all(
+            lefts, rights, extras, outgoing, shapes, plan, length
+        )
         shared = shared.reshape(devices, -1, every_image)
         every_cond = shared[:, :own_width].reshape(width, every_image)
         mask_grad = jnp.sum(shared[:, own_width : own_width + mask_rows.shape[0]], axis=0).reshape(width)
         bias_grad = lax.dynamic_slice_in_dim(bias_sum, me * bias_width, bias_width, axis=1)
     else:
+        incoming = swap_sections(outgoing)
         every_mod = lax.all_gather(grad_mod, "dp", axis=0, tiled=True)
         ada_grad = dot_rows(lifted, every_mod)
         bias_sum = jnp.sum(every_mod.astype(F32), axis=0, keepdims=True)
@@ -1716,11 +1723,13 @@
         lefts, rights = ([jnp.where(half_rows, x, jnp.zeros_like(x)) for x in xs] for xs in (lefts, rights))
         split = (dot_rows(x, y).astype(BF16).reshape((devices,) + s) for x, y, s in zip(lefts, rights, shapes))
         mine = tuple(lax.psum_scatter(g, "dp", scatter_dimension=0) for g in split)
-    inputs = jnp.concatenate([embedding, onehot], axis=1)
-    shared_grad = lax.dot_general(
-        inputs, every_cond.astype(BF16), (((0,), (1,)), ((), ())), preferred_element_type=F32
+    decoded_half = jnp.where(section == 0, incoming, decoded[:, :, half_width:])
+    token_half = jnp.where(section == 0, token_grad[:, :, :half_width], incoming)
+    every_cond = every_cond.astype(BF16)
+    time_grad, table_grad = (
+        lax.dot_general(x, every_cond, (((0,), (1,)), ((), ())), preferred_element_type=F32)
+        for x in (embedding, onehot)
     )
-    time_grad, table_grad = shared_grad[: time_weight.shape[0]], shared_grad[time_weight.shape[0] :]
     qkv_grad, proj_grad, up_grad, down_grad = (g.astype(F32) for g in mine)
     return (
         decoded_half,

time: 620 us -> 604 us (0.974)
    ppermute x2 -> x1, starting transfers between devices: 92.2 us -> 87 us  [swap_sections(): return lax.ppermute(x, 'section', [(0, 1), (1, 0)])]
    ppermute x2 -> x1, waiting for transfers between devices: 18.2 us -> 13.1 us  [swap_sections(): return lax.ppermute(x, 'section', [(0, 1), (1, 0)])]
  transfers between devices with their start and end apart: 2 -> 1, of which waited for: 2 -> 1; matrix products, arithmetic and copies ran while one was open for 1% -> 0% of each run, Pallas kernels for 0% -> 0%
where the time goes in v5:
time: 604 us; the launch traced here: 595 us
  Pallas kernels  454 us (75%)
  starting transfers between devices  87 us (14%)
  local copies, waits for them, and re-layouts  16.3 us (3%)
  other arithmetic  13.5 us (2%)
  waiting for transfers between devices  13.1 us (2%)
  matrix products  9.37 us (2%)
    pallas_call x1, Pallas kernels, scatter_all(): pl.pallas_call(functools.partial(scatter_kernel, length, plan, slots, pai...  208 us
    pallas_call x1, Pallas kernels, gather_encode(): pl.pallas_call(functools.partial(gather_encode_kernel, length, plan, name...  193 us
    ppermute x1, starting transfers between devices, swap_sections(): return lax.ppermute(x, 'section', [(0, 1), (1, 0)])  87 us
    pallas_call x1, Pallas kernels, encode_back(): pl.pallas_call(functools.partial(encode_back_kernel, names, RIGHTS, SAVED...  35.1 us
    ppermute x1, waiting for transfers between devices, swap_sections(): return lax.ppermute(x, 'section', [(0, 1), (1, 0)])  13.1 us
    pallas_call x1, Pallas kernels, small_gather(): pl.pallas_call(functools.partial(small_gather_kernel, length, sum_section...  12.7 us
  transfers between devices with their start and end apart: 1, of which 1 were waited for; matrix products, arithmetic and copies ran while one was open for 0% of the time, Pallas kernels for 0%

profile of v5, /device:TPU:0, one launch (start us, length us, event | category | flops | bytes accessed | tf_op | source)
XLA Modules:
  0.0 595.1 jit_solution(1447173172593038613)
XLA Ops:
  0.6 0.0 copy-start
  0.7 0.1 slice_reduce_fusion.1
  0.8 0.1 reshape.162
  0.9 0.7 compare_bitcast_fusion
  1.5 0.1 broadcast_in_dim.107
  1.6 0.1 broadcast_in_dim.108
  1.7 0.1 broadcast_in_dim.110
  1.8 0.1 broadcast_in_dim.111
  1.9 0.1 broadcast_in_dim.112
  1.9 0.8 reshape_reshape.22.refs_8_.row_ref
  2.7 0.7 reshape_reshape.18.refs_9_.column_ref
  3.4 0.1 broadcast_select_fusion.1
  3.5 0.8 reshape.155
  4.2 0.8 reshape.156
  5.0 0.6 pad.4.own_ref
  5.6 12.7 %small_gather.1 = s32[4,2,2,8,128]{4,3,2,1,0:T(8,128)} custom-call(s32[8,128]{1,0:T(8,128)} %pad.4.own_ref), custom_call_target="tpu_custom_call" | custom-call | tf_op jit(solution)/shard_map/small_gather/pallas_call | solution.py:695
  18.4 0.9 fusion.21
  19.3 0.1 convert_element_type.45
  19.4 0.1 eq.31
  19.5 0.7 add.45
  20.2 0.1 broadcast_in_dim.106
  20.2 0.7 convert_element_type.52.refs_5_
  20.9 0.1 broadcast_in_dim.113
  21.0 0.9 reshape_reshape.21.row_ref
  21.9 0.1 broadcast_in_dim.114
  22.0 0.7 broadcast_in_dim.115.column_ref
  22.6 1.3 reshape.165.mask_ref
  23.9 0.3 fusion.9
  24.2 2.7 fusion.3
  26.9 0.0 copy-start.2
  27.0 0.4 fusion.12
  27.3 0.6 fusion.15
  28.0 0.2 dynamic_update_slice.4
  28.2 1.9 fusion.1
  30.1 193.0 %gather_encode.1 = (bf16[4,2,2,72,3456]{4,3,2,1,0:T(8,128)(2,1)}, bf16[4,2,2,72,1152]{4,3,2,1,0:T(8,128)(2,1)}, bf16[4,2,2,72,4608]{4,3,2,1,0:T(8,128)(2,1)}, bf...) custom-call(bf16[72,3456]{1,0:T(8,128)(2,1)} %bitcast.81, ...), custom_call_target="tpu_custom_call" | custom-call | tf_op jit(solution)/shard_map/gather_encode/pallas_call | solution.py:1569
  223.0 5.3 decode.1
  228.3 87.0 %collective-permute-start = (bf16[2,128,1152]{2,1,0:T(8,128)(2,1)}, bf16[2,128,1152]{2,1,0:T(8,128)(2,1)S(1)}, u32[]{:S(2)}, u32[]{:S(2)}) collective-permute-start(bf16[2,128,1152]{2,1,0:T(8,128)(2,1)} %get-tuple-element.67), channel_id=1, source_target_pairs={{0,16},{16,0},{1,17},{17,1},{2,18},{18,2},{3,19},{19,3},{4,20},{20... | collective-permute-start | bytes 1769480 | tf_op jit(solution)/shard_map/ppermute | solution.py:1604
  315.4 0.1 broadcast_in_dim.118
  315.5 0.6 fusion.16
  316.1 13.1 %collective-permute-done = bf16[2,128,1152]{2,1,0:T(8,128)(2,1)S(1)} collective-permute-done((bf16[2,128,1152]{2,1,0:T(8,128)(2,1)}, bf16[2,128,1152]{2,1,0:T(8,128)(2,1)S(1)}, u32[]{:S(2)}, u32[]{:S(2)}) %collective-permute-start) | collective-permute-done | bytes 589856 | tf_op jit(solution)/shard_map/ppermute | solution.py:1604
  329.2 0.8 copy-done.10
  330.0 35.1 %encode_back.1 = (bf16[512,3456]{1,0:T(8,128)(2,1)}, bf16[512,1152]{1,0:T(8,128)(2,1)}, bf16[512,4608]{1,0:T(8,128)(2,1)}, bf16[512,1152]{1,0:T(8,128)(2,1)}, f3...) custom-call(bf16[256,1152]{1,0:T(8,128)(2,1)} %bitcast.79, ...), custom_call_target="tpu_custom_call", output_to_operand_aliasing={{0}: (15, {}), {1}: (16, {}), {2}: (17, {}), {3}: (18, {}),... | custom-call | tf_op jit(solution)/shard_map/encode_back/pallas_call | solution.py:1366
  365.1 0.0 copy-start.4
  365.1 0.0 copy-start.5
  365.1 1.6 reduce.1
  366.7 0.1 reshape.171
  366.8 0.1 fusion
  366.9 0.7 fusion.8.refs_8_
  367.7 2.2 slice_select_fusion.1.refs_13_
  369.8 208.4 %scatter_grads.1 = (bf16[72,3456]{1,0:T(8,128)(2,1)}, bf16[72,1152]{1,0:T(8,128)(2,1)}, bf16[72,4608]{1,0:T(8,128)(2,1)}, bf16[4,72,1152]{2,1,0:T(8,128)(2,1)}, ...) custom-call(bf16[512,1152]{1,0:T(8,128)(2,1)} %get-tuple-element.63.refs_0, ...), custom_call_target="tpu_custom_call" | custom-call | tf_op jit(solution)/shard_map/scatter_grads/pallas_call | solution.py:606
  578.3 1.1 slice.52
  579.4 3.1 fusion.4
  582.5 1.4 fusion.11
  583.8 1.5 slice_reduce_fusion
  585.4 0.3 slice_select_fusion.2
  585.7 1.1 copy.46
  586.7 1.1 copy.47
  587.8 1.1 bitcast_convert_fusion
  588.9 1.2 bitcast_convert_fusion.1
  590.1 1.0 bitcast_convert_fusion.2
  591.1 0.7 bitcast_convert_fusion.3
  591.9 1.3 constant_dynamic-slice_fusion
  593.2 1.3 copy.64
  594.5 0.2 copy-done.1
  (31 shorter events, 0.1 us)
Async XLA Ops:
  0.6 26.3 %copy-start = (bf16[256,1152]{1,0:T(8,128)(2,1)S(1)}, bf16[256,1152]{1,0:T(8,128)(2,1)}, u32[]{:S(2)}) copy-start(bf16[256,1152]{1,0:T(8,128)(2,1)} %param.22) | copy-start | bytes 1769476
  26.9 1.3 copy-start.2
  27.9 2.1 copy-start.12
  228.3 100.9 %collective-permute-start = (bf16[2,128,1152]{2,1,0:T(8,128)(2,1)}, bf16[2,128,1152]{2,1,0:T(8,128)(2,1)S(1)}, u32[]{:S(2)}, u32[]{:S(2)}) collective-permute-start(bf16[2,128,1152]{2,1,0:T(8,128)(2,1)} %get-tuple-element.67), channel_id=1, source_target_pairs={{0,16},{16,0},{1,17},{17,1},{2,18},{18,2},{3,19},{19,3},{4,20},{20... | collective-permute-start | bytes 1769480 | tf_op jit(solution)/shard_map/ppermute | solution.py:1604
  329.2 0.8 copy-start.10
  365.1 1.8 copy-start.4
  365.1 2.6 copy-start.5
  579.4 6.0 %copy-start.9 = (bf16[2,256,576]{2,1,0:T(8,128)(2,1)S(1)}, bf16[2,256,576]{2,1,0:T(8,128)(2,1)}, u32[]{:S(2)}) copy-start(bf16[2,256,576]{2,1,0:T(8,128)(2,1)} %get-tuple-element.87) | copy-start | bytes 1769476
  582.5 2.9 copy-start.6
  585.6 2.1 copy-start.8
  586.7 2.2 copy-start.7
  588.9 1.2 copy-start.11
  588.9 2.2 copy-start.13
  590.1 3.1 copy-start.3
  593.2 1.4 copy-start.1

commit v6 on v5

--- a/solution.py
+++ b/solution.py
@@ -205,6 +205,7 @@
 
 
 SIDE_TIMES = (2, 4, 5, 6, 8, 10)
+LAG, LINE_LAG = 1, (0, 1, 2, 3)
 
 
 def greet_all(length, a, b, c):
@@ -554,22 +555,24 @@
     right_load(0).start()
     raw_load(1).start()
     produce(0)
-    for t in range(n + length + 3):
+    for t in range(n + LAG + LINE_LAG[-1] + 1):
         if t in SIDE_TIMES:
             side_steps[SIDE_TIMES.index(t) + 1]()
         if t < n:
             first_add(t)
         if t + 1 < n:
             produce(t + 1)
-        if 0 <= t - 1 < n:
-            second_add(t - 1)
+        if 0 <= t - LAG < n:
+            second_add(t - LAG)
         for j in range(length):
-            if 0 <= t - 2 - j < n:
-                line_step(t - 2 - j, j)
-        if 0 <= t - 1 - length < n:
-            finish(t - 1 - length)
-        if 0 <= t - 2 - length < n:
-            finish_late(t - 2 - length)
+            i = t - LAG - LINE_LAG[j]
+            if 0 <= i < n:
+                line_step(i, j)
+        i = t - LAG - LINE_LAG[length - 1]
+        if 0 <= i < n:
+            finish(i)
+        if 0 <= i - 1 < n:
+            finish_late(i - 1)
     side_steps[-1]()
     swap.wait()
     for i in range(n):
@@ -643,66 +646,35 @@
     )(*lefts, *rights, *extras, outgoing)
 
 
-def small_gather_kernel(length, sum_sections, own_ref, out_ref, other, *sems):
-    line_s, line_r, pair_s, pair_r, core_s, core_r, side_s, side_r = sems
-    a, b, c = position()
-    partner = {"section": 1 - lax.axis_index("section")}
+def small_gather_kernel(devices, own_ref, out_ref, send, recv):
+    me = lax.axis_index("dp")
     barrier = pltpu.get_barrier_semaphore()
-
-    def tell(target):
-        pl.semaphore_signal(barrier, inc=1, device_id=target, device_id_type=MESH)
-
-    tell(at(a, 1 - b, c))
-    tell(at(a, b, 1 - c))
-    for k in range(1, length):
-        tell(at(lax.rem(a + k, length), b, c))
-    if sum_sections:
-        tell(partner)
-    pl.semaphore_wait(barrier, length + 1 + int(sum_sections))
-    value = own_ref[...]
-    if sum_sections:
-        side = remote(own_ref, other, side_s, side_r, partner)
-        side.start()
-        side.wait()
-        value = value + other[...]
-    out_ref[a, b, c] = value
-    mine = out_ref.at[a, b, c]
-    copies = []
-    for k in range(1, length):
-        to = lax.rem(a + k, length)
-        copy = remote(mine, mine, line_s.at[k - 1], line_r.at[k - 1], at(to, b, c))
+    ahead = [lax.rem(me + k, devices) for k in range(1, devices)]
+    for target in ahead:
+        pl.semaphore_signal(barrier, inc=1, device_id={"dp": target}, device_id_type=MESH)
+    pl.semaphore_wait(barrier, devices - 1)
+    out_ref[me] = own_ref[...]
+    mine = out_ref.at[me]
+    copies = [remote(mine, mine, send.at[k], recv.at[k], {"dp": to}) for k, to in enumerate(ahead)]
+    for copy in copies:
         copy.start()
-        copies.append(copy)
-    for k in range(1, length):
-        source = lax.rem(a + length - k, length)
-        slab = out_ref.at[source, b, c]
-        remote(slab, slab, line_s.at[k - 1], line_r.at[k - 1], at(a, 1 - b, c)).wait_recv()
-        copies[k - 1].wait_send()
-    for go, come, s, r, to in (
-        (out_ref.at[:, b, c], out_ref.at[:, 1 - b, c], pair_s, pair_r, at(a, 1 - b, c)),
-        (out_ref.at[:, :, c], out_ref.at[:, :, 1 - c], core_s, core_r, at(a, b, 1 - c)),
-    ):
-        copy = remote(go, go, s, r, to)
-        copy.start()
-        remote(come, come, s, r, to).wait_recv()
+    for k, copy in enumerate(copies):
+        slab = out_ref.at[lax.rem(me + devices - 1 - k, devices)]
+        remote(slab, slab, send.at[k], recv.at[k], {"dp": ahead[k]}).wait_recv()
         copy.wait_send()
 
 
-def small_gather(own, length, sum_sections, collective_id):
+def small_gather(own, devices, collective_id):
     dma = pltpu.SemaphoreType.DMA
-    vmem = pl.BlockSpec(memory_space=pltpu.VMEM)
-    shape = (length, 2, 2) + own.shape
     return pl.pallas_call(
-        functools.partial(small_gather_kernel, length, sum_sections),
-        out_shape=jax.ShapeDtypeStruct(shape, own.dtype),
-        in_specs=[vmem],
-        out_specs=vmem,
-        scratch_shapes=[
-            pltpu.VMEM(own.shape, own.dtype), dma((length - 1,)), dma((length - 1,)), dma, dma, dma, dma, dma, dma,
-        ],
+        functools.partial(small_gather_kernel, devices),
+        out_shape=jax.ShapeDtypeStruct((devices,) + own.shape, own.dtype),
+        in_specs=[in_vmem],
+        out_specs=in_vmem,
+        scratch_shapes=[dma((devices - 1,)), dma((devices - 1,))],
         compiler_params=pltpu.CompilerParams(collective_id=collective_id, has_side_effects=True),
         name="small_gather",
-    )(own).reshape((4 * length,) + own.shape)
+    )(own)
 
 
 def head_window(h):
@@ -1245,11 +1217,12 @@
         stream = Stream(ring, stream_sems, width)
         backward_stages(stream, (wq, wp, wu, wd))
         copies = Copies(sems)
-        copies.start(received, r.dy)
-        for name in saved:
-            copies.start(kept_in[name], getattr(r, name))
+        first = [copies.start(received, r.dy)]
+        for name in reversed(saved):
+            first.append(copies.start(kept_in[name], getattr(r, name)))
         stream.begin(0)
-        copies.finish()
+        for copy in first[:2]:
+            copy.wait()
         total_rows = r.x.shape[0]
         out_of = {**right_outs, "dmod": dmod_out, "slope": right_outs["dhid"]}
 
@@ -1266,6 +1239,9 @@
             r.dmod[q, :, 5 * width :] = jnp.sum(dy * r.mlp[rows, :].astype(F32), axis=0, keepdims=True)
 
         each_quarter(total_rows // 8, start)
+        for copy in first[2:]:
+            copy.wait()
+        copies.pending = []
 
         def finish(q, rows, grad):
             r.mlp[rows, :] = grad.astype(BF16)
@@ -1621,7 +1597,7 @@
     length = devices // 4
     ids = jnp.concatenate([timesteps.reshape(1, images), labels.reshape(1, images)])
     if length == 4:
-        ids = small_gather(jnp.pad(ids, ((0, 6), (0, 128 - images))), length, False, 2)
+        ids = small_gather(jnp.pad(ids, ((0, 6), (0, 128 - images))), devices, 2)
     else:
         ids = lax.all_gather(ids, "dp", axis=0)
     times = ids[:, 0, :images].reshape(devices * images)

time: 604 us -> 593 us (0.982)
  Pallas kernels: 454 us -> 441 us
    pallas_call x1, Pallas kernels: 208 us -> 199 us  [scatter_all(): pl.pallas_call(functools.partial(scatter_kernel, length, plan, slots, pai...]
where the time goes in v6:
time: 593 us; the launch traced here: 583 us
  Pallas kernels  441 us (74%)
  starting transfers between devices  87.3 us (15%)
  local copies, waits for them, and re-layouts  16.2 us (3%)
  other arithmetic  14.4 us (2%)
  waiting for transfers between devices  13.1 us (2%)
  matrix products  9.39 us (2%)
    pallas_call x1, Pallas kernels, scatter_all(): pl.pallas_call(functools.partial(scatter_kernel, length, plan, slots, pai...  199 us
    pallas_call x1, Pallas kernels, gather_encode(): pl.pallas_call(functools.partial(gather_encode_kernel, length, plan, name...  192 us
    ppermute x1, starting transfers between devices, swap_sections(): return lax.ppermute(x, 'section', [(0, 1), (1, 0)])  87.3 us
    pallas_call x1, Pallas kernels, encode_back(): pl.pallas_call(functools.partial(encode_back_kernel, names, RIGHTS, SAVED...  34.8 us
    ppermute x1, waiting for transfers between devices, swap_sections(): return lax.ppermute(x, 'section', [(0, 1), (1, 0)])  13.1 us
  transfers between devices with their start and end apart: 1, of which 1 were waited for; matrix products, arithmetic and copies ran while one was open for 0% of the time, Pallas kernels for 0%

profile of v6, /device:TPU:0, one launch (start us, length us, event | category | flops | bytes accessed | tf_op | source)
XLA Modules:
  0.0 582.5 jit_solution(3064090932467345011)
XLA Ops:
  0.6 0.0 copy-start
  0.7 0.8 reshape.152
  1.5 0.8 reshape.153
  2.3 0.6 pad.4.own_ref
  2.9 10.1 %small_gather.1 = s32[16,8,128]{2,1,0:T(8,128)} custom-call(s32[8,128]{1,0:T(8,128)} %pad.4.own_ref), custom_call_target="tpu_custom_call" | custom-call | tf_op jit(solution)/shard_map/small_gather/pallas_call | solution.py:669
  13.0 0.9 convert_reduce_fusion
  13.9 0.9 slice_reduce_fusion.1
  14.8 0.1 slice_reduce_fusion.2
  14.9 0.1 reshape.158
  15.0 0.7 compare_bitcast_fusion
  15.6 0.1 broadcast_in_dim.107
  15.7 0.1 broadcast_in_dim.108
  15.8 0.1 broadcast_in_dim.110
  15.9 0.1 broadcast_in_dim.111
  16.0 0.1 broadcast_in_dim.112
  16.0 0.8 reshape_reshape.22.refs_8_.row_ref
  16.8 0.6 reshape_reshape.18.refs_9_.column_ref
  17.5 0.1 broadcast_select_fusion.1
  17.5 0.1 convert_element_type.45
  17.6 0.1 eq.31
  17.7 0.7 add.45
  18.4 0.1 broadcast_in_dim.106
  18.5 0.7 convert_element_type.52.refs_5_
  19.1 0.1 broadcast_in_dim.113
  19.2 0.9 reshape_reshape.21.row_ref
  20.1 0.1 broadcast_in_dim.114
  20.2 0.7 broadcast_in_dim.115.column_ref
  20.9 1.3 reshape.161.mask_ref
  22.1 0.3 fusion.9
  22.5 2.7 fusion.3
  25.2 0.0 copy-start.2
  25.2 0.3 fusion.12
  25.5 0.6 fusion.15
  26.2 0.2 dynamic_update_slice.4
  26.4 1.9 fusion.1
  28.3 191.8 %gather_encode.1 = (bf16[4,2,2,72,3456]{4,3,2,1,0:T(8,128)(2,1)}, bf16[4,2,2,72,1152]{4,3,2,1,0:T(8,128)(2,1)}, bf16[4,2,2,72,4608]{4,3,2,1,0:T(8,128)(2,1)}, bf...) custom-call(bf16[72,3456]{1,0:T(8,128)(2,1)} %bitcast.74, ...), custom_call_target="tpu_custom_call" | custom-call | tf_op jit(solution)/shard_map/gather_encode/pallas_call | solution.py:1545
  220.1 5.3 decode.1
  225.4 87.3 %collective-permute-start = (bf16[2,128,1152]{2,1,0:T(8,128)(2,1)}, bf16[2,128,1152]{2,1,0:T(8,128)(2,1)S(1)}, u32[]{:S(2)}, u32[]{:S(2)}) collective-permute-start(bf16[2,128,1152]{2,1,0:T(8,128)(2,1)} %get-tuple-element.67), channel_id=1, source_target_pairs={{0,16},{16,0},{1,17},{17,1},{2,18},{18,2},{3,19},{19,3},{4,20},{20... | collective-permute-start | bytes 1769480 | tf_op jit(solution)/shard_map/ppermute | solution.py:1580
  312.7 0.1 broadcast_in_dim.118
  312.8 0.6 fusion.16
  313.4 13.1 %collective-permute-done = bf16[2,128,1152]{2,1,0:T(8,128)(2,1)S(1)} collective-permute-done((bf16[2,128,1152]{2,1,0:T(8,128)(2,1)}, bf16[2,128,1152]{2,1,0:T(8,128)(2,1)S(1)}, u32[]{:S(2)}, u32[]{:S(2)}) %collective-permute-start) | collective-permute-done | bytes 589856 | tf_op jit(solution)/shard_map/ppermute | solution.py:1580
  326.6 0.8 copy-done.10
  327.4 34.8 %encode_back.1 = (bf16[512,3456]{1,0:T(8,128)(2,1)}, bf16[512,1152]{1,0:T(8,128)(2,1)}, bf16[512,4608]{1,0:T(8,128)(2,1)}, bf16[512,1152]{1,0:T(8,128)(2,1)}, f3...) custom-call(bf16[256,1152]{1,0:T(8,128)(2,1)} %bitcast.72, ...), custom_call_target="tpu_custom_call", output_to_operand_aliasing={{0}: (15, {}), {1}: (16, {}), {2}: (17, {}), {3}: (18, {}),... | custom-call | tf_op jit(solution)/shard_map/encode_back/pallas_call | solution.py:1342
  362.2 0.0 copy-start.4
  362.2 1.6 reduce.3
  363.8 0.1 reshape.167
  363.8 0.1 fusion
  364.0 0.7 fusion.8.refs_8_
  364.7 2.2 slice_select_fusion.1.refs_13_
  366.9 198.8 %scatter_grads.1 = (bf16[72,3456]{1,0:T(8,128)(2,1)}, bf16[72,1152]{1,0:T(8,128)(2,1)}, bf16[72,4608]{1,0:T(8,128)(2,1)}, bf16[4,72,1152]{2,1,0:T(8,128)(2,1)}, ...) custom-call(bf16[512,1152]{1,0:T(8,128)(2,1)} %get-tuple-element.63.refs_0, ...), custom_call_target="tpu_custom_call" | custom-call | tf_op jit(solution)/shard_map/scatter_grads/pallas_call | solution.py:609
  565.7 1.1 slice.52
  566.8 3.1 fusion.4
  569.9 1.4 fusion.11
  571.3 1.5 slice_reduce_fusion
  572.8 0.3 slice_select_fusion.2
  573.1 1.1 copy.42
  574.2 1.1 copy.43
  575.2 1.1 bitcast_convert_fusion
  576.4 1.2 bitcast_convert_fusion.1
  577.6 1.0 bitcast_convert_fusion.2
  578.6 0.7 bitcast_convert_fusion.3
  579.3 1.3 constant_dynamic-slice_fusion
  580.6 1.3 copy.58
  581.9 0.2 copy-done.1
  (31 shorter events, 0.1 us)
Async XLA Ops:
  0.6 24.5 %copy-start = (bf16[256,1152]{1,0:T(8,128)(2,1)S(1)}, bf16[256,1152]{1,0:T(8,128)(2,1)}, u32[]{:S(2)}) copy-start(bf16[256,1152]{1,0:T(8,128)(2,1)} %param.22) | copy-start | bytes 1769476
  25.2 1.3 copy-start.2
  26.2 2.1 copy-start.12
  225.4 101.1 %collective-permute-start = (bf16[2,128,1152]{2,1,0:T(8,128)(2,1)}, bf16[2,128,1152]{2,1,0:T(8,128)(2,1)S(1)}, u32[]{:S(2)}, u32[]{:S(2)}) collective-permute-start(bf16[2,128,1152]{2,1,0:T(8,128)(2,1)} %get-tuple-element.67), channel_id=1, source_target_pairs={{0,16},{16,0},{1,17},{17,1},{2,18},{18,2},{3,19},{19,3},{4,20},{20... | collective-permute-start | bytes 1769480 | tf_op jit(solution)/shard_map/ppermute | solution.py:1580
  326.6 0.8 copy-start.10
  362.2 1.8 copy-start.4
  362.2 2.6 copy-start.5
  566.8 6.0 %copy-start.9 = (bf16[2,256,576]{2,1,0:T(8,128)(2,1)S(1)}, bf16[2,256,576]{2,1,0:T(8,128)(2,1)}, u32[]{:S(2)}) copy-start(bf16[2,256,576]{2,1,0:T(8,128)(2,1)} %get-tuple-element.87) | copy-start | bytes 1769476
  569.9 2.9 copy-start.6
  573.1 2.1 copy-start.8
  574.2 2.2 copy-start.7
  576.4 1.2 copy-start.11
  576.4 2.2 copy-start.13
  577.6 3.1 copy-start.3
  580.6 1.4 copy-start.1

commit v7 on v6

--- a/solution.py
+++ b/solution.py
@@ -330,13 +330,11 @@
         core_credit, pair_credit,
     ) = refs[32:45]
     a, b, c = position()
-    greet_all(length, a, b, c)
     side_steps = conditioning_steps(length, extras, extra_outs, refs[45:-1], a, b, c)
     swap_sem = refs[-1]
     swap = remote(
         outgoing, incoming, swap_sem.at[0], swap_sem.at[1], {"section": 1 - lax.axis_index("section")}
     )
-    swap.start()
     n = len(plan)
     rows, width = held.shape[3:]
     total_rows = raw.shape[1]
@@ -550,10 +548,12 @@
             add(held.at[i, a, b], pair_late.at[order[i]])
             result(i).start()
 
-    side_steps[0]()
     raw_load(0).start()
     right_load(0).start()
     raw_load(1).start()
+    greet_all(length, a, b, c)
+    side_steps[0]()
+    swap.start()
     produce(0)
     for t in range(n + LAG + LINE_LAG[-1] + 1):
         if t in SIDE_TIMES:

time: 593 us -> 590 us (level)
  no operation moved by 1% of the time
where the time goes in v7:
time: 590 us; the launch traced here: 581 us
  Pallas kernels  439 us (74%)
  starting transfers between devices  87.3 us (15%)
  local copies, waits for them, and re-layouts  16.2 us (3%)
  other arithmetic  14.4 us (2%)
  waiting for transfers between devices  13.1 us (2%)
  matrix products  9.4 us (2%)
    pallas_call x1, Pallas kernels, scatter_all(): pl.pallas_call(functools.partial(scatter_kernel, length, plan, slots, pai...  197 us
    pallas_call x1, Pallas kernels, gather_encode(): pl.pallas_call(functools.partial(gather_encode_kernel, length, plan, name...  192 us
    ppermute x1, starting transfers between devices, swap_sections(): return lax.ppermute(x, 'section', [(0, 1), (1, 0)])  87.3 us
    pallas_call x1, Pallas kernels, encode_back(): pl.pallas_call(functools.partial(encode_back_kernel, names, RIGHTS, SAVED...  34.8 us
    ppermute x1, waiting for transfers between devices, swap_sections(): return lax.ppermute(x, 'section', [(0, 1), (1, 0)])  13.1 us
  transfers between devices with their start and end apart: 1, of which 1 were waited for; matrix products, arithmetic and copies ran while one was open for 0% of the time, Pallas kernels for 0%

profile of v7, /device:TPU:0, one launch (start us, length us, event | category | flops | bytes accessed | tf_op | source)
XLA Modules:
  0.0 581.2 jit_solution(7104212691685213351)
XLA Ops:
  0.6 0.0 copy-start
  0.7 0.8 reshape.152
  1.5 0.8 reshape.153
  2.3 0.6 pad.4.own_ref
  2.9 10.1 %small_gather.1 = s32[16,8,128]{2,1,0:T(8,128)} custom-call(s32[8,128]{1,0:T(8,128)} %pad.4.own_ref), custom_call_target="tpu_custom_call" | custom-call | tf_op jit(solution)/shard_map/small_gather/pallas_call | solution.py:669
  13.0 0.9 convert_reduce_fusion
  13.9 0.9 slice_reduce_fusion.1
  14.8 0.1 slice_reduce_fusion.2
  14.9 0.1 reshape.158
  15.0 0.7 compare_bitcast_fusion
  15.6 0.1 broadcast_in_dim.107
  15.7 0.1 broadcast_in_dim.108
  15.8 0.1 broadcast_in_dim.110
  15.9 0.1 broadcast_in_dim.111
  16.0 0.1 broadcast_in_dim.112
  16.0 0.8 reshape_reshape.22.refs_8_.row_ref
  16.8 0.6 reshape_reshape.18.refs_9_.column_ref
  17.5 0.1 broadcast_select_fusion.1
  17.5 0.1 convert_element_type.45
  17.6 0.1 eq.31
  17.7 0.7 add.45
  18.4 0.1 broadcast_in_dim.106
  18.5 0.7 convert_element_type.52.refs_5_
  19.1 0.1 broadcast_in_dim.113
  19.2 0.9 reshape_reshape.21.row_ref
  20.1 0.1 broadcast_in_dim.114
  20.2 0.7 broadcast_in_dim.115.column_ref
  20.9 1.3 reshape.161.mask_ref
  22.1 0.3 fusion.9
  22.5 2.7 fusion.3
  25.2 0.0 copy-start.2
  25.2 0.3 fusion.12
  25.5 0.6 fusion.15
  26.2 0.2 dynamic_update_slice.4
  26.4 1.9 fusion.1
  28.3 191.8 %gather_encode.1 = (bf16[4,2,2,72,3456]{4,3,2,1,0:T(8,128)(2,1)}, bf16[4,2,2,72,1152]{4,3,2,1,0:T(8,128)(2,1)}, bf16[4,2,2,72,4608]{4,3,2,1,0:T(8,128)(2,1)}, bf...) custom-call(bf16[72,3456]{1,0:T(8,128)(2,1)} %bitcast.74, ...), custom_call_target="tpu_custom_call" | custom-call | tf_op jit(solution)/shard_map/gather_encode/pallas_call | solution.py:1545
  220.1 5.3 decode.1
  225.4 87.3 %collective-permute-start = (bf16[2,128,1152]{2,1,0:T(8,128)(2,1)}, bf16[2,128,1152]{2,1,0:T(8,128)(2,1)S(1)}, u32[]{:S(2)}, u32[]{:S(2)}) collective-permute-start(bf16[2,128,1152]{2,1,0:T(8,128)(2,1)} %get-tuple-element.67), channel_id=1, source_target_pairs={{0,16},{16,0},{1,17},{17,1},{2,18},{18,2},{3,19},{19,3},{4,20},{20... | collective-permute-start | bytes 1769480 | tf_op jit(solution)/shard_map/ppermute | solution.py:1580
  312.7 0.1 broadcast_in_dim.118
  312.8 0.6 fusion.16
  313.4 13.1 %collective-permute-done = bf16[2,128,1152]{2,1,0:T(8,128)(2,1)S(1)} collective-permute-done((bf16[2,128,1152]{2,1,0:T(8,128)(2,1)}, bf16[2,128,1152]{2,1,0:T(8,128)(2,1)S(1)}, u32[]{:S(2)}, u32[]{:S(2)}) %collective-permute-start) | collective-permute-done | bytes 589856 | tf_op jit(solution)/shard_map/ppermute | solution.py:1580
  326.6 0.8 copy-done.10
  327.4 34.8 %encode_back.1 = (bf16[512,3456]{1,0:T(8,128)(2,1)}, bf16[512,1152]{1,0:T(8,128)(2,1)}, bf16[512,4608]{1,0:T(8,128)(2,1)}, bf16[512,1152]{1,0:T(8,128)(2,1)}, f3...) custom-call(bf16[256,1152]{1,0:T(8,128)(2,1)} %bitcast.72, ...), custom_call_target="tpu_custom_call", output_to_operand_aliasing={{0}: (15, {}), {1}: (16, {}), {2}: (17, {}), {3}: (18, {}),... | custom-call | tf_op jit(solution)/shard_map/encode_back/pallas_call | solution.py:1342
  362.2 0.0 copy-start.5
  362.2 1.6 reduce.3
  363.8 0.1 reshape.167
  363.8 0.1 fusion
  364.0 0.7 fusion.8.refs_8_
  364.7 2.2 slice_select_fusion.1.refs_13_
  366.9 197.5 %scatter_grads.1 = (bf16[72,3456]{1,0:T(8,128)(2,1)}, bf16[72,1152]{1,0:T(8,128)(2,1)}, bf16[72,4608]{1,0:T(8,128)(2,1)}, bf16[4,72,1152]{2,1,0:T(8,128)(2,1)}, ...) custom-call(bf16[512,1152]{1,0:T(8,128)(2,1)} %get-tuple-element.63.refs_0, ...), custom_call_target="tpu_custom_call" | custom-call | tf_op jit(solution)/shard_map/scatter_grads/pallas_call | solution.py:609
  564.4 1.1 slice.52
  565.5 3.1 fusion.4
  568.6 1.4 fusion.11
  570.0 1.5 slice_reduce_fusion
  571.5 0.3 slice_select_fusion.2
  571.8 1.1 copy.42
  572.9 1.1 copy.43
  573.9 1.1 bitcast_convert_fusion
  575.1 1.2 bitcast_convert_fusion.1
  576.3 1.0 bitcast_convert_fusion.2
  577.3 0.7 bitcast_convert_fusion.3
  578.0 1.3 constant_dynamic-slice_fusion
  579.3 1.3 copy.58
  580.6 0.2 copy-done.1
  (31 shorter events, 0.1 us)
Async XLA Ops:
  0.6 24.5 %copy-start = (bf16[256,1152]{1,0:T(8,128)(2,1)S(1)}, bf16[256,1152]{1,0:T(8,128)(2,1)}, u32[]{:S(2)}) copy-start(bf16[256,1152]{1,0:T(8,128)(2,1)} %param.22) | copy-start | bytes 1769476
  25.2 1.3 copy-start.2
  26.2 2.1 copy-start.12
  225.4 101.1 %collective-permute-start = (bf16[2,128,1152]{2,1,0:T(8,128)(2,1)}, bf16[2,128,1152]{2,1,0:T(8,128)(2,1)S(1)}, u32[]{:S(2)}, u32[]{:S(2)}) collective-permute-start(bf16[2,128,1152]{2,1,0:T(8,128)(2,1)} %get-tuple-element.67), channel_id=1, source_target_pairs={{0,16},{16,0},{1,17},{17,1},{2,18},{18,2},{3,19},{19,3},{4,20},{20... | collective-permute-start | bytes 1769480 | tf_op jit(solution)/shard_map/ppermute | solution.py:1580
  326.6 0.8 copy-start.10
  362.2 1.8 copy-start.4
  362.2 2.6 copy-start.5
  565.5 6.0 %copy-start.9 = (bf16[2,256,576]{2,1,0:T(8,128)(2,1)S(1)}, bf16[2,256,576]{2,1,0:T(8,128)(2,1)}, u32[]{:S(2)}) copy-start(bf16[2,256,576]{2,1,0:T(8,128)(2,1)} %get-tuple-element.87) | copy-start | bytes 1769476
  568.6 2.9 copy-start.6
  571.8 2.1 copy-start.8
  572.9 2.2 copy-start.7
  575.1 1.2 copy-start.11
  575.1 2.2 copy-start.13
  576.3 3.1 copy-start.3
  579.3 1.4 copy-start.1

commit v8 on v7

--- a/solution.py
+++ b/solution.py
@@ -208,7 +208,7 @@
 LAG, LINE_LAG = 1, (0, 1, 2, 3)
 
 
-def greet_all(length, a, b, c):
+def greet_all(length, a, b, c, between):
     barrier = pltpu.get_barrier_semaphore()
 
     def tell(target):
@@ -219,6 +219,7 @@
     tell({"section": 1 - lax.axis_index("section")})
     for k in range(1, length):
         tell(at(lax.rem(a + k, length), b, c))
+    between()
     pl.semaphore_wait(barrier, length + 2)
 
 
@@ -458,7 +459,7 @@
 
     def produce(i):
         w = plan[i][0]
-        if i == 0 or plan[i - 1][0] != w:
+        if i > 0 and plan[i - 1][0] != w:
             turn(w)
         if progress["right"] + 1 < len(right_jobs) and right_jobs[progress["right"] + 1] == i:
             progress["right"] += 1
@@ -551,7 +552,7 @@
     raw_load(0).start()
     right_load(0).start()
     raw_load(1).start()
-    greet_all(length, a, b, c)
+    greet_all(length, a, b, c, lambda: turn(plan[0][0]))
     side_steps[0]()
     swap.start()
     produce(0)

time: 590 us -> 590 us (level)
  no operation moved by 1% of the time
where the time goes in v8:
time: 590 us; the launch traced here: 581 us
  Pallas kernels  439 us (74%)
  starting transfers between devices  87.3 us (15%)
  local copies, waits for them, and re-layouts  16.2 us (3%)
  other arithmetic  14.4 us (2%)
  waiting for transfers between devices  13.1 us (2%)
  matrix products  9.39 us (2%)
    pallas_call x1, Pallas kernels, scatter_all(): pl.pallas_call(functools.partial(scatter_kernel, length, plan, slots, pai...  197 us
    pallas_call x1, Pallas kernels, gather_encode(): pl.pallas_call(functools.partial(gather_encode_kernel, length, plan, name...  192 us
    ppermute x1, starting transfers between devices, swap_sections(): return lax.ppermute(x, 'section', [(0, 1), (1, 0)])  87.3 us
    pallas_call x1, Pallas kernels, encode_back(): pl.pallas_call(functools.partial(encode_back_kernel, names, RIGHTS, SAVED...  34.8 us
    ppermute x1, waiting for transfers between devices, swap_sections(): return lax.ppermute(x, 'section', [(0, 1), (1, 0)])  13.1 us
  transfers between devices with their start and end apart: 1, of which 1 were waited for; matrix products, arithmetic and copies ran while one was open for 0% of the time, Pallas kernels for 0%

profile of v8, /device:TPU:0, one launch (start us, length us, event | category | flops | bytes accessed | tf_op | source)
XLA Modules:
  0.0 580.9 jit_solution(5263904114945761748)
XLA Ops:
  0.6 0.0 copy-start
  0.7 0.8 reshape.152
  1.5 0.8 reshape.153
  2.3 0.6 pad.4.own_ref
  2.9 10.1 %small_gather.1 = s32[16,8,128]{2,1,0:T(8,128)} custom-call(s32[8,128]{1,0:T(8,128)} %pad.4.own_ref), custom_call_target="tpu_custom_call" | custom-call | tf_op jit(solution)/shard_map/small_gather/pallas_call | solution.py:670
  13.0 0.9 convert_reduce_fusion
  13.9 0.9 slice_reduce_fusion.1
  14.8 0.1 slice_reduce_fusion.2
  14.9 0.1 reshape.158
  15.0 0.7 compare_bitcast_fusion
  15.6 0.1 broadcast_in_dim.107
  15.7 0.1 broadcast_in_dim.108
  15.8 0.1 broadcast_in_dim.110
  15.9 0.1 broadcast_in_dim.111
  16.0 0.1 broadcast_in_dim.112
  16.0 0.8 reshape_reshape.22.refs_8_.row_ref
  16.8 0.6 reshape_reshape.18.refs_9_.column_ref
  17.5 0.1 broadcast_select_fusion.1
  17.5 0.1 convert_element_type.45
  17.6 0.1 eq.31
  17.7 0.7 add.45
  18.4 0.1 broadcast_in_dim.106
  18.5 0.7 convert_element_type.52.refs_5_
  19.1 0.1 broadcast_in_dim.113
  19.2 0.9 reshape_reshape.21.row_ref
  20.1 0.1 broadcast_in_dim.114
  20.2 0.7 broadcast_in_dim.115.column_ref
  20.9 1.3 reshape.161.mask_ref
  22.1 0.3 fusion.9
  22.5 2.7 fusion.3
  25.2 0.0 copy-start.2
  25.2 0.3 fusion.12
  25.5 0.6 fusion.15
  26.2 0.2 dynamic_update_slice.4
  26.4 1.9 fusion.1
  28.3 191.8 %gather_encode.1 = (bf16[4,2,2,72,3456]{4,3,2,1,0:T(8,128)(2,1)}, bf16[4,2,2,72,1152]{4,3,2,1,0:T(8,128)(2,1)}, bf16[4,2,2,72,4608]{4,3,2,1,0:T(8,128)(2,1)}, bf...) custom-call(bf16[72,3456]{1,0:T(8,128)(2,1)} %bitcast.74, ...), custom_call_target="tpu_custom_call" | custom-call | tf_op jit(solution)/shard_map/gather_encode/pallas_call | solution.py:1546
  220.1 5.3 decode.1
  225.4 87.3 %collective-permute-start = (bf16[2,128,1152]{2,1,0:T(8,128)(2,1)}, bf16[2,128,1152]{2,1,0:T(8,128)(2,1)S(1)}, u32[]{:S(2)}, u32[]{:S(2)}) collective-permute-start(bf16[2,128,1152]{2,1,0:T(8,128)(2,1)} %get-tuple-element.67), channel_id=1, source_target_pairs={{0,16},{16,0},{1,17},{17,1},{2,18},{18,2},{3,19},{19,3},{4,20},{20... | collective-permute-start | bytes 1769480 | tf_op jit(solution)/shard_map/ppermute | solution.py:1581
  312.7 0.1 broadcast_in_dim.118
  312.8 0.6 fusion.16
  313.4 13.1 %collective-permute-done = bf16[2,128,1152]{2,1,0:T(8,128)(2,1)S(1)} collective-permute-done((bf16[2,128,1152]{2,1,0:T(8,128)(2,1)}, bf16[2,128,1152]{2,1,0:T(8,128)(2,1)S(1)}, u32[]{:S(2)}, u32[]{:S(2)}) %collective-permute-start) | collective-permute-done | bytes 589856 | tf_op jit(solution)/shard_map/ppermute | solution.py:1581
  326.6 0.8 copy-done.10
  327.4 34.8 %encode_back.1 = (bf16[512,3456]{1,0:T(8,128)(2,1)}, bf16[512,1152]{1,0:T(8,128)(2,1)}, bf16[512,4608]{1,0:T(8,128)(2,1)}, bf16[512,1152]{1,0:T(8,128)(2,1)}, f3...) custom-call(bf16[256,1152]{1,0:T(8,128)(2,1)} %bitcast.72, ...), custom_call_target="tpu_custom_call", output_to_operand_aliasing={{0}: (15, {}), {1}: (16, {}), {2}: (17, {}), {3}: (18, {}),... | custom-call | tf_op jit(solution)/shard_map/encode_back/pallas_call | solution.py:1343
  362.2 0.0 copy-start.4
  362.2 1.6 reduce.3
  363.8 0.1 reshape.167
  363.8 0.1 fusion
  364.0 0.7 fusion.8.refs_8_
  364.7 2.2 slice_select_fusion.1.refs_13_
  366.9 197.2 %scatter_grads.1 = (bf16[72,3456]{1,0:T(8,128)(2,1)}, bf16[72,1152]{1,0:T(8,128)(2,1)}, bf16[72,4608]{1,0:T(8,128)(2,1)}, bf16[4,72,1152]{2,1,0:T(8,128)(2,1)}, ...) custom-call(bf16[512,1152]{1,0:T(8,128)(2,1)} %get-tuple-element.63.refs_0, ...), custom_call_target="tpu_custom_call" | custom-call | tf_op jit(solution)/shard_map/scatter_grads/pallas_call | solution.py:610
  564.1 1.1 slice.52
  565.2 3.1 fusion.4
  568.3 1.4 fusion.11
  569.7 1.5 slice_reduce_fusion
  571.2 0.3 slice_select_fusion.2
  571.5 1.1 copy.42
  572.6 1.1 copy.43
  573.6 1.1 bitcast_convert_fusion
  574.8 1.2 bitcast_convert_fusion.1
  576.0 1.0 bitcast_convert_fusion.2
  577.0 0.7 bitcast_convert_fusion.3
  577.7 1.3 constant_dynamic-slice_fusion
  579.0 1.3 copy.58
  580.3 0.2 copy-done.1
  (31 shorter events, 0.1 us)
Async XLA Ops:
  0.6 24.5 %copy-start = (bf16[256,1152]{1,0:T(8,128)(2,1)S(1)}, bf16[256,1152]{1,0:T(8,128)(2,1)}, u32[]{:S(2)}) copy-start(bf16[256,1152]{1,0:T(8,128)(2,1)} %param.22) | copy-start | bytes 1769476
  25.2 1.3 copy-start.2
  26.2 2.1 copy-start.12
  225.4 101.1 %collective-permute-start = (bf16[2,128,1152]{2,1,0:T(8,128)(2,1)}, bf16[2,128,1152]{2,1,0:T(8,128)(2,1)S(1)}, u32[]{:S(2)}, u32[]{:S(2)}) collective-permute-start(bf16[2,128,1152]{2,1,0:T(8,128)(2,1)} %get-tuple-element.67), channel_id=1, source_target_pairs={{0,16},{16,0},{1,17},{17,1},{2,18},{18,2},{3,19},{19,3},{4,20},{20... | collective-permute-start | bytes 1769480 | tf_op jit(solution)/shard_map/ppermute | solution.py:1581
  326.6 0.8 copy-start.10
  362.2 1.8 copy-start.4
  362.2 2.6 copy-start.5
  565.2 6.0 %copy-start.9 = (bf16[2,256,576]{2,1,0:T(8,128)(2,1)S(1)}, bf16[2,256,576]{2,1,0:T(8,128)(2,1)}, u32[]{:S(2)}) copy-start(bf16[2,256,576]{2,1,0:T(8,128)(2,1)} %get-tuple-element.87) | copy-start | bytes 1769476
  568.3 2.9 copy-start.6
  571.5 2.1 copy-start.8
  572.6 2.2 copy-start.7
  574.8 1.2 copy-start.11
  574.8 2.2 copy-start.13
  575.9 3.1 copy-start.3
  579.0 1.4 copy-start.1
